TPU v7x, 128 devices: a whole 4x4x4 slice. The times are simulated.
128 devices in a mesh: fsdp: 16 (over y_hi, z, core), rep: 8 (over x, y_lo).
Axes of the slice: x: 4, y: 4 (y_hi: 2, y_lo: 2; y = y_hi * 2 + y_lo), z: 4, core: 2. Of those that a mesh axis runs over, the one named last changes fastest.
Arguments:
- tokens: bfloat16 [32768, 1536], P(('fsdp', 'rep')), may hold values from -6 to 6
- cotangent: bfloat16 [32768, 1536], P(('fsdp', 'rep')), may hold values from -6 to 6
- lengths: int32 [16, 3], replicated, may hold values from 1 to 2046, as said below
- w_in: float32 [1536, 6400], P('fsdp'), may hold values from -0.15625 to 0.15625
- w_dt: float32 [1536, 48], P('fsdp'), may hold values from -0.15625 to 0.15625
- w_out: float32 [3072, 1536], P('fsdp'), may hold values from -0.109375 to 0.109375
- small: float32 [21392], P('fsdp'), may hold values from -6 to 1.5
- first_in: float32 [1536, 6400], P('fsdp'), may hold values from -80 to 80
- first_dt: float32 [1536, 48], P('fsdp'), may hold values from -12 to 12
- first_out: float32 [3072, 1536], P('fsdp'), may hold values from -128 to 128
- first_small: float32 [21392], P('fsdp'), may hold values from -64 to 64
- second_in: float32 [1536, 6400], P('fsdp'), may hold values from 16.384 to 65.536
- second_dt: float32 [1536, 48], P('fsdp'), may hold values from 0.32768 to 1.31072
- second_out: float32 [3072, 1536], P('fsdp'), may hold values from 32.768 to 131.072
- second_small: float32 [21392], P('fsdp'), may hold values from 8.192 to 32.768
Outputs:
- block_out: float32 [32768, 1536], P(('fsdp', 'rep'))
- input_grad: float32 [32768, 1536], P(('fsdp', 'rep'))
- grad_in: float32 [1536, 6400], P('fsdp')
- grad_dt: float32 [1536, 48], P('fsdp')
- grad_out: float32 [3072, 1536], P('fsdp')
- grad_small: float32 [21392], P('fsdp')
- new_first_in: float32 [1536, 6400], P('fsdp')
- new_first_dt: float32 [1536, 48], P('fsdp')
- new_first_out: float32 [3072, 1536], P('fsdp')
- new_first_small: float32 [21392], P('fsdp')
- new_second_in: float32 [1536, 6400], P('fsdp')
- new_second_dt: float32 [1536, 48], P('fsdp')
- new_second_out: float32 [3072, 1536], P('fsdp')
- new_second_small: float32 [21392], P('fsdp')
- new_in: float32 [1536, 6400], P('fsdp')
- new_dt: float32 [1536, 48], P('fsdp')
- new_out: float32 [3072, 1536], P('fsdp')
- new_small: float32 [21392], P('fsdp')
Inputs may be any that keep to these rules, and one draw needn't show every extreme that they name: Row f holds the lengths of the three sequences that fill pack f from its position 0; the rest of its 2048 positions is padding. The first and third are at most 64 long, the padding at most 128, so the second begins within the first 256 positions and ends within the last 256. In every draw some pack has first and third sequences of length 1 and no padding.
All inputs are finite; a program needn't handle non-finite values.
Results may differ from a plain program's by a relative error of at most 0.003.
The roundings to bfloat16 on the way count: a program that leaves them out, or rounds other values in their place, can miss the bound.
Values may be sent and summed in bfloat16 or wider, within the bound.
No kernel may reach another device: no remote copies, remote signals or barrier semaphores. Data moves between devices by JAX's collectives and lax.ppermute only.
A program may use at most 320 MiB of HBM per device.

v0:
```python
from functools import partial
import math

import jax
import jax.numpy as jnp
from jax import lax
from jax.sharding import PartitionSpec as P

D = 1536
H = 48
P_SIZE = 64
N = 128
CONV = 4
STEP = 10


NORM_EPS = 1e-05
BETA_ONE = 0.9
BETA_TWO = 0.999
ADAM_EPS = 1e-08
WEIGHT_DECAY = 0.1
RATE_MATRIX = 0.04
RATE_SMALL = 0.4
PRECISE = lax.Precision.HIGHEST


def shifted(value, axis, steps):
    count = lax.axis_size(axis)
    leading, last = (max(0, -steps), min(count, count - steps))
    return lax.ppermute(value, axis, [(source, source + steps) for source in range(leading, last)])


def prefix(value, axis, join, neutral, backward):
    count, mine = (lax.axis_size(axis), lax.axis_index(axis))
    pieces = jax.tree.map(lambda part: lax.all_gather(part, axis), value)
    if backward:
        pieces = jax.tree.map(lambda part: part[::-1], pieces)
        mine = count - 1 - mine
    running = jax.tree.map(
        lambda part, zero: jnp.full_like(part, 0) + jnp.asarray(zero, part.dtype), value, neutral
    )

    def turn(position, running):
        longer = join(running, jax.tree.map(lambda part: part[position], pieces))
        return jax.tree.map(lambda new, old: jnp.where(position < mine, new, old), longer, running)

    return lax.fori_loop(0, count - 1, turn, running)


def unpack_small(vector):
    inner_width = H * P_SIZE
    channels = inner_width + 2 * N
    offset = 0
    gain_in = vector[offset : offset + D]
    offset = offset + D
    gain_out = vector[offset : offset + inner_width]
    offset = offset + inner_width
    conv_taps = vector[offset : offset + CONV * channels].reshape(CONV, channels)
    offset = offset + CONV * channels
    conv_bias = vector[offset : offset + channels]
    offset = offset + channels
    dt_bias = vector[offset : offset + H]
    a_log = vector[offset + H : offset + 2 * H]
    d_skip = vector[offset + 2 * H : offset + 3 * H]
    return (gain_in, gain_out, conv_taps, conv_bias, dt_bias, a_log, d_skip)


def segment_at(positions, seg_ends):
    counted = jnp.sum((positions[:, None] >= seg_ends[None, :]).astype(jnp.int32), axis=1)
    return jnp.where(positions < 0, jnp.int32(-1), counted)


def conv_part(extended, dt_raw, conv_taps, conv_bias, dt_bias, a_log, same_masks):
    row_count = dt_raw.shape[0]
    conv_width = conv_taps.shape[0]
    inner_width = H * P_SIZE
    summed = conv_bias[None, :] + conv_taps[conv_width - 1][None, :] * extended[conv_width - 1 :]
    for offset in range(1, conv_width):
        tap_index = conv_width - 1 - offset
        summed = (
            summed
            + conv_taps[tap_index][None, :]
            * extended[tap_index : tap_index + row_count]
            * same_masks[offset][:, None]
        )
    active = jax.nn.silu(summed)
    heads_x = active[:, :inner_width].reshape(row_count, H, P_SIZE)
    state_b = active[:, inner_width : inner_width + N]
    state_c = active[:, inner_width + N :]
    step_dt = jax.nn.softplus(dt_raw + dt_bias[None, :])
    log_decay = -step_dt * jnp.exp(a_log)[None, :]
    return (heads_x, state_b, state_c, step_dt, log_decay)


def block_terms(
    carry_state, prior_segment, heads_x, state_b, state_c, step_dt, log_decay, segments
):
    block_rows = heads_x.shape[0]
    cumulative = jnp.cumsum(log_decay, axis=0)
    positions_in = jnp.arange(block_rows, dtype=jnp.int32)
    same_seg = (
        (segments[:, None] == segments[None, :]) & (positions_in[:, None] >= positions_in[None, :])
    ).astype(jnp.float32)
    span_logs = cumulative.T[:, :, None] - cumulative.T[:, None, :]
    decay_matrix = jnp.exp(jnp.where(same_seg[None] > 0, span_logs, 0.0)) * same_seg[None]
    scores = jnp.dot(state_c, state_b.T, precision=PRECISE)
    mixing = decay_matrix * scores[None] * step_dt.T[:, None, :]
    outputs = jnp.einsum("hts,shp->thp", mixing, heads_x, precision=PRECISE)
    entering = (segments == prior_segment).astype(jnp.float32)[:, None] * jnp.exp(cumulative)
    outputs = outputs + entering[:, :, None] * jnp.einsum(
        "tn,hpn->thp", state_c, carry_state, precision=PRECISE
    )
    leaving = (
        (segments == segments[-1]).astype(jnp.float32)[:, None]
        * jnp.exp(cumulative[-1][None, :] - cumulative)
        * step_dt
    )
    passing = (segments[-1] == prior_segment).astype(jnp.float32) * jnp.exp(cumulative[-1])
    new_state = passing[:, None, None] * carry_state + jnp.einsum(
        "sh,shp,sn->hpn", leaving, heads_x, state_b, precision=PRECISE
    )
    return (new_state, outputs)


def reshape_blocks(array, block_rows):
    return array.reshape((array.shape[0] // block_rows, block_rows) + array.shape[1:])


def local_scan(heads_x, state_b, state_c, step_dt, log_decay, segments, entry_segment, block_rows):
    row_count = heads_x.shape[0]
    priors = jnp.concatenate(
        [jnp.reshape(entry_segment, (1,)), segments[block_rows - 1 : row_count - 1 : block_rows]]
    )

    def advance(carry_state, pieces):
        return block_terms(
            carry_state, pieces[6], pieces[0], pieces[1], pieces[2], pieces[3], pieces[4], pieces[5]
        )

    start_state = jnp.zeros((heads_x.shape[1], heads_x.shape[2], state_b.shape[1]), jnp.float32)
    pieces = (
        reshape_blocks(heads_x, block_rows),
        reshape_blocks(state_b, block_rows),
        reshape_blocks(state_c, block_rows),
        reshape_blocks(step_dt, block_rows),
        reshape_blocks(log_decay, block_rows),
        reshape_blocks(segments, block_rows),
        priors,
    )
    final_state, outputs = lax.scan(jax.checkpoint(advance), start_state, pieces)
    return (outputs.reshape(heads_x.shape), final_state)


def local_part(heads_x, state_b, state_c, step_dt, log_decay, segments, entry_segment, block_rows):
    local_out, local_state = local_scan(
        heads_x, state_b, state_c, step_dt, log_decay, segments, entry_segment, block_rows
    )
    decays = jnp.exp(jnp.sum(log_decay, axis=0)) * (segments[-1] == entry_segment).astype(
        jnp.float32
    )
    return (local_out, local_state, decays)


def carry_terms(state_c, log_decay, state_in, segments, entry_segment):
    entering = (segments == entry_segment).astype(jnp.float32)[:, None] * jnp.exp(
        jnp.cumsum(log_decay, axis=0)
    )
    return entering[:, :, None] * jnp.einsum("tn,hpn->thp", state_c, state_in, precision=PRECISE)


def gate_norm(
    local_out,
    heads_x,
    state_c,
    log_decay,
    state_in,
    gate_z,
    d_skip,
    gain_out,
    segments,
    entry_segment,
):
    mixed = (
        local_out
        + carry_terms(state_c, log_decay, state_in, segments, entry_segment)
        + d_skip[None, :, None] * heads_x
    )
    gated = mixed.reshape(gate_z.shape) * jax.nn.silu(gate_z)
    return (
        gated
        * lax.rsqrt(jnp.mean(gated * gated, axis=1, keepdims=True) + NORM_EPS)
        * gain_out[None, :]
    )


def input_norm(inputs, gain_in):
    return (
        inputs
        * lax.rsqrt(jnp.mean(inputs * inputs, axis=1, keepdims=True) + NORM_EPS)
        * gain_in[None, :]
    )


def combine_states(earlier, later_part):
    return (earlier[0] * later_part[0], later_part[0][:, None, None] * earlier[1] + later_part[1])


def adam_update(weight, gradient, moment_one, moment_two, learn_rate, decay_rate):
    moment_one = BETA_ONE * moment_one + (1.0 - BETA_ONE) * gradient
    moment_two = BETA_TWO * moment_two + (1.0 - BETA_TWO) * gradient * gradient
    scaled = (
        moment_one
        / (1.0 - BETA_ONE**STEP)
        / (jnp.sqrt(moment_two / (1.0 - BETA_TWO**STEP)) + ADAM_EPS)
    )
    return (weight - learn_rate * (scaled + decay_rate * weight), moment_one, moment_two)


def contract_rows(left_side, right_side):
    return lax.dot_general(
        left_side, right_side, (((0,), (0,)), ((), ())), preferred_element_type=jnp.float32
    )


def contract_cols(left_side, right_side):
    return lax.dot_general(
        left_side, right_side, (((1,), (1,)), ((), ())), preferred_element_type=jnp.float32
    )


def body(
    tokens,
    cotangent,
    lengths,
    w_in,
    w_dt,
    w_out,
    small,
    first_in,
    first_dt,
    first_out,
    first_small,
    second_in,
    second_dt,
    second_out,
    second_small,
):
    row_count = tokens.shape[0]
    conv_width = CONV
    inner_width = H * P_SIZE
    block_rows = math.gcd(row_count, 256)
    pack_index = lax.axis_index("fsdp")
    rep_index = lax.axis_index("rep")
    pack_lengths = lax.dynamic_slice_in_dim(lengths, pack_index, 1, 0)[0]
    seg_ends = jnp.cumsum(pack_lengths)
    first_place = rep_index * row_count
    positions = first_place + jnp.arange(row_count, dtype=jnp.int32)
    segments = segment_at(positions, seg_ends)
    entry_segment = segment_at(jnp.reshape(first_place - 1, (1,)), seg_ends)[0]
    live_rows = (segments < 3).astype(jnp.float32)
    same_masks = jnp.stack(
        [
            (segment_at(positions - offset, seg_ends) == segments).astype(jnp.float32)
            for offset in range(conv_width)
        ],
        0,
    )
    gathered = (
        lax.all_gather(w_in.astype(jnp.bfloat16), "fsdp", axis=0, tiled=True),
        lax.all_gather(w_dt.astype(jnp.bfloat16), "fsdp", axis=0, tiled=True),
        lax.all_gather(w_out.astype(jnp.bfloat16), "fsdp", axis=0, tiled=True),
        lax.all_gather(small.astype(jnp.bfloat16), "fsdp", axis=0, tiled=True),
    )
    full_in, full_dt, full_out, full_small = gathered
    gain_in, gain_out, conv_taps, conv_bias, dt_bias, a_log, d_skip = unpack_small(
        full_small.astype(jnp.float32)
    )
    inputs = tokens.astype(jnp.float32)
    normed, norm_back = jax.vjp(input_norm, inputs, gain_in)
    normed_low = normed.astype(jnp.bfloat16)
    projected = jnp.dot(normed_low, full_in, preferred_element_type=jnp.float32)
    dt_raw = jnp.dot(normed_low, full_dt, preferred_element_type=jnp.float32)
    gate_z = projected[:, :inner_width]
    conv_input = projected[:, inner_width:].astype(jnp.bfloat16)
    from_prev = shifted(conv_input[row_count - conv_width + 1 :], "rep", 1)
    extended = jnp.concatenate([from_prev, conv_input], 0).astype(jnp.float32)
    conv_fn = partial(conv_part, same_masks=same_masks)
    (heads_x, state_b, state_c, step_dt, log_decay), conv_back = jax.vjp(
        conv_fn, extended, dt_raw, conv_taps, conv_bias, dt_bias, a_log
    )
    local_fn = partial(
        local_part, segments=segments, entry_segment=entry_segment, block_rows=block_rows
    )
    (local_out, local_state, decays), scan_back = jax.vjp(
        local_fn, heads_x, state_b, state_c, step_dt, log_decay
    )
    identity_pair = (jnp.ones((H,), jnp.float32), jnp.zeros((H, P_SIZE, N), jnp.float32))
    entering_pair = prefix((decays, local_state), "rep", combine_states, identity_pair, False)
    state_in = entering_pair[1]
    gate_fn = partial(gate_norm, segments=segments, entry_segment=entry_segment)
    normed_out, gate_back = jax.vjp(
        gate_fn, local_out, heads_x, state_c, log_decay, state_in, gate_z, d_skip, gain_out
    )
    out_low = normed_out.astype(jnp.bfloat16)
    branch = jnp.dot(out_low, full_out, preferred_element_type=jnp.float32)
    block_out = inputs + live_rows[:, None] * branch
    grad_branch = (cotangent.astype(jnp.float32) * live_rows[:, None]).astype(jnp.bfloat16)
    grad_out_full = contract_rows(out_low, grad_branch)
    full_in, full_dt, full_out = (
        lax.all_gather(w_in.astype(jnp.bfloat16), "fsdp", axis=0, tiled=True),
        lax.all_gather(w_dt.astype(jnp.bfloat16), "fsdp", axis=0, tiled=True),
        lax.all_gather(w_out.astype(jnp.bfloat16), "fsdp", axis=0, tiled=True),
    )
    grad_normed_out = contract_cols(grad_branch, full_out)
    (
        grad_local,
        grad_x_one,
        grad_c_one,
        grad_decay_one,
        entry_grad,
        grad_z,
        grad_skip,
        grad_gain_out,
    ) = gate_back(grad_normed_out)
    later_pair = prefix((decays, entry_grad), "rep", combine_states, identity_pair, True)
    later_grad = later_pair[1]
    decay_grad = jnp.sum(later_grad * state_in, axis=(1, 2))
    grad_x_two, grad_b, grad_c_two, grad_step, grad_decay_two = scan_back(
        (grad_local, later_grad, decay_grad)
    )
    grad_ext, grad_dtraw, grad_taps, grad_cbias, grad_dtbias, grad_alog = conv_back(
        (
            grad_x_one + grad_x_two,
            grad_b,
            grad_c_one + grad_c_two,
            grad_step,
            grad_decay_one + grad_decay_two,
        )
    )
    from_next = shifted(grad_ext[: conv_width - 1].astype(jnp.bfloat16), "rep", -1).astype(
        jnp.float32
    )
    grad_conv_in = grad_ext[conv_width - 1 :] + jnp.concatenate(
        [jnp.zeros((row_count - conv_width + 1, from_next.shape[1]), jnp.float32), from_next], 0
    )
    grad_proj = jnp.concatenate([grad_z, grad_conv_in], 1).astype(jnp.bfloat16)
    grad_dtraw_low = grad_dtraw.astype(jnp.bfloat16)
    grad_h = contract_cols(grad_proj, full_in) + contract_cols(grad_dtraw_low, full_dt)
    grad_inputs, grad_gain_in = norm_back(grad_h)
    input_grad = cotangent.astype(jnp.float32) + grad_inputs
    grad_in_full = contract_rows(normed_low, grad_proj)
    grad_dt_full = contract_rows(normed_low, grad_dtraw_low)
    grad_small_full = jnp.concatenate(
        [
            grad_gain_in,
            grad_gain_out,
            grad_taps.reshape(-1),
            grad_cbias,
            grad_dtbias,
            grad_alog,
            grad_skip,
        ]
    )
    shards = (
        lax.psum_scatter(grad_in_full, "fsdp", scatter_dimension=0, tiled=True),
        lax.psum_scatter(grad_dt_full, "fsdp", scatter_dimension=0, tiled=True),
        lax.psum_scatter(grad_out_full, "fsdp", scatter_dimension=0, tiled=True),
        lax.psum_scatter(grad_small_full, "fsdp", scatter_dimension=0, tiled=True),
    )
    totals = lax.psum((shards[0], shards[1], shards[2], shards[3]), "rep")
    grad_in, grad_dt, grad_out, grad_small = totals
    new_in, new_first_in, new_second_in = adam_update(
        w_in, grad_in, first_in, second_in, RATE_MATRIX, WEIGHT_DECAY
    )
    new_dt, new_first_dt, new_second_dt = adam_update(
        w_dt, grad_dt, first_dt, second_dt, RATE_MATRIX, WEIGHT_DECAY
    )
    new_out, new_first_out, new_second_out = adam_update(
        w_out, grad_out, first_out, second_out, RATE_MATRIX, WEIGHT_DECAY
    )
    new_small, new_first_small, new_second_small = adam_update(
        small, grad_small, first_small, second_small, RATE_SMALL, 0.0
    )
    return (
        block_out,
        input_grad,
        grad_in,
        grad_dt,
        grad_out,
        grad_small,
        new_first_in,
        new_first_dt,
        new_first_out,
        new_first_small,
        new_second_in,
        new_second_dt,
        new_second_out,
        new_second_small,
        new_in,
        new_dt,
        new_out,
        new_small,
    )


def solution(mesh):
    return jax.shard_map(
        body,
        mesh=mesh,
        in_specs=(
            P(("fsdp", "rep"), None),
            P(("fsdp", "rep"), None),
            P(),
            P("fsdp", None),
            P("fsdp", None),
            P("fsdp", None),
            P("fsdp"),
            P("fsdp", None),
            P("fsdp", None),
            P("fsdp", None),
            P("fsdp"),
            P("fsdp", None),
            P("fsdp", None),
            P("fsdp", None),
            P("fsdp"),
        ),
        out_specs=(
            P(("fsdp", "rep"), None),
            P(("fsdp", "rep"), None),
            P("fsdp", None),
            P("fsdp", None),
            P("fsdp", None),
            P("fsdp"),
            P("fsdp", None),
            P("fsdp", None),
            P("fsdp", None),
            P("fsdp"),
            P("fsdp", None),
            P("fsdp", None),
            P("fsdp", None),
            P("fsdp"),
            P("fsdp", None),
            P("fsdp", None),
            P("fsdp", None),
            P("fsdp"),
        ),
        check_vma=False,
    )
```

profile of v0, /device:TPU:0, one launch (start us, length us, event | category | flops | bytes accessed | tf_op | source)
XLA Modules:
  0.0 1611.6 jit_solution(15615626886923649152)
XLA Ops:
  12.0 72.2 %all-reduce.14 = bf16[21392]{0:T(1024)(128)(2,1)S(1)} all-reduce(bf16[21392]{0:T(1024)(128)(2,1)S(1)} %dynamic-update-slice), channel_id=1, replica_groups=mesh['fsdp'=16,'rep'=8] {'fsdp'}, use_global_device_ids=true, to_apply=%add.14 | all-reduce | flops 21392 | bytes 85568
  87.3 20.5 %all-gather.3 = bf16[16,96,48]{1,2,0:T(8,128)(2,1)S(1)} all-gather(bf16[1,96,48]{1,2,0:T(8,128)(2,1)S(1)} %convert_bitcast_fusion), channel_id=1, replica_groups=mesh['fsdp'=16,'rep'=8] {'fsdp'}, dimensions={0}, use_global_device_ids=true | all-gather | bytes 156672 | tf_op jit(solution)/shard_map/all_gather | solution.py:270
  114.6 23.1 %all-gather.9.cloned.1.call-done = bf16[1536,6400]{1,0:T(8,128)(2,1)} async-done(((bf16[96,6400]{1,0:T(8,128)(2,1)}), bf16[1536,6400]{1,0:T(8,128)(2,1)}) %all-gather.9.cloned.1.call-update) | async-done | bytes 19660816 | tf_op jit(solution)/shard_map/all_gather | solution.py:269
  137.7 13.9 fusion.163
  185.0 28.1 %all-reduce.15 = f32[384]{0:T(512)S(1)} all-reduce(f32[384]{0:T(512)S(1)} %multiply_dynamic-update-slice_fusion), channel_id=2, replica_groups=mesh['fsdp'=16,'rep'=8] {'rep'}, use_global_device_ids=true, to_apply=%add.15 | all-reduce | flops 384 | bytes 3072
  221.3 200.2 %all-gather.13.cloned.1.call-done = f32[384,64,128]{2,1,0:T(8,128)} async-done(((f32[48,64,128]{2,1,0:T(8,128)}), f32[384,64,128]{2,1,0:T(8,128)}) %all-gather.13.cloned.1.call-update) | async-done | bytes 12582928 | tf_op jit(solution)/shard_map/all_gather | solution.py:35
  421.4 22.8 %while.18 = (s32[]{:T(128)}, f32[48,64,128]{2,1,0:T(8,128)}, s32[]{:T(128)}, f32[8,48]{1,0:T(8,128)S(1)}, f32[8,48,64,128]{3,2,1,0:T(8,128)}, /*index=5*/s32[]{:T(128)}, s32[]{:T(128)}) while((s32[]{:T(128)}, f32[48,64,128]{2,1,0:T(8,128)}, s32[]{:T(128)}, f32[8,48]{1,0:T(8,128)S(1)}, f32[8,48,64,128]{3,2,1,0:T(8,128)}, ...), condition=%wide.region_11.12_spmd.clone, body=%wide.region_10.11_spmd.clone.sunk | while | flops 1572868 | bytes 4719281 | solution.py:47
  448.7 17.9 %fusion.41 = f32[256,48,64]{0,2,1:T(8,128)} fusion(f32[256,48,64]{0,2,1:T(8,128)S(1)} %bitcast.208, f32[256,48,64]{0,2,1:T(8,128)S(1)} %fusion.111, f32[256,48,64]{0,2,1:T(8,128)} %fusion.88, f32[48,256]{1,0:T(8,128)S(1)} %copy-done.73, f32[256,256]{1,0:T(8,128)S(1)} %copy-done.52, f32[256,256]{1,0:T(8,128)S(1)} %copy-done.50, ...), kind=kOutput, calls=%fused_computation.66 | convolution fusion | flops 2436366336 | bytes 13320384 | tf_op jit(solution)/shard_map/jvp()/while/body/eval_jaxpr/hts,shp->thp/dot_general | solution.py:108
  475.7 27.4 %all-gather.11.cloned.1.call-done = bf16[3072,1536]{1,0:T(8,128)(2,1)} async-done(((bf16[192,1536]{1,0:T(8,128)(2,1)}), bf16[3072,1536]{1,0:T(8,128)(2,1)}) %all-gather.11.cloned.1.call-update) | async-done | bytes 9437200 | tf_op jit(solution)/shard_map/all_gather | solution.py:271
  503.1 8.5 multiply_reduce_fusion.8
  526.8 11.6 fusion.91
  542.4 8.1 fusion.78
  550.5 221.0 %all-gather.15.cloned.1.call-done = f32[384,64,128]{2,1,0:T(8,128)} async-done(((f32[48,64,128]{2,1,0:T(8,128)}), f32[384,64,128]{2,1,0:T(8,128)}) %all-gather.15.cloned.1.call-update) | async-done | bytes 12582928 | tf_op jit(solution)/shard_map/all_gather | solution.py:35
  771.5 11.8 rev.7
  783.3 30.8 %while.19 = (s32[]{:T(128)}, f32[48,64,128]{2,1,0:T(8,128)}, s32[]{:T(128)}, f32[8,48]{1,0:T(8,128)}, f32[8,48,64,128]{3,2,1,0:T(8,128)}, /*index=5*/s32[]{:T(128)}, s32[]{:T(128)}) while((s32[]{:T(128)}, f32[48,64,128]{2,1,0:T(8,128)}, s32[]{:T(128)}, f32[8,48]{1,0:T(8,128)}, f32[8,48,64,128]{3,2,1,0:T(8,128)}, ...), condition=%wide.region_15.16_spmd.clone, body=%wide.region_14.15_spmd.clone.sunk | while | flops 1572868 | bytes 4719281 | solution.py:47
  835.6 24.8 %fusion.15 = (f32[48,256]{1,0:T(8,128)}, f32[48,256]{1,0:T(8,128)}, f32[48,256]{1,0:T(8,128)}, f32[256,256]{1,0:T(8,128)}) fusion(f32[256,256]{1,0:T(8,128)S(1)} %fusion.164, f32[48,256]{1,0:T(8,128)} %copy.146, f32[256,256]{1,0:T(8,128)S(1)} %get-tuple-element.449, f32[48,256]{1,0:T(8,128)} %copy.144, pred[256,256]{1,0:T(8,128)(4,1)S(1)} %get-tuple-element.448, ...), kind=kOutput, calls=%fused_computation.22 | convolution fusion | flops 2463002624 | bytes 7389184 | tf_op jit(solution)/shard_map/transpose(jvp())/while/body/eval_jaxpr/checkpoint/hts,shp->thp/dot_general | solution.py:108
  878.0 14.2 bitcast_add_fusion.2
  932.2 15.4 fusion.54
  978.4 16.8 %fusion.64 = (f32[1536]{0:T(1024)S(1)}, f32[256]{0:T(256)}, f32[256,1536]{1,0:T(8,128)}) fusion(bf16[256,1536]{1,0:T(8,128)(2,1)S(1)} %copy-done.19, f32[256]{0:T(256)S(1)} %fusion.127, f32[1536]{0:T(1024)S(1)} %slice.161, f32[256,1536]{1,0:T(8,128)S(1)} %fusion.120, bf16[1536,6400]{1,0:T(8,128)(2,1)} %all-gather.9.cloned.1.call-done, ...), kind=kOutput, calls=%fused_computation.108 | convolution fusion | flops 5042862080 | bytes 26884096 | tf_op jit(solution)/shard_map/dot_general | solution.py:226
  999.8 222.9 %reduce-scatter.6.cloned.1.call-done = f32[96,6400]{1,0:T(8,128)} async-done(((f32[1536,6400]{1,0:T(8,128)}), f32[96,6400]{1,0:T(8,128)}) %reduce-scatter.6.cloned.1.call-update) | async-done | bytes 2457616 | tf_op jit(solution)/shard_map/reduce_scatter | solution.py:365
  1232.8 121.7 %all-reduce.22.cloned.1.call-done = f32[21392]{0:T(1024)} async-done(((f32[21392]{0:T(1024)}), f32[21392]{0:T(1024)}) %all-reduce.22.cloned.1.call-update) | async-done | bytes 85584
  1355.3 70.3 %reduce-scatter.10.cloned.1.call-done = f32[96,48]{1,0:T(8,128)} async-done(((f32[1536,48]{1,0:T(8,128)}), f32[96,48]{1,0:T(8,128)}) %reduce-scatter.10.cloned.1.call-update) | async-done | bytes 18448
  1427.1 36.5 %all-reduce.17 = (f32[96,48]{0,1:T(8,128)}, f32[1337]{0:T(1024)}) all-reduce(f32[96,48]{0,1:T(8,128)} %copy.165, f32[1337]{0:T(1024)S(1)} %dynamic-slice.13), channel_id=1, replica_groups=mesh['fsdp'=16,'rep'=8] {'rep'}, use_global_device_ids=true, to_apply=%region_35.36 | all-reduce | flops 5945 | bytes 47560 | tf_op jit(solution)/shard_map/psum | solution.py:370
  1466.4 124.3 %all-reduce.24.cloned.1.call-done = (f32[96,6400]{1,0:T(8,128)}, f32[192,1536]{1,0:T(8,128)}) async-done(((f32[96,6400]{1,0:T(8,128)}, f32[192,1536]{1,0:T(8,128)}), (f32[96,6400]{1,0:T(8,128)}, f32[192,1536]{1,0:T(8,128)})) %all-reduce.24.cloned.1.call-update) | async-done | bytes 3637264 | tf_op jit(solution)/shard_map/psum | solution.py:370
  (403 shorter events, 280.4 us)
Async XLA Ops:
  7.2 77.1 %copy-start = (s32[16,3]{0,1:T(4,128)S(1)}, s32[16,3]{0,1:T(4,128)}, u32[]{:S(2)}) copy-start(s32[16,3]{0,1:T(4,128)} %param.21) | copy-start | bytes 580
  7.2 80.1 %copy-start.65 = (f32[96,48]{0,1:T(8,128)S(1)}, f32[96,48]{0,1:T(8,128)}, u32[]{:S(2)}) copy-start(f32[96,48]{0,1:T(8,128)} %param.23) | copy-start | bytes 55300
  7.2 100.8 %copy-start.17 = (bf16[256,1536]{1,0:T(8,128)(2,1)S(1)}, bf16[256,1536]{1,0:T(8,128)(2,1)}, u32[]{:S(2)}) copy-start(bf16[256,1536]{1,0:T(8,128)(2,1)} %param.19) | copy-start | bytes 2359300
  7.3 130.5 %all-gather.9.cloned.1.call-start = ((), (), s32[]{:S(2)}) async-start(), calls=%async_computation.3 | async-start | bytes 20889600 | tf_op jit(solution)/shard_map/all_gather | solution.py:269
  10.2 411.2 %all-gather.13.cloned.1.call-start = ((), (), s32[]{:S(2)}) async-start(), calls=%async_computation.7 | async-start | bytes 14155776 | tf_op jit(solution)/shard_map/all_gather | solution.py:35
  84.2 67.4 %copy-start.41 = (bf16[21392]{0:T(1024)(128)(2,1)}, bf16[21392]{0:T(1024)(128)(2,1)S(1)}, u32[]{:S(2)}) copy-start(bf16[21392]{0:T(1024)(128)(2,1)S(1)} %all-reduce.14) | copy-start | bytes 128356
  86.1 65.6 %copy-start.87 = (f32[256]{0:T(256)}, f32[256]{0:T(256)S(1)}, u32[]{:S(2)}) copy-start(f32[256]{0:T(256)S(1)} %get-tuple-element.411) | copy-start | bytes 3076
  151.7 6.0 collective-permute-start
  175.9 327.3 %all-gather.11.cloned.1.call-start = ((), (), s32[]{:S(2)}) async-start(), calls=%async_computation.4 | async-start | bytes 10027008 | tf_op jit(solution)/shard_map/all_gather | solution.py:271
  178.1 593.4 %all-gather.15.cloned.1.call-start = ((), (), s32[]{:S(2)}) async-start(), calls=%async_computation.8 | async-start | bytes 14155776 | tf_op jit(solution)/shard_map/all_gather | solution.py:35
  178.8 348.0 %copy-start.55 = (f32[3072]{0:T(1024)}, f32[3072]{0:T(1024)S(1)}, u32[]{:S(2)}) copy-start(f32[3072]{0:T(1024)S(1)} %slice.180) | copy-start | bytes 36868
  526.7 473.0 %reduce-scatter.8.cloned.1.call-start = ((), (), s32[]{:S(2)}) async-start(), calls=%async_computation.6 | async-start | bytes 20054016 | tf_op jit(solution)/shard_map/reduce_scatter | solution.py:367
  538.5 684.1 %reduce-scatter.6.cloned.1.call-start = ((), (), s32[]{:S(2)}) async-start(), calls=%async_computation.5 | async-start | bytes 41779200 | tf_op jit(solution)/shard_map/reduce_scatter | solution.py:365
  924.8 5.9 collective-permute-start.1
  947.6 407.0 %all-reduce.22.cloned.1.call-start = ((), (), s32[]{:S(2)}) async-start(), calls=%async_computation.10 | async-start | bytes 172032
  995.2 228.1 %copy-start.9 = (f32[256,3072]{1,0:T(8,128)S(1)}, f32[256,3072]{1,0:T(8,128)}, u32[]{:S(2)}) copy-start(f32[256,3072]{1,0:T(8,128)} %get-tuple-element.410) | copy-start | bytes 9437188
  995.2 228.1 %copy-start.56 = (f32[3072]{0:T(1024)S(1)}, f32[3072]{0:T(1024)}, u32[]{:S(2)}) copy-start(f32[3072]{0:T(1024)} %copy-done.55) | copy-start | bytes 36868
  995.2 228.1 %copy-start.85 = (f32[256]{0:T(256)S(1)}, f32[256]{0:T(256)}, u32[]{:S(2)}) copy-start(f32[256]{0:T(256)} %copy-done.84) | copy-start | bytes 3076
  995.2 228.1 %copy-start.93 = (f32[256]{0:T(256)S(1)}, f32[256]{0:T(256)}, u32[]{:S(2)}) copy-start(f32[256]{0:T(256)} %get-tuple-element.456) | copy-start | bytes 3076
  996.0 429.7 %reduce-scatter.10.cloned.1.call-start = ((), (), s32[]{:S(2)}) async-start(), calls=%async_computation.9 | async-start | bytes 835584
  999.7 591.0 %all-reduce.24.cloned.1.call-start = ((), (), s32[]{:S(2)}) async-start(), calls=%async_computation.11 | async-start | bytes 7274496 | tf_op jit(solution)/shard_map/psum | solution.py:370
  1231.1 359.6 %copy-start.25 = (f32[192,1536]{1,0:T(8,128)S(1)}, f32[192,1536]{1,0:T(8,128)}, u32[]{:S(2)}) copy-start(f32[192,1536]{1,0:T(8,128)} %param.24) | copy-start | bytes 3538948
  1231.1 359.6 %copy-start.38 = (f32[192,1536]{1,0:T(8,128)S(1)}, f32[192,1536]{1,0:T(8,128)}, u32[]{:S(2)}) copy-start(f32[192,1536]{1,0:T(8,128)} %param.32) | copy-start | bytes 3538948
  1231.2 359.6 %copy-start.39 = (f32[192,1536]{1,0:T(8,128)S(1)}, f32[192,1536]{1,0:T(8,128)}, u32[]{:S(2)}) copy-start(f32[192,1536]{1,0:T(8,128)} %param.28) | copy-start | bytes 3538948
  (88 other events, 993.6 us)
Sparse Core Ops, SparseCore 0:
  11.1 126.5 all-gather.8
  176.0 245.4 all-gather.12
  424.5 78.5 all-gather.10
  526.9 244.6 all-gather.14
  775.7 159.9 reduce-scatter.7
  947.7 274.8 reduce-scatter.5
  1225.7 128.8 all-reduce.21
  1359.4 66.2 reduce-scatter.9
  1428.2 162.4 all-reduce.23
where the time goes:
time: 1620 us; the launch traced here: 1610 us
  waiting for transfers between devices  1020 us (63%)
  matrix products  197 us (12%)
  blocking collectives  157 us (10%)
  other arithmetic  125 us (8%)
  local copies, waits for them, and re-layouts  92.2 us (6%)
  between operations  19.6 us (1%)
    all_gather x2, waiting for transfers between devices, prefix(): pieces = jax.tree.map(lambda part: lax.all_gather(part, axis), value)  421 us
    reduce_scatter x1, waiting for transfers between devices, body(): lax.psum_scatter(grad_in_full, 'fsdp', scatter_dimension=0, tiled=True)  223 us
    unnamed x11, waiting for transfers between devices  192 us
    psum x1, waiting for transfers between devices, body(): totals = lax.psum((shards[0], shards[1], shards[2], shards[3]), 'rep')  124 us
    unnamed x2, blocking collectives  100 us
    dot_general x3, matrix products, block_terms(): outputs = jnp.einsum('hts,shp->thp', mixing, heads_x, precision=PRECISE)  56.9 us
    select_n x14, other arithmetic, turn(): jnp.where(position < mine, new, old)  48.4 us
    psum x1, blocking collectives, body(): totals = lax.psum((shards[0], shards[1], shards[2], shards[3]), 'rep')  36.5 us
  transfers between devices with their start and end apart: 11, of which 9 were waited for; matrix products, arithmetic and copies ran while one was open for 21% of the time, Pallas kernels for 0%

commit v1 on v0

v1 whole, which is shorter than its diff:
```python
import jax
import jax.numpy as jnp
from jax import lax
from jax.experimental import pallas as pl
from jax.experimental.pallas import tpu as pltpu
from jax.sharding import PartitionSpec as P

D = 1536
H = 48
P_SIZE = 64
N = 128
CONV = 4
STEP = 10
DI = 3072
CHANNELS = DI + 2 * N
SMALL = 21392
N_FSDP = 16
N_REP = 8
ROWS = 256
PACK = 2048
OWN = DI // N_REP
OWN_H = H // N_REP
OWN_BC = 2 * N // N_REP
SHARD_IN = D // N_FSDP
SHARD_OUT = DI // N_FSDP
SHARD_SMALL = SMALL // N_FSDP
TAIL = 512
WIDE = 384
CHUNK = 128
CHUNKS = PACK // CHUNK
VMEM_LIMIT = 40 * 1024 * 1024

NORM_EPS = 1e-05
BETA_ONE = 0.9
BETA_TWO = 0.999
ADAM_EPS = 1e-08
WEIGHT_DECAY = 0.1
RATE_MATRIX = 0.04
RATE_SMALL = 0.4
PRECISE = lax.Precision.HIGHEST
BF16 = jnp.bfloat16
F32 = jnp.float32


def move(value, target):
    pairs = []
    for f in range(N_FSDP):
        for r in range(N_REP):
            yh, z, c, x, yl = target(f // 8, (f // 2) % 4, f % 2, r // 2, r % 2)
            pairs.append((f * N_REP + r, ((yh % 2) * 8 + (z % 4) * 2 + c % 2) * N_REP + (x % 4) * 2 + yl % 2))
    return lax.ppermute(value, ("fsdp", "rep"), pairs)


def along_x(steps):
    return lambda yh, z, c, x, yl: (yh, z, c, x + steps, yl)


def along_z(steps):
    return lambda yh, z, c, x, yl: (yh, z + steps, c, x, yl)


def swap_y(yh, z, c, x, yl):
    return (yh, z, c, x, yl + 1)


def swap_y_hi(yh, z, c, x, yl):
    return (yh + 1, z, c, x, yl)


def swap_core(yh, z, c, x, yl):
    return (yh, z, c + 1, x, yl)


class Place:
    def __init__(self):
        f = lax.axis_index("fsdp")
        r = lax.axis_index("rep")
        self.f, self.r = f, r
        self.yh, self.z, self.c = f // 8, (f // 2) % 4, f % 2
        self.x, self.yl = r // 2, r % 2


def at(value, index, axis=0):
    return lax.dynamic_index_in_dim(value, index, axis, keepdims=False)


def gather_rep_wide(value, place):
    rows = value.shape[0]
    half = rows // 2
    from_left = move(value, along_x(1))
    from_right = move(value, along_x(-1))
    partner = move(value, swap_y)
    far_top = move(from_left[:half], along_x(1))
    far_low = move(from_right[half:], along_x(-1))
    partner_left = move(from_left, swap_y)
    partner_right_top = move(partner[:half], along_x(-1))
    partner_right_low = move(from_right[half:], swap_y)
    partner_far_top = move(partner_left[:half], along_x(1))
    partner_far_low = move(partner_right_low, along_x(-1))
    pieces = (
        (value, 0, 0, 0),
        (from_left, 3, 0, 0),
        (from_right, 1, 0, 0),
        (partner, 0, 1, 0),
        (far_top, 2, 0, 0),
        (far_low, 2, 0, half),
        (partner_left, 3, 1, 0),
        (partner_right_top, 1, 1, 0),
        (partner_right_low, 1, 1, half),
        (partner_far_top, 2, 1, 0),
        (partner_far_low, 2, 1, half),
    )
    out = jnp.zeros((N_REP * rows, value.shape[1]), value.dtype)
    for piece, dx, dy, start in pieces:
        offset = (((place.x + dx) % 4) * 2 + (place.yl + dy) % 2) * rows + start
        out = lax.dynamic_update_slice(out, piece, (offset, jnp.int32(0)))
    return out


def both(mine, other, second):
    first = jnp.where(second == 0, mine, other)
    last = jnp.where(second == 0, other, mine)
    return jnp.stack([first, last], 0)


def put(out, piece, axis, index):
    starts = [jnp.int32(0)] * out.ndim
    starts[axis] = jnp.int32(index)
    return lax.dynamic_update_slice(out, jnp.expand_dims(piece, axis), tuple(starts))


def gather_ring(pair, step, here, axis=0):
    left = move(pair, step(1))
    right = move(pair, step(-1))
    half = pair.shape[0] // 2
    far = jnp.concatenate([move(left[:half], step(1)), move(right[half:], step(-1))], 0)
    shape = pair.shape[:axis] + (4,) + pair.shape[axis:]
    out = jnp.zeros(shape, pair.dtype)
    for piece, offset in ((pair, 0), (right, 1), (left, 3), (far, 2)):
        out = put(out, piece, axis, (here + offset) % 4)
    return out


def gather_rep(value, place):
    pair = both(value, move(value, swap_y), place.yl)
    out = gather_ring(pair, along_x, place.x)
    return out.reshape((N_REP,) + value.shape)


def gather_halves(halves, place):
    mine = jnp.where(place.c == 0, halves[0], halves[1])
    sent = jnp.where(place.c == 0, halves[1], halves[0])
    cores = both(mine, move(sent, swap_core), place.c)
    pair = both(cores, move(cores, swap_y_hi), place.yh)
    ring = gather_ring(pair, along_z, place.z, 1).reshape((N_FSDP,) + mine.shape)
    return ring, move(ring, swap_core)


def sum_rep(value):
    steps = [move(value, along_x(step)) for step in (1, 3, 2)]
    value = value + steps[0] + steps[1] + steps[2]
    return value + move(value, swap_y)


def sum_all(value):
    value = sum_rep(value)
    steps = [move(value, along_z(step)) for step in (1, 3, 2)]
    value = value + steps[0] + steps[1] + steps[2]
    value = value + move(value, swap_core)
    return value + move(value, swap_y_hi)


def with_rows(block, extra):
    width = block.shape[-1]
    flat = block.reshape(-1, width)
    return flat if extra is None else jnp.concatenate([flat, extra], 0)


def scatter_fsdp(value, extra, place):
    count, width = value.shape[1:]
    split = value.reshape(2, 4, 2, count, width)
    more = 0 if extra is None else extra.shape[0]

    def receive(block, target, base, add_to):
        got = move(with_rows(block, base), target)
        rows = got.shape[0] - more
        return got[:rows].reshape(add_to.shape), got[rows:]

    total = at(split, place.c, 2)
    got, got_extra = receive(at(split, 1 - place.c, 2), swap_core, extra, total)
    total = total + got
    if more:
        extra = extra + got_extra
    z_sum = at(total, place.z, 1)
    found = [receive(at(total, (place.z + step) % 4, 1), along_z(step), extra, z_sum) for step in (1, 3, 2)]
    z_sum = z_sum + found[0][0] + found[1][0] + found[2][0]
    if more:
        extra = extra + found[0][1] + found[1][1] + found[2][1]
    mine = at(z_sum, place.yh)
    got, got_extra = receive(at(z_sum, 1 - place.yh), swap_y_hi, extra, mine)
    if more:
        extra = extra + got_extra
    return mine + got, extra


def rows_to_owners(value, place):
    width = value.shape[1]
    split = value.reshape(4, 2, ROWS, width)
    kept = []
    sent = []
    for step in (0, 1, 3, 2):
        block = at(split, (place.x + step) % 4)
        got = block if step == 0 else move(block, along_x(step))
        kept.append(at(got, place.yl))
        sent.append(at(got, 1 - place.yl))
    other = move(jnp.stack(sent, 0), swap_y)
    out = jnp.zeros((4, 2, ROWS, width), value.dtype)
    zero = jnp.int32(0)
    for k, step in enumerate((0, 1, 3, 2)):
        source = (place.x - step) % 4
        out = lax.dynamic_update_slice(out, kept[k][None, None], (source, place.yl, zero, zero))
        out = lax.dynamic_update_slice(out, other[k][None, None], (source, 1 - place.yl, zero, zero))
    return out.reshape(N_REP, ROWS, width)


def sum_to_owners(value, place):
    count = value.shape[0] // N_REP
    split = value.reshape(4, 2, count, value.shape[1])
    total = at(split, place.x)
    for step in (1, 3, 2):
        total = total + move(at(split, (place.x + step) % 4), along_x(step))
    return at(total, place.yl) + move(at(total, 1 - place.yl), swap_y)


def adam_update(weight, gradient, moment_one, moment_two, learn_rate, decay_rate):
    moment_one = BETA_ONE * moment_one + (1.0 - BETA_ONE) * gradient
    moment_two = BETA_TWO * moment_two + (1.0 - BETA_TWO) * gradient * gradient
    scaled = (
        moment_one
        / (1.0 - BETA_ONE**STEP)
        / (jnp.sqrt(moment_two / (1.0 - BETA_TWO**STEP)) + ADAM_EPS)
    )
    return (weight - learn_rate * (scaled + decay_rate * weight), moment_one, moment_two)


def contract_rows(left_side, right_side):
    return lax.dot_general(
        left_side, right_side, (((0,), (0,)), ((), ())), preferred_element_type=F32
    )


def contract_cols(left_side, right_side):
    return lax.dot_general(
        left_side, right_side, (((1,), (1,)), ((), ())), preferred_element_type=F32
    )


def matmul(left_side, right_side):
    return jnp.dot(left_side, right_side, preferred_element_type=F32)


def segment_at(positions, seg_ends):
    counted = jnp.sum((positions[:, None] >= seg_ends[None, :]).astype(jnp.int32), axis=1)
    return jnp.where(positions < 0, jnp.int32(-1), counted)


def split_two(value):
    high = value.astype(BF16)
    return high, (value - high.astype(F32)).astype(BF16)


def split_three(value):
    high = value.astype(BF16)
    rest = value - high.astype(F32)
    middle = rest.astype(BF16)
    return high, middle, (rest - middle.astype(F32)).astype(BF16)


def product(left, right, left_dim, right_dim):
    return lax.dot_general(
        left, right, (((left_dim,), (right_dim,)), ((), ())), preferred_element_type=F32
    )


def joined_product(left_parts, right_parts, left_dim=1, right_dim=0):
    left_high, left_low = left_parts
    right_high, right_low = right_parts
    return product(
        jnp.concatenate([left_high, left_high, left_low], left_dim),
        jnp.concatenate([right_high, right_low, right_high], right_dim),
        left_dim,
        right_dim,
    )


def precise_product(left, right, left_dim=1, right_dim=0):
    return joined_product(split_two(left), split_two(right), left_dim, right_dim)


def ones_product(ones, value):
    return product(jnp.concatenate([ones] * 3, 1), jnp.concatenate(split_three(value), 0), 1, 0)


def spread(per_head, lane):
    return jnp.concatenate(
        [
            jnp.where(lane < P_SIZE, per_head[:, 2 * k : 2 * k + 1], per_head[:, 2 * k + 1 : 2 * k + 2])
            for k in range(OWN_H // 2)
        ],
        1,
    )


def head_sums(value):
    column = lax.broadcasted_iota(jnp.int32, (OWN, N), 0)
    head = lax.broadcasted_iota(jnp.int32, (OWN, N), 1)
    members = ((column >= head * P_SIZE) & (column < (head + 1) * P_SIZE)).astype(F32).astype(BF16)
    high, low = split_two(value)
    return product(jnp.concatenate([high, low], 1), jnp.concatenate([members, members], 0), 1, 0)


def two_heads(pair, lane):
    zero = jnp.zeros_like(pair)
    return jnp.concatenate([jnp.where(lane < P_SIZE, pair, zero), jnp.where(lane < P_SIZE, zero, pair)], 0)


def chunk_facts(ends, chunk, dt_pre, par):
    column = lax.broadcasted_iota(jnp.int32, (CHUNK, 1), 0) + chunk * CHUNK
    row = lax.broadcasted_iota(jnp.int32, (1, CHUNK), 1) + chunk * CHUNK

    def segment(position):
        counted = jnp.zeros_like(position)
        for k in range(3):
            counted = counted + (position >= ends[k]).astype(jnp.int32)
        return jnp.where(position < 0, -1, counted)

    def one_segment(position):
        counted = jnp.int32(0)
        for k in range(3):
            counted = counted + (position >= ends[k]).astype(jnp.int32)
        return jnp.where(position < 0, -1, counted)

    here_column, here_row = segment(column), segment(row)
    prior = one_segment(chunk * CHUNK - 1)
    last = one_segment(chunk * CHUNK + CHUNK - 1)
    lane = lax.broadcasted_iota(jnp.int32, (CHUNK, N), 1)
    shifted = dt_pre + par[6:7, :N]
    soft = jnp.maximum(shifted, 0.0) + jnp.log1p(jnp.exp(-jnp.abs(shifted)))
    step = jnp.where(lane < OWN_H, soft, 0.0)
    decay = step * par[7:8, :N]
    tri_row = lax.broadcasted_iota(jnp.int32, (CHUNK, CHUNK), 0)
    tri_column = lax.broadcasted_iota(jnp.int32, (CHUNK, CHUNK), 1)
    lower = (tri_row >= tri_column).astype(F32).astype(BF16)
    upper = (tri_row <= tri_column).astype(F32).astype(BF16)
    total = ones_product(lower, decay)
    entering = (here_column == prior).astype(F32) * jnp.exp(total)
    end = total[CHUNK - 1 : CHUNK]
    leaving = (here_column == last).astype(F32) * jnp.exp(jnp.minimum(end - total, 0.0))
    passing = jnp.where(last == prior, 1.0, 0.0) * jnp.exp(end)
    return dict(
        column=column,
        segment=segment,
        here_column=here_column,
        here_row=here_row,
        lane=lane,
        shifted=shifted,
        step=step,
        decay=decay,
        total=total,
        entering=entering,
        leaving=leaving,
        passing=passing,
        tri_row=tri_row,
        tri_column=tri_column,
        upper=upper,
    )


def forward_kernel(ends, proj, par, pre_out, mixed_out, state_out, extended, state):
    chunk = pl.program_id(0)

    @pl.when(chunk == 0)
    def _():
        extended[0:8, :] = jnp.zeros((8, 640), F32)
        state[...] = jnp.zeros_like(state)

    facts = chunk_facts(ends, chunk, proj[:, 1024:1152], par)
    lane = facts["lane"]
    conv = proj[:, OWN:1024].astype(BF16).astype(F32)
    extended[8 : 8 + CHUNK, :] = conv
    pre = par[4:5] + par[3:4] * conv
    for back in range(1, CONV):
        same = (facts["segment"](facts["column"] - back) == facts["here_column"]).astype(F32)
        pre = pre + par[3 - back : 4 - back] * (extended[8 - back : 8 - back + CHUNK, :] * same)
    extended[0:8, :] = extended[CHUNK : CHUNK + 8, :]
    pre_out[...] = pre
    act = pre * jax.nn.sigmoid(pre)
    own_x, state_b, state_c = act[:, :OWN], act[:, OWN : OWN + N], act[:, OWN + N :]
    stepped = own_x * spread(facts["step"], lane)
    b_parts, c_parts = split_two(state_b), split_two(state_c)
    inside = (facts["tri_row"] >= facts["tri_column"]) & (facts["here_column"] == facts["here_row"])
    scores = jnp.where(inside, joined_product(c_parts, b_parts, 1, 1), 0.0)
    total_rows = facts["total"].T
    state_in = state[...]
    state_out[...] = state_in
    outs = []
    for pair in range(OWN_H // 2):
        mixing = []
        for head in (2 * pair, 2 * pair + 1):
            span = facts["total"][:, head : head + 1] - total_rows[head : head + 1, :]
            mixing.append(jnp.exp(jnp.minimum(span, 0.0)) * scores)
        inner = two_heads(stepped[:, pair * N : pair * N + N], lane)
        outs.append(precise_product(jnp.concatenate(mixing, 1), inner))
    scanned = jnp.concatenate(outs, 1) + spread(facts["entering"], lane) * joined_product(
        c_parts, split_two(state_in)
    )
    state[...] = spread(facts["passing"], lane[:1]) * state_in + precise_product(
        state_b.T, stepped * spread(facts["leaving"], lane)
    )
    mixed_out[...] = scanned + par[5:6, :OWN] * own_x


def run_forward(ends, proj, par):
    chunked = lambda width: pl.BlockSpec((CHUNK, width), lambda i: (i, 0))
    return pl.pallas_call(
        forward_kernel,
        grid=(CHUNKS,),
        in_specs=[
            pl.BlockSpec(memory_space=pltpu.SMEM),
            chunked(1152),
            pl.BlockSpec((16, 640), lambda i: (0, 0)),
        ],
        out_specs=[chunked(640), chunked(OWN), pl.BlockSpec((N, OWN), lambda i: (i, 0))],
        out_shape=[
            jax.ShapeDtypeStruct((PACK, 640), F32),
            jax.ShapeDtypeStruct((PACK, OWN), F32),
            jax.ShapeDtypeStruct((CHUNKS * N, OWN), F32),
        ],
        scratch_shapes=[pltpu.VMEM((CHUNK + 8, 640), F32), pltpu.VMEM((N, OWN), F32)],
        compiler_params=pltpu.CompilerParams(
            dimension_semantics=("arbitrary",), vmem_limit_bytes=VMEM_LIMIT
        ),
        cost_estimate=pl.CostEstimate(flops=8_000_000_000, bytes_accessed=24_000_000, transcendentals=3_000_000),
        name="scan_forward",
    )(ends, proj, par)


def backward_kernel(
    ends, conv_in, dt_in, pre_in, mixed_in, grad_mixed, state_all, par,
    grad_x, grad_dt, grad_bc, sums, head_acc,
    carried, extended, end_dot,
):
    step_index = pl.program_id(0)
    chunk = CHUNKS - 1 - step_index

    @pl.when(step_index == 0)
    def _():
        carried[...] = jnp.zeros_like(carried)
        extended[CHUNK : CHUNK + 8, :] = jnp.zeros((8, OWN), F32)
        end_dot[...] = jnp.zeros_like(end_dot)
        sums[...] = jnp.zeros_like(sums)
        head_acc[...] = jnp.zeros_like(head_acc)

    facts = chunk_facts(ends, chunk, dt_in[...], par)
    lane = facts["lane"]
    pre = pre_in[...]
    sig = jax.nn.sigmoid(pre)
    act = pre * sig
    own_x, state_b, state_c = act[:, :OWN], act[:, OWN : OWN + N], act[:, OWN + N :]
    step = facts["step"]
    step_wide = spread(step, lane)
    stepped = own_x * step_wide
    skip = par[5:6, :OWN]
    scanned = mixed_in[...] - skip * own_x
    grad_m = grad_mixed[...]
    sums[6:7] += jnp.sum(grad_m * own_x, 0, keepdims=True)

    b_parts, c_parts = split_two(state_b), split_two(state_c)
    inside = (facts["tri_row"] <= facts["tri_column"]) & (facts["here_column"] == facts["here_row"])
    scores = jnp.where(inside, joined_product(b_parts, c_parts, 1, 1), 0.0)
    total_rows = facts["total"].T
    grad_scores = jnp.zeros((CHUNK, CHUNK), F32)
    grad_stepped = []
    for pair in range(OWN_H // 2):
        columns = slice(pair * N, pair * N + N)
        grad_pair = grad_m[:, columns]
        high, low = split_two(grad_pair)
        stepped_parts = split_two(two_heads(stepped[:, columns], lane))
        grad_mixing = joined_product(stepped_parts, (high, low), 1, 1)
        mixing = []
        for k in range(2):
            head = 2 * pair + k
            span = total_rows[head : head + 1, :] - facts["total"][:, head : head + 1]
            decays = jnp.exp(jnp.minimum(span, 0.0))
            mixing.append(decays * scores)
            grad_scores = grad_scores + decays * grad_mixing[k * CHUNK : (k + 1) * CHUNK]
        grad_stepped.append(
            joined_product(
                split_two(jnp.concatenate(mixing, 1)), (two_heads(high, lane), two_heads(low, lane))
            )
        )
    grad_scores = jnp.where(inside, grad_scores, 0.0)
    carry = carried[...]
    carry_parts = split_two(carry)
    leaving = spread(facts["leaving"], lane)
    grad_stepped = jnp.concatenate(grad_stepped, 1) + leaving * joined_product(b_parts, carry_parts)
    state_in = state_all[...]
    entered = spread(facts["entering"], lane) * grad_m
    entered_parts = split_two(entered)
    grad_b = precise_product(grad_scores, state_c) + joined_product(
        split_two(leaving * stepped), carry_parts, 1, 1
    )
    grad_c = precise_product(grad_scores.T, state_b) + joined_product(
        entered_parts, split_two(state_in), 1, 1
    )
    grad_bc[0:N, :] = grad_b.T
    grad_bc[N:, :] = grad_c.T
    new_carry = spread(facts["passing"], lane[:1]) * carry + joined_product(
        split_two(state_c.T), entered_parts
    )
    carried[...] = new_carry

    grad_step = head_sums(own_x * grad_stepped)
    last_row = lax.broadcasted_iota(jnp.int32, (CHUNK, N), 0) == CHUNK - 1
    grad_total = head_sums(grad_m * scanned) - step * grad_step
    grad_total = grad_total + jnp.where(last_row, end_dot[0:1, :], 0.0)
    grad_decay = ones_product(facts["upper"], grad_total)
    end_dot[...] = head_sums(
        jnp.broadcast_to(jnp.sum(new_carry * state_in, 0, keepdims=True), (8, OWN))
    )
    grad_pre_dt = (grad_step + grad_decay * par[7:8, :N]) * jax.nn.sigmoid(facts["shifted"])
    grad_pre_dt = jnp.where(lane < OWN_H, grad_pre_dt, 0.0)
    grad_dt[...] = grad_pre_dt.astype(BF16)
    head_acc[0:1] += jnp.sum(grad_pre_dt, 0, keepdims=True)
    head_acc[1:2] += jnp.sum(grad_decay * facts["decay"], 0, keepdims=True)

    sig_x, pre_x = sig[:, :OWN], pre[:, :OWN]
    grad_pre = (step_wide * grad_stepped + skip * grad_m) * (sig_x * (1.0 + pre_x * (1.0 - sig_x)))
    extended[0:CHUNK, :] = grad_pre
    conv = conv_in[...].astype(BF16).astype(F32)
    sums[5:6] += jnp.sum(grad_pre, 0, keepdims=True)
    sums[4:5] += jnp.sum(conv * grad_pre, 0, keepdims=True)
    grad_conv = par[3:4, :OWN] * grad_pre
    for ahead in range(1, CONV):
        same = (facts["segment"](facts["column"] + ahead) == facts["here_column"]).astype(F32)
        later = extended[ahead : ahead + CHUNK, :] * same
        sums[4 - ahead : 5 - ahead] += jnp.sum(conv * later, 0, keepdims=True)
        grad_conv = grad_conv + par[3 - ahead : 4 - ahead, :OWN] * later
    extended[CHUNK : CHUNK + 8, :] = extended[0:8, :]
    grad_x[...] = grad_conv.astype(BF16)


def run_backward(ends, proj, pre, mixed, grad_mixed, states, par):
    back = lambda i: (CHUNKS - 1 - i, 0)
    chunked = lambda width: pl.BlockSpec((CHUNK, width), back)
    fixed = lambda shape: pl.BlockSpec(shape, lambda i: (0, 0))
    return pl.pallas_call(
        backward_kernel,
        grid=(CHUNKS,),
        in_specs=[
            pl.BlockSpec(memory_space=pltpu.SMEM),
            pl.BlockSpec((CHUNK, OWN), lambda i: (CHUNKS - 1 - i, 1)),
            pl.BlockSpec((CHUNK, N), lambda i: (CHUNKS - 1 - i, 8)),
            chunked(640),
            chunked(OWN),
            chunked(OWN),
            pl.BlockSpec((N, OWN), back),
            fixed((16, 640)),
        ],
        out_specs=[
            chunked(OWN),
            chunked(N),
            pl.BlockSpec((2 * N, CHUNK), lambda i: (0, CHUNKS - 1 - i)),
            fixed((8, OWN)),
            fixed((8, N)),
        ],
        out_shape=[
            jax.ShapeDtypeStruct((PACK, OWN), BF16),
            jax.ShapeDtypeStruct((PACK, N), BF16),
            jax.ShapeDtypeStruct((2 * N, PACK), F32),
            jax.ShapeDtypeStruct((8, OWN), F32),
            jax.ShapeDtypeStruct((8, N), F32),
        ],
        scratch_shapes=[
            pltpu.VMEM((N, OWN), F32),
            pltpu.VMEM((CHUNK + 8, OWN), F32),
            pltpu.VMEM((8, N), F32),
        ],
        compiler_params=pltpu.CompilerParams(
            dimension_semantics=("arbitrary",), vmem_limit_bytes=VMEM_LIMIT
        ),
        cost_estimate=pl.CostEstimate(flops=20_000_000_000, bytes_accessed=32_000_000, transcendentals=6_000_000),
        name="scan_backward",
    )(ends, proj, proj, pre, mixed, grad_mixed, states, par)


def project_kernel(tokens, gain, w_z, w_x, w_rest, normed_out, proj):
    values = tokens[...].astype(F32)
    scale = lax.rsqrt(jnp.mean(values * values, axis=1, keepdims=True) + NORM_EPS)
    normed = (values * scale * gain[...]).astype(BF16)
    normed_out[...] = normed
    proj[:, :WIDE] = matmul(normed, w_z[...])
    proj[:, WIDE : 2 * WIDE] = matmul(normed, w_x[...])
    proj[:, 2 * WIDE :] = matmul(normed, w_rest[...])


def run_project(tokens, gain, w_z, w_x, w_rest):
    rows = lambda width: pl.BlockSpec((ROWS, width), lambda i: (i, 0))
    fixed = lambda shape: pl.BlockSpec(shape, lambda i: (0, 0))
    return pl.pallas_call(
        project_kernel,
        grid=(PACK // ROWS,),
        in_specs=[rows(D), fixed((1, D)), fixed((D, WIDE)), fixed((D, WIDE)), fixed((D, WIDE))],
        out_specs=[rows(D), rows(3 * WIDE)],
        out_shape=[jax.ShapeDtypeStruct((PACK, D), BF16), jax.ShapeDtypeStruct((PACK, 3 * WIDE), F32)],
        compiler_params=pltpu.CompilerParams(
            dimension_semantics=("arbitrary",), vmem_limit_bytes=VMEM_LIMIT
        ),
        cost_estimate=pl.CostEstimate(flops=7_250_000_000, bytes_accessed=26_000_000, transcendentals=0),
        name="project",
    )(tokens, gain, w_z, w_x, w_rest)


def column_sums(value):
    ones = jnp.ones((8, value.shape[1]), BF16)
    return product(jnp.concatenate([ones] * 3, 1), jnp.concatenate(split_three(value), 1), 1, 1)


def out_grad_kernel(grad_branch, w_out, mixed, gate_in, gain, grad_out, sums):
    total = jnp.zeros((ROWS, WIDE), F32)
    for k in range(4):
        total = total + product(
            grad_branch[:, k * WIDE : (k + 1) * WIDE], w_out[k * WIDE : (k + 1) * WIDE, :], 1, 1
        )
    grad_out[...] = total
    gate = gate_in[...]
    gated = mixed[...] * (gate * jax.nn.sigmoid(gate))
    row = lax.broadcasted_iota(jnp.int32, (8, ROWS), 0)
    sums[...] = jnp.where(row == 0, column_sums(gated * gated), column_sums(total * gain[...] * gated))


def run_out_grad(grad_branch, w_out, mixed, proj, gain):
    rows = lambda width: pl.BlockSpec((ROWS, width), lambda i: (i, 0))
    fixed = lambda shape: pl.BlockSpec(shape, lambda i: (0, 0))
    return pl.pallas_call(
        out_grad_kernel,
        grid=(PACK // ROWS,),
        in_specs=[rows(D), fixed((D, WIDE)), rows(OWN), rows(OWN), fixed((1, OWN))],
        out_specs=[rows(OWN), pl.BlockSpec((8, ROWS), lambda i: (0, i))],
        out_shape=[jax.ShapeDtypeStruct((PACK, OWN), F32), jax.ShapeDtypeStruct((8, PACK), F32)],
        compiler_params=pltpu.CompilerParams(
            dimension_semantics=("arbitrary",), vmem_limit_bytes=VMEM_LIMIT
        ),
        cost_estimate=pl.CostEstimate(flops=2_420_000_000, bytes_accessed=17_000_000, transcendentals=800_000),
        name="out_grad",
    )(grad_branch, w_out, mixed, proj, gain)


def gate_kernel(
    grad_out, mixed_in, gate_in, sums, gain, grad_branch, normed,
    low_out, grad_mixed, grad_weights, grad_gain,
):
    step = pl.program_id(0)
    rows = grad_out.shape[0]
    mixed, gate, grad_o = mixed_in[...], gate_in[...], grad_out[...]
    stats = jnp.concatenate([sums[...], jnp.zeros((N - 8, rows), F32)], 0).T
    out_scale = lax.rsqrt(stats[:, 0:1] * (1.0 / DI) + NORM_EPS)
    pull = out_scale * out_scale * out_scale * (stats[:, 1:2] * (1.0 / DI))
    gate_sig = jax.nn.sigmoid(gate)
    silu = gate * gate_sig
    gated = mixed * silu
    unit = gated * out_scale
    low = (unit * gain[...]).astype(BF16)
    grad_gated = out_scale * (grad_o * gain[...]) - gated * pull
    grad_mixed[...] = grad_gated * silu
    grad_z = (grad_gated * mixed * (gate_sig * (1.0 + gate * (1.0 - gate_sig)))).astype(BF16)
    low_out[:, :OWN] = low
    low_out[:, OWN:] = grad_z
    gain_part = jnp.sum(grad_o * unit, 0, keepdims=True)

    @pl.when(step == 0)
    def _():
        grad_gain[...] = jnp.zeros_like(grad_gain)
        grad_weights[...] = jnp.zeros_like(grad_weights)

    grad_gain[0:1] += gain_part
    for k in range(4):
        part = product(low, grad_branch[:, k * WIDE : (k + 1) * WIDE], 0, 0)
        for m in range(4):
            grad_weights[4 * k + m, :SHARD_IN] += part[m * SHARD_IN : (m + 1) * SHARD_IN]
    part = product(normed[...], grad_z, 0, 0)
    for f in range(N_FSDP):
        grad_weights[f, SHARD_IN:] += part[f * SHARD_IN : (f + 1) * SHARD_IN]


def run_gate(grad_out, mixed, proj, sums, gain, grad_branch, normed):
    count = 256
    rows = lambda width: pl.BlockSpec((count, width), lambda i: (i, 0))
    fixed = lambda shape: pl.BlockSpec(shape, lambda i: (0,) * len(shape))
    return pl.pallas_call(
        gate_kernel,
        grid=(PACK // count,),
        in_specs=[
            rows(OWN),
            rows(OWN),
            rows(OWN),
            pl.BlockSpec((8, count), lambda i: (0, i)),
            fixed((1, OWN)),
            rows(D),
            rows(D),
        ],
        out_specs=[rows(2 * OWN), rows(OWN), fixed((N_FSDP, 2 * SHARD_IN, WIDE)), fixed((8, OWN))],
        out_shape=[
            jax.ShapeDtypeStruct((PACK, 2 * OWN), BF16),
            jax.ShapeDtypeStruct((PACK, OWN), F32),
            jax.ShapeDtypeStruct((N_FSDP, 2 * SHARD_IN, WIDE), F32),
            jax.ShapeDtypeStruct((8, OWN), F32),
        ],
        compiler_params=pltpu.CompilerParams(
            dimension_semantics=("arbitrary",), vmem_limit_bytes=VMEM_LIMIT
        ),
        cost_estimate=pl.CostEstimate(flops=4_840_000_000, bytes_accessed=34_000_000, transcendentals=800_000),
        name="gate_backward",
    )(grad_out, mixed, proj, sums, gain, grad_branch, normed)


def body(
    tokens,
    cotangent,
    lengths,
    w_in,
    w_dt,
    w_out,
    small,
    first_in,
    first_dt,
    first_out,
    first_small,
    second_in,
    second_dt,
    second_out,
    second_small,
):
    place = Place()
    r = place.r
    pack_lengths = lax.dynamic_slice_in_dim(lengths, place.f, 1, 0)[0]
    seg_ends = jnp.cumsum(pack_lengths)
    own_positions = r * ROWS + jnp.arange(ROWS, dtype=jnp.int32)
    own_live = (segment_at(own_positions, seg_ends) < 3).astype(F32)

    full_tokens = gather_rep_wide(tokens, place)
    own_branch = (cotangent.astype(F32) * own_live[:, None]).astype(BF16)
    own_branch, _ = lax.optimization_barrier((own_branch, full_tokens))
    grad_branch = gather_rep_wide(own_branch, place)

    in_low = w_in.astype(BF16)
    out_low_shard = w_out.astype(BF16)
    dt_low = w_dt.astype(BF16)
    small_rows = jnp.pad(small.astype(BF16), (0, 4 * WIDE - SHARD_SMALL)).reshape(4, WIDE)
    small_rows = jnp.concatenate([small_rows, jnp.zeros((12, WIDE), BF16)], 0)
    zero = jnp.int32(0)
    out_piece = lax.dynamic_slice(
        out_low_shard, (SHARD_IN * (place.x // 2), WIDE * ((place.x % 2) * 2 + place.yl)), (SHARD_IN, WIDE)
    )
    out_piece = move(
        out_piece, lambda yh, z, c, x, yl: (x % 2, yl * 2 + c, x // 2, yh * 2 + z // 2, z % 2)
    )
    rest = jnp.concatenate(
        [
            in_low[:, 2 * DI :],
            lax.dynamic_slice_in_dim(dt_low, r * OWN_H, OWN_H, 1),
            jnp.zeros((SHARD_IN, 2), BF16),
            dt_low,
            jnp.zeros((SHARD_IN, N - 8 - H), BF16),
        ],
        1,
    )
    first_halves = [
        jnp.concatenate([lax.dynamic_slice_in_dim(in_low, DI + r * OWN, OWN, 1), small_rows], 0),
        jnp.concatenate([rest, small_rows], 0),
    ]
    first_mine, first_other = gather_halves(first_halves, place)
    second_mine, second_other = gather_halves(
        [lax.dynamic_slice_in_dim(in_low, r * OWN, OWN, 1), out_piece], place
    )
    vector = first_mine[:, SHARD_IN : SHARD_IN + 4].reshape(N_FSDP, 4 * WIDE)[:, :SHARD_SMALL]
    vector = vector.reshape(-1).astype(F32)
    first_mine, first_other = first_mine[:, :SHARD_IN], first_other[:, :SHARD_IN]

    def ordered(mine, other):
        return (
            jnp.where(place.c == 0, mine, other).reshape(D, WIDE),
            jnp.where(place.c == 0, other, mine).reshape(D, WIDE),
        )

    slice_x, slice_rest = ordered(first_mine, first_other)
    slice_z, slice_out = ordered(second_mine, second_other)
    full_dt = slice_rest[:, 2 * N + 8 : 2 * N + 8 + H]

    in_low, _ = lax.optimization_barrier((in_low, second_other))
    full_in = lax.all_gather(in_low, "fsdp", axis=0, tiled=True)
    out_low_shard, _ = lax.optimization_barrier((out_low_shard, full_in))
    full_out = lax.all_gather(out_low_shard, "fsdp", axis=0, tiled=True)

    offset = 0
    gain_in = vector[:D]
    offset = D
    gain_out = lax.dynamic_slice_in_dim(vector, offset + r * OWN, OWN, 0)
    offset += DI
    taps = vector[offset : offset + (CONV + 1) * CHANNELS].reshape(CONV + 1, CHANNELS)
    offset += (CONV + 1) * CHANNELS
    per_head = vector[offset:].reshape(3, H)
    dt_bias, a_log, d_skip = lax.dynamic_slice_in_dim(per_head, r * OWN_H, OWN_H, 1)
    taps_bc = taps[:, DI:]
    conv_par = jnp.concatenate([lax.dynamic_slice_in_dim(taps, r * OWN, OWN, 1), taps_bc], 1)
    head_par = jnp.stack(
        [
            jnp.pad(jnp.broadcast_to(d_skip[:, None], (OWN_H, P_SIZE)).reshape(-1), (0, 2 * N)),
            jnp.pad(dt_bias, (0, 640 - OWN_H)),
            jnp.pad(-jnp.exp(a_log), (0, 640 - OWN_H)),
        ],
        0,
    )
    par = jnp.concatenate([conv_par, head_par, jnp.zeros((8, 640), F32)], 0)
    gain_row = gain_out[None, :]

    normed, proj = run_project(full_tokens, gain_in[None, :], slice_z, slice_x, slice_rest)
    pre, mixed, states = run_forward(seg_ends, proj, par)
    grad_normed_out, sums = run_out_grad(grad_branch, slice_out, mixed, proj, gain_row)
    sums = jnp.concatenate([sum_rep(sums[:2].reshape(32, 128)).reshape(2, PACK), jnp.zeros((6, PACK), F32)], 0)

    low_rows, grad_mixed, early_grads, grad_gain = run_gate(
        grad_normed_out, mixed, proj, sums, gain_row, grad_branch, normed
    )
    first_rows = rows_to_owners(low_rows, place)
    early_part, _ = scatter_fsdp(early_grads, None, place)
    out_part = move(
        early_part[:SHARD_IN],
        lambda yh, z, c, x, yl: (x // 2, (x % 2) * 2 + yl, z % 2, 2 * c + yh, z // 2),
    )
    early_parts = gather_rep(jnp.concatenate([out_part, early_part[SHARD_IN:]], 0), place)
    grad_out = early_parts[:, :SHARD_IN].reshape(2, 4, SHARD_IN, WIDE).transpose(0, 2, 1, 3).reshape(SHARD_OUT, D)
    z_parts = early_parts[:, SHARD_IN:]

    grad_x, grad_dtraw, grad_bc, grad_sums, grad_heads = run_backward(
        seg_ends, proj, pre, mixed, grad_mixed, states, par
    )
    grad_bc = sum_to_owners(grad_bc, place)
    own_taps = lax.dynamic_slice_in_dim(taps_bc, r * OWN_BC, OWN_BC, 1)
    own_pre = lax.dynamic_slice_in_dim(pre, OWN + r * OWN_BC, OWN_BC, 1).T
    own_conv = lax.dynamic_slice_in_dim(proj, 2 * OWN + r * OWN_BC, OWN_BC, 1).T
    own_conv = own_conv.astype(BF16).astype(F32)
    sig = jax.nn.sigmoid(own_pre)
    grad_pre = grad_bc * (sig * (1.0 + own_pre * (1.0 - sig)))
    positions = jnp.arange(PACK, dtype=jnp.int32)
    segments = segment_at(positions, seg_ends)
    grad_conv_bc = own_taps[CONV - 1][:, None] * grad_pre
    grad_taps_bc = [jnp.sum(own_conv * grad_pre, 1)]
    for ahead in range(1, CONV):
        same = (segment_at(positions + ahead, seg_ends) == segments) & (positions + ahead < PACK)
        later = jnp.concatenate([grad_pre[:, ahead:], jnp.zeros((OWN_BC, ahead), F32)], 1)
        later = later * same.astype(F32)[None, :]
        grad_taps_bc.insert(0, jnp.sum(own_conv * later, 1))
        grad_conv_bc = grad_conv_bc + own_taps[CONV - 1 - ahead][:, None] * later
    grad_bias_bc = jnp.sum(grad_pre, 1)
    grad_tail = jnp.concatenate(
        [
            grad_x,
            grad_conv_bc.T.astype(BF16),
            grad_dtraw[:, :OWN_H],
            jnp.zeros((PACK, TAIL - OWN - OWN_BC - OWN_H), BF16),
        ],
        1,
    )

    grad_tail_own = contract_rows(normed, grad_tail).reshape(N_FSDP, SHARD_IN, TAIL)
    row = lambda value: jnp.pad(value, (0, OWN - value.shape[0]))[None, :]
    head_columns = jnp.concatenate(
        [grad_gain[0:1]]
        + [grad_sums[1:6]]
        + [row(grad_heads[1, :OWN_H]), row(grad_sums[6].reshape(OWN_H, P_SIZE).sum(1))],
        0,
    )
    bc_columns = jnp.stack(
        [jnp.pad(grad_heads[0, :OWN_H], (0, OWN_BC - OWN_H))]
        + grad_taps_bc
        + [grad_bias_bc, jnp.zeros_like(grad_bias_bc), jnp.zeros_like(grad_bias_bc)],
        0,
    )
    small_own = jnp.concatenate(
        [head_columns, bc_columns, jnp.zeros((8, TAIL - OWN - OWN_BC), F32)], 1
    )

    tail_part, small_sum = scatter_fsdp(grad_tail_own, small_own, place)
    tail_parts = gather_rep(jnp.concatenate([tail_part, small_sum], 0), place)
    small_parts = tail_parts[:, SHARD_IN:]
    tail_parts = tail_parts[:, :SHARD_IN]

    def columns(parts):
        return parts.transpose(1, 0, 2).reshape(parts.shape[1], -1)

    grad_in = jnp.concatenate(
        [columns(z_parts), columns(tail_parts[:, :, :OWN]), columns(tail_parts[:, :, OWN : OWN + OWN_BC])], 1
    )
    grad_dt = columns(tail_parts[:, :, OWN + OWN_BC : OWN + OWN_BC + OWN_H])

    tail_rows = rows_to_owners(grad_tail, place)
    row_grads = jnp.concatenate(
        [columns(first_rows[:, :, OWN:]), columns(tail_rows[:, :, :OWN]), columns(tail_rows[:, :, OWN : OWN + OWN_BC])], 1
    )
    dt_rows = columns(tail_rows[:, :, OWN + OWN_BC : OWN + OWN_BC + OWN_H])
    grad_h = contract_cols(row_grads, full_in) + contract_cols(dt_rows, full_dt)
    own_inputs = tokens.astype(F32)
    own_scale = lax.rsqrt(jnp.mean(own_inputs * own_inputs, axis=1, keepdims=True) + NORM_EPS)
    unit = own_inputs * own_scale
    grad_gain_in = sum_all(jnp.sum(grad_h * unit, 0).reshape(12, 128)).reshape(-1)
    grad_unit = grad_h * gain_in[None, :]
    grad_inputs = own_scale * (grad_unit - unit * jnp.mean(grad_unit * unit, axis=1, keepdims=True))
    input_grad = cotangent.astype(F32) + grad_inputs

    branch = matmul(columns(first_rows[:, :, :OWN]), full_out)
    block_out = own_inputs + own_live[:, None] * branch

    def channels(row):
        return jnp.concatenate(
            [small_parts[:, row, :OWN].reshape(-1), small_parts[:, row, OWN : OWN + OWN_BC].reshape(-1)]
        )

    grad_small_all = jnp.concatenate(
        [grad_gain_in, small_parts[:, 0, :OWN].reshape(-1)]
        + [channels(row) for row in range(1, 6)]
        + [
            small_parts[:, 0, OWN : OWN + OWN_H].reshape(-1),
            small_parts[:, 6, :OWN_H].reshape(-1),
            small_parts[:, 7, :OWN_H].reshape(-1),
        ]
    )
    grad_small = lax.dynamic_slice_in_dim(grad_small_all, place.f * SHARD_SMALL, SHARD_SMALL, 0)

    new_in, new_first_in, new_second_in = adam_update(
        w_in, grad_in, first_in, second_in, RATE_MATRIX, WEIGHT_DECAY
    )
    new_dt, new_first_dt, new_second_dt = adam_update(
        w_dt, grad_dt, first_dt, second_dt, RATE_MATRIX, WEIGHT_DECAY
    )
    new_out, new_first_out, new_second_out = adam_update(
        w_out, grad_out, first_out, second_out, RATE_MATRIX, WEIGHT_DECAY
    )
    new_small, new_first_small, new_second_small = adam_update(
        small, grad_small, first_small, second_small, RATE_SMALL, 0.0
    )
    return (
        block_out,
        input_grad,
        grad_in,
        grad_dt,
        grad_out,
        grad_small,
        new_first_in,
        new_first_dt,
        new_first_out,
        new_first_small,
        new_second_in,
        new_second_dt,
        new_second_out,
        new_second_small,
        new_in,
        new_dt,
        new_out,
        new_small,
    )


def solution(mesh):
    rows = P(("fsdp", "rep"), None)
    matrix = P("fsdp", None)
    vector = P("fsdp")
    group = (matrix, matrix, matrix, vector)
    return jax.shard_map(
        body,
        mesh=mesh,
        in_specs=(rows, rows, P()) + group * 3,
        out_specs=(rows, rows) + group * 4,
        check_vma=False,
    )
```

time: 1620 us -> 687 us (0.42)
  waiting for transfers between devices: 1020 us -> 227 us
  matrix products: 197 us -> 27.2 us
  blocking collectives: 157 us -> 0 us
  starting transfers between devices: 5.11 us -> 138 us
  Pallas kernels: 0 us -> 94.2 us
  other arithmetic: 125 us -> 36.7 us
  local copies, waits for them, and re-layouts: 92.2 us -> 135 us
    all_gather x4 -> x2, waiting for transfers between devices: 472 us -> 0.01 us  [the longest x1 0.01 us: body(): full_in = lax.all_gather(in_low, 'fsdp', axis=0, tiled=True)]
    ppermute x2 -> x81, waiting for transfers between devices: 4.45 us -> 227 us  [move(): return lax.ppermute(value, ('fsdp', 'rep'), pairs)]
    reduce_scatter x2 -> x0, waiting for transfers between devices: 223 us -> none  [the longest x1 223 us: body(): lax.psum_scatter(grad_in_full, 'fsdp', scatter_dimension=0, tiled=True)]
    unnamed x11 -> x2, waiting for transfers between devices: 192 us -> 0.03 us
    ppermute x2 -> x81, starting transfers between devices: 4.53 us -> 138 us  [move(): return lax.ppermute(value, ('fsdp', 'rep'), pairs)]
    dot_general x19 -> x1, matrix products: 140 us -> 7.44 us  [matmul(): return jnp.dot(left_side, right_side, preferred_element_type=F32)]
    psum x1 -> x0, waiting for transfers between devices: 124 us -> none  [body(): totals = lax.psum((shards[0], shards[1], shards[2], shards[3]), 'rep')]
    unnamed x2 -> x0, blocking collectives: 100 us -> none
  transfers between devices with their start and end apart: 11 -> 83, of which waited for: 9 -> 36; matrix products, arithmetic and copies ran while one was open for 21% -> 27% of each run, Pallas kernels for 0% -> 14%
where the time goes in v1:
time: 687 us; the launch traced here: 675 us
  waiting for transfers between devices  227 us (33%)
  starting transfers between devices  138 us (20%)
  local copies, waits for them, and re-layouts  135 us (20%)
  Pallas kernels  94.2 us (14%)
  other arithmetic  36.7 us (5%)
  matrix products  27.2 us (4%)
  between operations  16.5 us (2%)
    ppermute x81, waiting for transfers between devices, move(): return lax.ppermute(value, ('fsdp', 'rep'), pairs)  227 us
    ppermute x81, starting transfers between devices, move(): return lax.ppermute(value, ('fsdp', 'rep'), pairs)  138 us
    pallas_call x1, Pallas kernels, run_backward(): pl.pallas_call(backward_kernel, grid=(CHUNKS,), in_specs=[pl.BlockSpec(me...  32.1 us
    pallas_call x1, Pallas kernels, run_forward(): pl.pallas_call(forward_kernel, grid=(CHUNKS,), in_specs=[pl.BlockSpec(mem...  20.4 us
    dynamic_update_slice x22, local copies, waits for them, and re-layouts, gather_rep_wide(): out = lax.dynamic_update_slice(out, piece, (offset, jnp.int32(0)))  18.5 us
    dynamic_update_slice x8, local copies, waits for them, and re-layouts, rows_to_owners(): lax.dynamic_update_slice(out, kept[k][None, None], (source, place.yl, zer...  17.7 us
    pallas_call x1, Pallas kernels, run_gate(): pl.pallas_call(gate_kernel, grid=(PACK // count,), in_specs=[rows(OWN), r...  16.3 us
    pallas_call x1, Pallas kernels, run_project(): pl.pallas_call(project_kernel, grid=(PACK // ROWS,), in_specs=[rows(D), f...  15.8 us
  transfers between devices with their start and end apart: 83, of which 36 were waited for; matrix products, arithmetic and copies ran while one was open for 27% of the time, Pallas kernels for 14%

profile of v1, /device:TPU:0, one launch (start us, length us, event | category | flops | bytes accessed | tf_op | source)
XLA Modules:
  0.0 674.6 jit_solution(15367682818564366990)
XLA Ops:
  17.1 6.6 collective-permute-start.22
  34.6 6.7 collective-permute-done.24
  68.6 24.2 %collective-permute-done.29 = bf16[2,112,384]{2,1,0:T(8,128)(2,1)S(1)} collective-permute-done((bf16[2,112,384]{2,1,0:T(8,128)(2,1)S(1)}, bf16[2,112,384]{2,1,0:T(8,128)(2,1)S(1)}, u32[]{:S(2)}, u32[]{:S(2)}) %collective-permute-start.29) | collective-permute-done | bytes 172064 | tf_op jit(solution)/shard_map/ppermute | solution.py:51
  97.0 11.7 %collective-permute-done.30 = bf16[2,2,112,384]{3,2,1,0:T(8,128)(2,1)S(1)} collective-permute-done((bf16[2,2,112,384]{3,2,1,0:T(8,128)(2,1)S(1)}, bf16[2,2,112,384]{3,2,1,0:T(8,128)(2,1)S(1)}, u32[]{:S(2)}, u32[]{:S(2)}) %collective-permute-start.30) | collective-permute-done | bytes 344096 | tf_op jit(solution)/shard_map/ppermute | solution.py:51
  142.5 28.9 %collective-permute-done.5 = bf16[256,1536]{1,0:T(8,128)(2,1)} collective-permute-done((bf16[256,1536]{1,0:T(8,128)(2,1)}, bf16[256,1536]{1,0:T(8,128)(2,1)}, u32[]{:S(2)}, u32[]{:S(2)}) %collective-permute-start.5) | collective-permute-done | bytes 786464 | tf_op jit(solution)/shard_map/ppermute | solution.py:51
  187.3 15.8 %project.1 = (bf16[2048,1536]{1,0:T(8,128)(2,1)S(1)}, f32[2048,1152]{1,0:T(8,128)}) custom-call(bf16[2048,1536]{1,0:T(8,128)(2,1)} %constant_dynamic-update-slice_fusion.13.tokens, f32[1,1536]{1,0:T(1,128)S(1)} %broadcast_in_dim.171.gain, bf16[1536,384]{1,0:T(8,128)(2,1)S(1)} %bitcast.343, bf16[1536,384]{1,0:T(8,128)(2,1)S(1)} %bitcast.344, ...), custom_call_target="tpu_custom_call" | custom-call | flops 7249999872 | bytes 26000000 | tf_op jit(solution)/shard_map/project/pallas_call | solution.py:610
  205.8 20.4 %scan_forward.1 = (f32[2048,640]{1,0:T(8,128)S(1)}, f32[2048,384]{1,0:T(8,128)S(1)}, f32[2048,384]{1,0:T(8,128)S(1)}) custom-call(s32[3]{0:T(128)S(1)} %bitcast.348, f32[2048,1152]{1,0:T(8,128)} %get-tuple-element.38.proj.gate_in.conv_in.dt_in, f32[16,640]{1,0:T(8,128)S(1)} %concatenate.87.par), custom_call_target="tpu_custom_call" | custom-call | flops 8000000000 | bytes 24000000 | tf_op jit(solution)/shard_map/scan_forward/pallas_call | solution.py:425
  233.7 6.4 collective-permute-done.17
  240.3 10.7 %collective-permute-done.15 = bf16[256,1536]{1,0:T(8,128)(2,1)S(1)} collective-permute-done((bf16[256,1536]{1,0:T(8,128)(2,1)S(1)}, bf16[256,1536]{1,0:T(8,128)(2,1)S(1)}, u32[]{:S(2)}, u32[]{:S(2)}) %collective-permute-start.15) | collective-permute-done | bytes 786464 | tf_op jit(solution)/shard_map/ppermute | solution.py:51
  252.7 7.3 %collective-permute-done.18 = bf16[128,1536]{1,0:T(8,128)(2,1)S(1)} collective-permute-done((bf16[128,1536]{1,0:T(8,128)(2,1)S(1)}, bf16[128,1536]{1,0:T(8,128)(2,1)S(1)}, u32[]{:S(2)}, u32[]{:S(2)}) %collective-permute-start.18) | collective-permute-done | bytes 393248 | tf_op jit(solution)/shard_map/ppermute | solution.py:51
  260.1 9.6 %out_grad.1 = (f32[2048,384]{1,0:T(8,128)S(1)}, f32[8,2048]{1,0:T(8,128)S(1)}) custom-call(bf16[2048,1536]{1,0:T(8,128)(2,1)S(1)} %constant_dynamic-update-slice_fusion.2.grad_branch, bf16[1536,384]{1,0:T(8,128)(2,1)S(1)} %bitcast.336, f32[2048,384]{1,0:T(8,128)S(1)} %get-tuple-element.39.mixed.mixed_in, ...), custom_call_target="tpu_custom_call" | custom-call | flops 2420000000 | bytes 17000000 | tf_op jit(solution)/shard_map/out_grad/pallas_call | solution.py:645
  286.1 16.3 %gate_backward.1 = (bf16[2048,768]{1,0:T(8,128)(2,1)S(1)}, f32[2048,384]{1,0:T(8,128)S(1)}, f32[16,192,384]{2,1,0:T(8,128)}, f32[8,384]{1,0:T(8,128)S(1)}) custom-call(f32[2048,384]{1,0:T(8,128)S(1)} %copy-done.5, f32[2048,384]{1,0:T(8,128)S(1)} %get-tuple-element.39.mixed.mixed_in, f32[2048,1152]{1,0:T(8,128)} %get-tuple-element.38.proj.gate_in.conv_in.dt_in, ...), custom_call_target="tpu_custom_call" | custom-call | flops 4840000000 | bytes 34000000 | tf_op jit(solution)/shard_map/gate_backward/pallas_call | solution.py:700
  302.4 32.1 %scan_backward.1 = (bf16[2048,384]{1,0:T(8,128)(2,1)S(1)}, bf16[2048,128]{1,0:T(8,128)(2,1)S(1)}, f32[256,2048]{1,0:T(8,128)S(1)}, f32[8,384]{1,0:T(8,128)S(1)}, f32[8,128]{1,0:T(8,128)S(1)}) custom-call(s32[3]{0:T(128)S(1)} %bitcast.349, f32[2048,1152]{1,0:T(8,128)} %get-tuple-element.38.proj.gate_in.conv_in.dt_in, ...), custom_call_target="tpu_custom_call" | custom-call | flops 20000000000 | bytes 32000000 | tf_op jit(solution)/shard_map/scan_backward/pallas_call | solution.py:557
  343.0 9.7 %collective-permute-done.43 = f32[2,32,2048]{2,1,0:T(8,128)S(1)} collective-permute-done((f32[2,32,2048]{2,1,0:T(8,128)S(1)}, f32[2,32,2048]{2,1,0:T(8,128)S(1)}, u32[]{:S(2)}, u32[]{:S(2)}) %collective-permute-start.43) | collective-permute-done | bytes 524320 | tf_op jit(solution)/shard_map/ppermute | solution.py:51
  352.7 7.6 %collective-permute-done.45 = f32[2,32,2048]{2,1,0:T(8,128)S(1)} collective-permute-done((f32[2,32,2048]{2,1,0:T(8,128)S(1)}, f32[2,32,2048]{2,1,0:T(8,128)S(1)}, u32[]{:S(2)}, u32[]{:S(2)}) %collective-permute-start.45) | collective-permute-done | bytes 524320 | tf_op jit(solution)/shard_map/ppermute | solution.py:51
  397.0 9.7 %collective-permute-done.48 = bf16[2,256,512]{2,1,0:T(8,128)(2,1)} collective-permute-done((bf16[2,256,512]{2,1,0:T(8,128)(2,1)}, bf16[2,256,512]{2,1,0:T(8,128)(2,1)}, u32[]{:S(2)}, u32[]{:S(2)}) %collective-permute-start.48) | collective-permute-done | bytes 524320 | tf_op jit(solution)/shard_map/ppermute | solution.py:51
  419.8 24.9 %collective-permute-done.50 = bf16[4,256,512]{2,1,0:T(8,128)(2,1)S(1)} collective-permute-done((bf16[4,256,512]{2,1,0:T(8,128)(2,1)S(1)}, bf16[4,256,512]{2,1,0:T(8,128)(2,1)S(1)}, u32[]{:S(2)}, u32[]{:S(2)}) %collective-permute-start.50) | collective-permute-done | bytes 1048608 | tf_op jit(solution)/shard_map/ppermute | solution.py:51
  491.1 16.8 %collective-permute-done.63 = f32[200,512]{1,0:T(8,128)S(1)} collective-permute-done((f32[200,512]{1,0:T(8,128)S(1)}, f32[200,512]{1,0:T(8,128)S(1)}, u32[]{:S(2)}, u32[]{:S(2)}) %collective-permute-start.63) | collective-permute-done | bytes 409632 | tf_op jit(solution)/shard_map/ppermute | solution.py:51
  522.8 9.0 %collective-permute-done.52 = f32[384,384]{1,0:T(8,128)} collective-permute-done((f32[384,384]{1,0:T(8,128)}, f32[384,384]{1,0:T(8,128)}, u32[]{:S(2)}, u32[]{:S(2)}) %collective-permute-start.52) | collective-permute-done | bytes 589856 | tf_op jit(solution)/shard_map/ppermute | solution.py:51
  531.8 5.8 collective-permute-done.53
  553.5 7.0 %collective-permute-start.57 = (f32[192,384]{1,0:T(8,128)S(1)}, f32[192,384]{1,0:T(8,128)S(1)}, u32[]{:S(2)}, u32[]{:S(2)}) collective-permute-start(f32[192,384]{1,0:T(8,128)S(1)} %pad_maximum_fusion.10), channel_id=1, source_target_pairs={{0,1},{1,0},{2,3},{3,2},{4,5},{5,4},{6,7},{7,6},{8,9},{9,8},{10,11... | collective-permute-start | bytes 884744 | tf_op jit(solution)/shard_map/ppermute | solution.py:51
  613.0 11.6 %fusion.18 = (f32[1536]{0:T(1024)S(1)}, f32[256]{0:T(256)S(1)}, f32[256,1536]{1,0:T(8,128)}) fusion(bf16[256,1536]{1,0:T(8,128)(2,1)S(1)} %copy-done.16, f32[256]{0:T(256)S(1)} %copy-done.65, f32[1536]{0:T(1024)S(1)} %copy-done.40, f32[256,1536]{1,0:T(8,128)} %fusion.37, bf16[1536,6400]{1,0:T(8,128)(2,1)} %all-gather.3.cloned.1.call-done, ...), kind=kOutput, calls=%fused_computation.29 | convolution fusion | flops 5046138880 | bytes 26884096 | tf_op jit(solution)/shard_map/dot_general | solution.py:253
  636.2 5.8 multiply_subtract_fusion
  659.9 7.4 %fusion.6 = f32[256,1536]{1,0:T(8,128)} fusion(bf16[256,3072]{0,1:T(8,128)(2,1)S(1)} %bitcast.351, bf16[3072,1536]{1,0:T(8,128)(2,1)} %all-gather.5.cloned.1.call-done, bf16[256,1536]{1,0:T(8,128)(2,1)S(1)} %copy-done.16, f32[256]{0:T(256)S(1)} %copy-done.58), kind=kOutput, calls=%fused_computation.8 | convolution fusion | flops 2417098752 | bytes 13370368 | tf_op jit(solution)/shard_map/dot_general | solution.py:259
  (566 shorter events, 346.2 us)
Async XLA Ops:
  7.2 442.3 %all-gather.3.cloned.1.call-start = ((), (), s32[]{:S(2)}) async-start(), calls=%async_computation | async-start | bytes 20889600 | tf_op jit(solution)/shard_map/all_gather | solution.py:801
  50.7 609.2 %all-gather.5.cloned.1.call-start = ((), (), s32[]{:S(2)}) async-start(), calls=%async_computation.1 | async-start | bytes 10027008 | tf_op jit(solution)/shard_map/all_gather | solution.py:803
  50.8 67.4 %collective-permute-start = (bf16[256,1536]{1,0:T(8,128)(2,1)S(1)}, bf16[256,1536]{1,0:T(8,128)(2,1)}, u32[]{:S(2)}, u32[]{:S(2)}) collective-permute-start(bf16[256,1536]{1,0:T(8,128)(2,1)S(1)} %copy-done.15), channel_id=1, source_target_pairs={{0,2},{1,3},{2,4},{3,5},{4,6},{5,7},{6,0},{7,1},{8,10},{9,11},{10,... | collective-permute-start | bytes 2359304 | tf_op jit(solution)/shard_map/ppermute | solution.py:51
  52.6 63.1 %collective-permute-start.1 = (bf16[256,1536]{1,0:T(8,128)(2,1)S(1)}, bf16[256,1536]{1,0:T(8,128)(2,1)}, u32[]{:S(2)}, u32[]{:S(2)}) collective-permute-start(bf16[256,1536]{1,0:T(8,128)(2,1)S(1)} %copy-done.15), channel_id=1, source_target_pairs={{0,6},{1,7},{2,0},{3,1},{4,2},{5,3},{6,4},{7,5},{8,14},{9,15},{10,... | collective-permute-start | bytes 2359304 | tf_op jit(solution)/shard_map/ppermute | solution.py:51
  55.3 64.8 %collective-permute-start.2 = (bf16[256,1536]{1,0:T(8,128)(2,1)S(1)}, bf16[256,1536]{1,0:T(8,128)(2,1)}, u32[]{:S(2)}, u32[]{:S(2)}) collective-permute-start(bf16[256,1536]{1,0:T(8,128)(2,1)S(1)} %copy-done.15), channel_id=1, source_target_pairs={{0,1},{1,0},{2,3},{3,2},{4,5},{5,4},{6,7},{7,6},{8,9},{9,8},{10,11... | collective-permute-start | bytes 2359304 | tf_op jit(solution)/shard_map/ppermute | solution.py:51
  128.7 47.4 %collective-permute-start.6 = (bf16[128,1536]{1,0:T(8,128)(2,1)S(1)}, bf16[128,1536]{1,0:T(8,128)(2,1)}, u32[]{:S(2)}, u32[]{:S(2)}) collective-permute-start(bf16[128,1536]{1,0:T(8,128)(2,1)S(1)} %slice.359), channel_id=1, source_target_pairs={{0,6},{1,7},{2,0},{3,1},{4,2},{5,3},{6,4},{7,5},{8,14},{9,15},{10,... | collective-permute-start | bytes 1179656 | tf_op jit(solution)/shard_map/ppermute | solution.py:51
  130.6 40.8 %collective-permute-start.5 = (bf16[256,1536]{1,0:T(8,128)(2,1)}, bf16[256,1536]{1,0:T(8,128)(2,1)}, u32[]{:S(2)}, u32[]{:S(2)}) collective-permute-start(bf16[256,1536]{1,0:T(8,128)(2,1)} %collective-permute-done), channel_id=1, source_target_pairs={{0,1},{1,0},{2,3},{3,2},{4,5},{5,4},{6,7},{7,6},{8,9},{9,8},{10,11... | collective-permute-start | bytes 2359304 | tf_op jit(solution)/shard_map/ppermute | solution.py:51
  133.7 53.4 %collective-permute-start.34 = (bf16[16,112,384]{2,1,0:T(8,128)(2,1)S(1)}, bf16[16,112,384]{2,1,0:T(8,128)(2,1)S(1)}, u32[]{:S(2)}, u32[]{:S(2)}) collective-permute-start(bf16[16,112,384]{2,1,0:T(8,128)(2,1)S(1)} %bitcast.361), channel_id=1, source_target_pairs={{0,8},{1,9},{2,10},{3,11},{4,12},{5,13},{6,14},{7,15},{8,0},{9,1},... | collective-permute-start | bytes 4128776 | tf_op jit(solution)/shard_map/ppermute | solution.py:51
  138.9 43.4 %collective-permute-start.9 = (bf16[128,1536]{1,0:T(8,128)(2,1)}, bf16[128,1536]{1,0:T(8,128)(2,1)S(1)}, u32[]{:S(2)}, u32[]{:S(2)}) collective-permute-start(bf16[128,1536]{1,0:T(8,128)(2,1)} %collective-permute-done.7), channel_id=1, source_target_pairs={{0,6},{1,7},{2,0},{3,1},{4,2},{5,3},{6,4},{7,5},{8,14},{9,15},{10,... | collective-permute-start | bytes 1179656 | tf_op jit(solution)/shard_map/ppermute | solution.py:51
  183.1 46.7 %collective-permute-start.10 = (bf16[256,1536]{1,0:T(8,128)(2,1)S(1)}, bf16[256,1536]{1,0:T(8,128)(2,1)S(1)}, u32[]{:S(2)}, u32[]{:S(2)}) collective-permute-start(bf16[256,1536]{1,0:T(8,128)(2,1)S(1)} %copy-done.26), channel_id=1, source_target_pairs={{0,2},{1,3},{2,4},{3,5},{4,6},{5,7},{6,0},{7,1},{8,10},{9,11},{10,... | collective-permute-start | bytes 2359304 | tf_op jit(solution)/shard_map/ppermute | solution.py:51
  183.6 44.2 %collective-permute-start.11 = (bf16[256,1536]{1,0:T(8,128)(2,1)S(1)}, bf16[256,1536]{1,0:T(8,128)(2,1)S(1)}, u32[]{:S(2)}, u32[]{:S(2)}) collective-permute-start(bf16[256,1536]{1,0:T(8,128)(2,1)S(1)} %copy-done.26), channel_id=1, source_target_pairs={{0,6},{1,7},{2,0},{3,1},{4,2},{5,3},{6,4},{7,5},{8,14},{9,15},{10,... | collective-permute-start | bytes 2359304 | tf_op jit(solution)/shard_map/ppermute | solution.py:51
  186.3 45.5 %collective-permute-start.12 = (bf16[256,1536]{1,0:T(8,128)(2,1)S(1)}, bf16[256,1536]{1,0:T(8,128)(2,1)S(1)}, u32[]{:S(2)}, u32[]{:S(2)}) collective-permute-start(bf16[256,1536]{1,0:T(8,128)(2,1)S(1)} %copy-done.26), channel_id=1, source_target_pairs={{0,1},{1,0},{2,3},{3,2},{4,5},{5,4},{6,7},{7,6},{8,9},{9,8},{10,11... | collective-permute-start | bytes 2359304 | tf_op jit(solution)/shard_map/ppermute | solution.py:51
  339.4 44.0 %collective-permute-start.40 = (bf16[2,256,768]{2,1,0:T(8,128)(2,1)}, bf16[2,256,768]{2,1,0:T(8,128)(2,1)}, u32[]{:S(2)}, u32[]{:S(2)}) collective-permute-start(bf16[2,256,768]{2,1,0:T(8,128)(2,1)} %get-tuple-element.90), channel_id=1, source_target_pairs={{0,6},{1,7},{2,0},{3,1},{4,2},{5,3},{6,4},{7,5},{8,14},{9,15},{10,... | collective-permute-start | bytes 2359304 | tf_op jit(solution)/shard_map/ppermute | solution.py:51
  340.9 44.2 %collective-permute-start.39 = (bf16[2,256,768]{2,1,0:T(8,128)(2,1)}, bf16[2,256,768]{2,1,0:T(8,128)(2,1)}, u32[]{:S(2)}, u32[]{:S(2)}) collective-permute-start(bf16[2,256,768]{2,1,0:T(8,128)(2,1)} %get-tuple-element.88), channel_id=1, source_target_pairs={{0,2},{1,3},{2,4},{3,5},{4,6},{5,7},{6,0},{7,1},{8,10},{9,11},{10,... | collective-permute-start | bytes 2359304 | tf_op jit(solution)/shard_map/ppermute | solution.py:51
  352.7 38.4 %collective-permute-start.41 = (bf16[2,256,768]{2,1,0:T(8,128)(2,1)}, bf16[2,256,768]{2,1,0:T(8,128)(2,1)}, u32[]{:S(2)}, u32[]{:S(2)}) collective-permute-start(bf16[2,256,768]{2,1,0:T(8,128)(2,1)} %get-tuple-element.89), channel_id=1, source_target_pairs={{0,4},{1,5},{2,6},{3,7},{4,0},{5,1},{6,2},{7,3},{8,12},{9,13},{10,... | collective-permute-start | bytes 2359304 | tf_op jit(solution)/shard_map/ppermute | solution.py:51
  364.1 120.5 %collective-permute-start.51 = (f32[1536,384]{1,0:T(8,128)}, f32[1536,384]{1,0:T(8,128)}, u32[]{:S(2)}, u32[]{:S(2)}) collective-permute-start(f32[1536,384]{1,0:T(8,128)} %bitcast.78), channel_id=1, source_target_pairs={{0,8},{1,9},{2,10},{3,11},{4,12},{5,13},{6,14},{7,15},{8,0},{9,1},... | collective-permute-start | bytes 7077896 | tf_op jit(solution)/shard_map/ppermute | solution.py:51
  376.5 30.2 %collective-permute-start.48 = (bf16[2,256,512]{2,1,0:T(8,128)(2,1)}, bf16[2,256,512]{2,1,0:T(8,128)(2,1)}, u32[]{:S(2)}, u32[]{:S(2)}) collective-permute-start(bf16[2,256,512]{2,1,0:T(8,128)(2,1)} %get-tuple-element.104), channel_id=1, source_target_pairs={{0,6},{1,7},{2,0},{3,1},{4,2},{5,3},{6,4},{7,5},{8,14},{9,15},{10,... | collective-permute-start | bytes 1572872 | tf_op jit(solution)/shard_map/ppermute | solution.py:51
  393.5 56.0 %collective-permute-start.42 = (bf16[4,256,768]{2,1,0:T(8,128)(2,1)}, bf16[4,256,768]{2,1,0:T(8,128)(2,1)}, u32[]{:S(2)}, u32[]{:S(2)}) collective-permute-start(bf16[4,256,768]{2,1,0:T(8,128)(2,1)} %pad_maximum_fusion.1), channel_id=1, source_target_pairs={{0,1},{1,0},{2,3},{3,2},{4,5},{5,4},{6,7},{7,6},{8,9},{9,8},{10,11... | collective-permute-start | bytes 4718600 | tf_op jit(solution)/shard_map/ppermute | solution.py:51
  409.8 34.9 %collective-permute-start.50 = (bf16[4,256,512]{2,1,0:T(8,128)(2,1)S(1)}, bf16[4,256,512]{2,1,0:T(8,128)(2,1)S(1)}, u32[]{:S(2)}, u32[]{:S(2)}) collective-permute-start(bf16[4,256,512]{2,1,0:T(8,128)(2,1)S(1)} %pad_maximum_fusion.2), channel_id=1, source_target_pairs={{0,1},{1,0},{2,3},{3,2},{4,5},{5,4},{6,7},{7,6},{8,9},{9,8},{10,11... | collective-permute-start | bytes 3145736 | tf_op jit(solution)/shard_map/ppermute | solution.py:51
  419.8 57.5 %collective-permute-start.62 = (f32[776,512]{1,0:T(8,128)}, f32[776,512]{1,0:T(8,128)}, u32[]{:S(2)}, u32[]{:S(2)}) collective-permute-start(f32[776,512]{1,0:T(8,128)} %maximum_maximum_fusion.1), channel_id=1, source_target_pairs={{0,8},{1,9},{2,10},{3,11},{4,12},{5,13},{6,14},{7,15},{8,0},{9,1},... | collective-permute-start | bytes 4767752 | tf_op jit(solution)/shard_map/ppermute | solution.py:51
  487.9 43.9 %collective-permute-start.52 = (f32[384,384]{1,0:T(8,128)}, f32[384,384]{1,0:T(8,128)}, u32[]{:S(2)}, u32[]{:S(2)}) collective-permute-start(f32[384,384]{1,0:T(8,128)} %bitcast.81), channel_id=1, source_target_pairs={{0,16},{1,17},{2,18},{3,19},{4,20},{5,21},{6,22},{7,23},{8,24},{9,... | collective-permute-start | bytes 1769480 | tf_op jit(solution)/shard_map/ppermute | solution.py:51
  488.9 48.8 %collective-permute-start.53 = (f32[384,384]{1,0:T(8,128)}, f32[384,384]{1,0:T(8,128)}, u32[]{:S(2)}, u32[]{:S(2)}) collective-permute-start(f32[384,384]{1,0:T(8,128)} %bitcast.83), channel_id=1, source_target_pairs={{0,48},{1,49},{2,50},{3,51},{4,52},{5,53},{6,54},{7,55},{8,56},{9,... | collective-permute-start | bytes 1769480 | tf_op jit(solution)/shard_map/ppermute | solution.py:51
  507.9 30.0 %collective-permute-start.54 = (f32[384,384]{1,0:T(8,128)S(1)}, f32[384,384]{1,0:T(8,128)}, u32[]{:S(2)}, u32[]{:S(2)}) collective-permute-start(f32[384,384]{1,0:T(8,128)S(1)} %bitcast.384), channel_id=1, source_target_pairs={{0,32},{1,33},{2,34},{3,35},{4,36},{5,37},{6,38},{7,39},{8,40},{9,... | collective-permute-start | bytes 1769480 | tf_op jit(solution)/shard_map/ppermute | solution.py:51
  571.3 32.9 %collective-permute-start.58 = (f32[2,192,384]{2,1,0:T(8,128)}, f32[2,192,384]{2,1,0:T(8,128)}, u32[]{:S(2)}, u32[]{:S(2)}) collective-permute-start(f32[2,192,384]{2,1,0:T(8,128)} %pad_maximum_fusion.6), channel_id=1, source_target_pairs={{0,6},{1,7},{2,0},{3,1},{4,2},{5,3},{6,4},{7,5},{8,14},{9,15},{10,... | collective-permute-start | bytes 1769480 | tf_op jit(solution)/shard_map/ppermute | solution.py:51
  (128 other events, 1244.1 us)
Sparse Core Ops, SparseCore 0:
  50.9 177.9 all-gather.2
  449.6 90.7 all-gather.4

commit v2 on v1

v2 whole, which is shorter than its diff:
```python
from functools import partial

import jax
import jax.numpy as jnp
from jax import lax
from jax.experimental import pallas as pl
from jax.experimental.pallas import tpu as pltpu
from jax.sharding import PartitionSpec as P

D = 1536
H = 48
P_SIZE = 64
N = 128
CONV = 4
STEP = 10
DI = 3072
CHANNELS = DI + 2 * N
SMALL = 21392
N_FSDP = 16
N_REP = 8
ROWS = 256
PACK = 2048
OWN = DI // N_REP
OWN_H = H // N_REP
OWN_BC = 2 * N // N_REP
SHARD_IN = D // N_FSDP
SHARD_OUT = DI // N_FSDP
SHARD_SMALL = SMALL // N_FSDP
TAIL = 512
WIDE = 384
CHUNK = 128
CHUNKS = PACK // CHUNK
HALF = CHUNKS // 2
VMEM_LIMIT = 40 * 1024 * 1024

NORM_EPS = 1e-05
BETA_ONE = 0.9
BETA_TWO = 0.999
ADAM_EPS = 1e-08
WEIGHT_DECAY = 0.1
RATE_MATRIX = 0.04
RATE_SMALL = 0.4
PRECISE = lax.Precision.HIGHEST
BF16 = jnp.bfloat16
F32 = jnp.float32


def move(value, target):
    pairs = []
    for f in range(N_FSDP):
        for r in range(N_REP):
            yh, z, c, x, yl = target(f // 8, (f // 2) % 4, f % 2, r // 2, r % 2)
            pairs.append((f * N_REP + r, ((yh % 2) * 8 + (z % 4) * 2 + c % 2) * N_REP + (x % 4) * 2 + yl % 2))
    return lax.ppermute(value, ("fsdp", "rep"), pairs)


def along_x(steps):
    return lambda yh, z, c, x, yl: (yh, z, c, x + steps, yl)


def along_z(steps):
    return lambda yh, z, c, x, yl: (yh, z + steps, c, x, yl)


def swap_y(yh, z, c, x, yl):
    return (yh, z, c, x, yl + 1)


def swap_y_hi(yh, z, c, x, yl):
    return (yh + 1, z, c, x, yl)


def swap_core(yh, z, c, x, yl):
    return (yh, z, c + 1, x, yl)


class Place:
    def __init__(self):
        f = lax.axis_index("fsdp")
        r = lax.axis_index("rep")
        self.f, self.r = f, r
        self.yh, self.z, self.c = f // 8, (f // 2) % 4, f % 2
        self.x, self.yl = r // 2, r % 2


def at(value, index, axis=0):
    return lax.dynamic_index_in_dim(value, index, axis, keepdims=False)


def tie(values, *others):
    return lax.optimization_barrier((values, others))[0]


def both(mine, other, second):
    first = jnp.where(second == 0, mine, other)
    last = jnp.where(second == 0, other, mine)
    return jnp.stack([first, last], 0)


def put(out, piece, axis, index):
    starts = [jnp.int32(0)] * out.ndim
    starts[axis] = jnp.int32(index)
    return lax.dynamic_update_slice(out, jnp.expand_dims(piece, axis), tuple(starts))


def in_ring_order(pieces, here, axis):
    first = pieces[0]
    out = jnp.zeros(first.shape[:axis] + (4,) + first.shape[axis:], first.dtype)
    for offset, piece in enumerate(pieces):
        out = put(out, piece, axis, (here + offset) % 4)
    return out


def exchange_rep(value):
    found = {(0, 0): value}
    for dx, dy in ((1, 0), (3, 0), (0, 1), (2, 0), (1, 1), (3, 1), (2, 1)):
        found[dx, dy] = move(value, lambda yh, z, c, x, yl: (yh, z, c, x - dx, yl + dy))
    return [found[k // 2, k % 2] for k in range(N_REP)]


def sum_rep(value):
    value = value + move(value, swap_y)
    value = value + move(value, lambda yh, z, c, x, yl: (yh, z, c, x ^ 1, yl))
    return value + move(value, lambda yh, z, c, x, yl: (yh, z, c, x ^ 2, yl))


def sum_all(value):
    value = sum_rep(value)
    value = value + move(value, swap_core)
    value = value + move(value, lambda yh, z, c, x, yl: (yh, z ^ 1, c, x, yl))
    value = value + move(value, lambda yh, z, c, x, yl: (yh, z ^ 2, c, x, yl))
    return value + move(value, swap_y_hi)


def with_rows(block, extra):
    width = block.shape[-1]
    flat = block.reshape(-1, width)
    return flat if extra is None else jnp.concatenate([flat, extra], 0)


def received(block, target, base, add_to):
    got = move(with_rows(block, base), target)
    rows = got.shape[0] - (0 if base is None else base.shape[0])
    return got[:rows].reshape(add_to.shape), got[rows:]


def scatter_ring(keep, got, extra, place):
    z_sum = at(keep, place.z, 1) + at(got, place.z, 1)
    found = []
    for step in (1, 3, 2):
        there = (place.z + step) % 4
        found.append(received(at(keep, there, 1) + at(got, there, 1), along_z(step), extra, z_sum))
    z_sum = z_sum + found[0][0] + found[1][0] + found[2][0]
    if extra is not None:
        extra = extra + found[0][1] + found[1][1] + found[2][1]
    mine = at(z_sum, place.yh)
    more, more_extra = received(at(z_sum, 1 - place.yh), swap_y_hi, extra, mine)
    return mine + more, (None if extra is None else extra + more_extra)


def adam_update(weight, gradient, moment_one, moment_two, learn_rate, decay_rate):
    moment_one = BETA_ONE * moment_one + (1.0 - BETA_ONE) * gradient
    moment_two = BETA_TWO * moment_two + (1.0 - BETA_TWO) * gradient * gradient
    scaled = (
        moment_one
        / (1.0 - BETA_ONE**STEP)
        / (jnp.sqrt(moment_two / (1.0 - BETA_TWO**STEP)) + ADAM_EPS)
    )
    return (weight - learn_rate * (scaled + decay_rate * weight), moment_one, moment_two)


def contract_rows(left_side, right_side):
    return lax.dot_general(
        left_side, right_side, (((0,), (0,)), ((), ())), preferred_element_type=F32
    )


def contract_cols(left_side, right_side):
    return lax.dot_general(
        left_side, right_side, (((1,), (1,)), ((), ())), preferred_element_type=F32
    )


def matmul(left_side, right_side):
    return jnp.dot(left_side, right_side, preferred_element_type=F32)


def segment_at(positions, seg_ends):
    counted = jnp.sum((positions[:, None] >= seg_ends[None, :]).astype(jnp.int32), axis=1)
    return jnp.where(positions < 0, jnp.int32(-1), counted)


def split_two(value):
    high = value.astype(BF16)
    return high, (value - high.astype(F32)).astype(BF16)


def split_three(value):
    high = value.astype(BF16)
    rest = value - high.astype(F32)
    middle = rest.astype(BF16)
    return high, middle, (rest - middle.astype(F32)).astype(BF16)


def product(left, right, left_dim, right_dim):
    return lax.dot_general(
        left, right, (((left_dim,), (right_dim,)), ((), ())), preferred_element_type=F32
    )


def joined_product(left_parts, right_parts, left_dim=1, right_dim=0):
    left_high, left_low = left_parts
    right_high, right_low = right_parts
    return product(
        jnp.concatenate([left_high, left_high, left_low], left_dim),
        jnp.concatenate([right_high, right_low, right_high], right_dim),
        left_dim,
        right_dim,
    )


def precise_product(left, right, left_dim=1, right_dim=0):
    return joined_product(split_two(left), split_two(right), left_dim, right_dim)


def ones_product(ones, value):
    return product(jnp.concatenate([ones] * 3, 1), jnp.concatenate(split_three(value), 0), 1, 0)


def spread(per_head, lane):
    return jnp.concatenate(
        [
            jnp.where(lane < P_SIZE, per_head[:, 2 * k : 2 * k + 1], per_head[:, 2 * k + 1 : 2 * k + 2])
            for k in range(OWN_H // 2)
        ],
        1,
    )


def head_sums(value):
    column = lax.broadcasted_iota(jnp.int32, (OWN, N), 0)
    head = lax.broadcasted_iota(jnp.int32, (OWN, N), 1)
    members = ((column >= head * P_SIZE) & (column < (head + 1) * P_SIZE)).astype(F32).astype(BF16)
    high, low = split_two(value)
    return product(jnp.concatenate([high, low], 1), jnp.concatenate([members, members], 0), 1, 0)


def two_heads(pair, lane):
    zero = jnp.zeros_like(pair)
    return jnp.concatenate([jnp.where(lane < P_SIZE, pair, zero), jnp.where(lane < P_SIZE, zero, pair)], 0)


def chunk_facts(ends, chunk, dt_pre, par):
    column = lax.broadcasted_iota(jnp.int32, (CHUNK, 1), 0) + chunk * CHUNK
    row = lax.broadcasted_iota(jnp.int32, (1, CHUNK), 1) + chunk * CHUNK

    def segment(position):
        counted = jnp.zeros_like(position)
        for k in range(3):
            counted = counted + (position >= ends[k]).astype(jnp.int32)
        return jnp.where(position < 0, -1, counted)

    def one_segment(position):
        counted = jnp.int32(0)
        for k in range(3):
            counted = counted + (position >= ends[k]).astype(jnp.int32)
        return jnp.where(position < 0, -1, counted)

    here_column, here_row = segment(column), segment(row)
    prior = one_segment(chunk * CHUNK - 1)
    last = one_segment(chunk * CHUNK + CHUNK - 1)
    lane = lax.broadcasted_iota(jnp.int32, (CHUNK, N), 1)
    shifted = dt_pre + par[6:7, :N]
    soft = jnp.maximum(shifted, 0.0) + jnp.log1p(jnp.exp(-jnp.abs(shifted)))
    step = jnp.where(lane < OWN_H, soft, 0.0)
    decay = step * par[7:8, :N]
    tri_row = lax.broadcasted_iota(jnp.int32, (CHUNK, CHUNK), 0)
    tri_column = lax.broadcasted_iota(jnp.int32, (CHUNK, CHUNK), 1)
    lower = (tri_row >= tri_column).astype(F32).astype(BF16)
    upper = (tri_row <= tri_column).astype(F32).astype(BF16)
    total = ones_product(lower, decay)
    entering = (here_column == prior).astype(F32) * jnp.exp(total)
    end = total[CHUNK - 1 : CHUNK]
    leaving = (here_column == last).astype(F32) * jnp.exp(jnp.minimum(end - total, 0.0))
    passing = jnp.where(last == prior, 1.0, 0.0) * jnp.exp(end)
    return dict(
        column=column,
        segment=segment,
        here_column=here_column,
        here_row=here_row,
        lane=lane,
        shifted=shifted,
        step=step,
        decay=decay,
        total=total,
        entering=entering,
        leaving=leaving,
        passing=passing,
        tri_row=tri_row,
        tri_column=tri_column,
        upper=upper,
    )


def forward_kernel(part, ends, proj, par, *refs):
    if part:
        carry_in, refs = refs[3], refs[4:]
    pre_out, mixed_out, state_out, carry_out, extended, state = refs
    chunk = pl.program_id(0) + part * HALF

    @pl.when(pl.program_id(0) == 0)
    def _():
        if part:
            state[...] = carry_in[:N, :OWN]
            extended[0:8, :] = carry_in[N:, :]
        else:
            state[...] = jnp.zeros_like(state)
            extended[0:8, :] = jnp.zeros((8, 640), F32)

    facts = chunk_facts(ends, chunk, proj[:, 1024:1152], par)
    lane = facts["lane"]
    conv = proj[:, OWN:1024].astype(BF16).astype(F32)
    extended[8 : 8 + CHUNK, :] = conv
    pre = par[4:5] + par[3:4] * conv
    for back in range(1, CONV):
        same = (facts["segment"](facts["column"] - back) == facts["here_column"]).astype(F32)
        pre = pre + par[3 - back : 4 - back] * (extended[8 - back : 8 - back + CHUNK, :] * same)
    extended[0:8, :] = extended[CHUNK : CHUNK + 8, :]
    pre_out[...] = pre
    act = pre * jax.nn.sigmoid(pre)
    own_x, state_b, state_c = act[:, :OWN], act[:, OWN : OWN + N], act[:, OWN + N :]
    stepped = own_x * spread(facts["step"], lane)
    b_parts, c_parts = split_two(state_b), split_two(state_c)
    inside = (facts["tri_row"] >= facts["tri_column"]) & (facts["here_column"] == facts["here_row"])
    scores = jnp.where(inside, joined_product(c_parts, b_parts, 1, 1), 0.0)
    total_rows = facts["total"].T
    state_in = state[...]
    state_out[...] = state_in
    outs = []
    for pair in range(OWN_H // 2):
        mixing = []
        for head in (2 * pair, 2 * pair + 1):
            span = facts["total"][:, head : head + 1] - total_rows[head : head + 1, :]
            mixing.append(jnp.exp(jnp.minimum(span, 0.0)) * scores)
        inner = two_heads(stepped[:, pair * N : pair * N + N], lane)
        outs.append(precise_product(jnp.concatenate(mixing, 1), inner))
    scanned = jnp.concatenate(outs, 1) + spread(facts["entering"], lane) * joined_product(
        c_parts, split_two(state_in)
    )
    state[...] = spread(facts["passing"], lane[:1]) * state_in + precise_product(
        state_b.T, stepped * spread(facts["leaving"], lane)
    )
    mixed_out[...] = scanned + par[5:6, :OWN] * own_x

    @pl.when(pl.program_id(0) == HALF - 1)
    def _():
        carry_out[:N, :OWN] = state[...]
        carry_out[:N, OWN:] = jnp.zeros((N, 640 - OWN), F32)
        carry_out[N:, :] = extended[0:8, :]


def run_forward(part, ends, proj, par, before=()):
    here = lambda i: (i + part * HALF, 0)
    chunked = lambda width: pl.BlockSpec((CHUNK, width), here)
    fixed = lambda shape: pl.BlockSpec(shape, lambda i: (0, 0))
    carry = fixed((N + 8, 640))
    return pl.pallas_call(
        partial(forward_kernel, part),
        grid=(HALF,),
        in_specs=[pl.BlockSpec(memory_space=pltpu.SMEM), chunked(1152), fixed((16, 640))]
        + ([pl.BlockSpec(memory_space=pl.ANY)] * 3 + [carry] if part else []),
        out_specs=[chunked(640), chunked(OWN), pl.BlockSpec((N, OWN), here), carry],
        out_shape=[
            jax.ShapeDtypeStruct((PACK, 640), F32),
            jax.ShapeDtypeStruct((PACK, OWN), F32),
            jax.ShapeDtypeStruct((CHUNKS * N, OWN), F32),
            jax.ShapeDtypeStruct((N + 8, 640), F32),
        ],
        input_output_aliases={3: 0, 4: 1, 5: 2} if part else {},
        scratch_shapes=[pltpu.VMEM((CHUNK + 8, 640), F32), pltpu.VMEM((N, OWN), F32)],
        compiler_params=pltpu.CompilerParams(
            dimension_semantics=("arbitrary",), vmem_limit_bytes=VMEM_LIMIT
        ),
        cost_estimate=pl.CostEstimate(flops=8_000_000_000, bytes_accessed=12_000_000, transcendentals=1_500_000),
        name="scan_forward",
    )(ends, proj, par, *before)


def backward_kernel(part, ends, conv_in, dt_in, pre_in, mixed_in, grad_mixed, state_all, par, *refs):
    if part:
        carry_in, sums_in, head_in, refs = refs[3], refs[4], refs[5], refs[6:]
    grad_x, grad_dt, grad_bc, sums, head_acc, carry_out, carried, extended, end_dot = refs
    step_index = pl.program_id(0)
    chunk = CHUNKS - 1 - part * HALF - step_index

    @pl.when(step_index == 0)
    def _():
        if part:
            carried[...] = carry_in[:N, :]
            extended[CHUNK : CHUNK + 8, :] = carry_in[N : N + 8, :]
            end_dot[...] = carry_in[N + 8 :, :N]
            sums[...] = sums_in[...]
            head_acc[...] = head_in[...]
        else:
            carried[...] = jnp.zeros_like(carried)
            extended[CHUNK : CHUNK + 8, :] = jnp.zeros((8, OWN), F32)
            end_dot[...] = jnp.zeros_like(end_dot)
            sums[...] = jnp.zeros_like(sums)
            head_acc[...] = jnp.zeros_like(head_acc)

    facts = chunk_facts(ends, chunk, dt_in[...], par)
    lane = facts["lane"]
    pre = pre_in[...]
    sig = jax.nn.sigmoid(pre)
    act = pre * sig
    own_x, state_b, state_c = act[:, :OWN], act[:, OWN : OWN + N], act[:, OWN + N :]
    step = facts["step"]
    step_wide = spread(step, lane)
    stepped = own_x * step_wide
    skip = par[5:6, :OWN]
    scanned = mixed_in[...] - skip * own_x
    grad_m = grad_mixed[...]
    sums[6:7] += jnp.sum(grad_m * own_x, 0, keepdims=True)

    b_parts, c_parts = split_two(state_b), split_two(state_c)
    inside = (facts["tri_row"] <= facts["tri_column"]) & (facts["here_column"] == facts["here_row"])
    scores = jnp.where(inside, joined_product(b_parts, c_parts, 1, 1), 0.0)
    total_rows = facts["total"].T
    grad_scores = jnp.zeros((CHUNK, CHUNK), F32)
    grad_stepped = []
    for pair in range(OWN_H // 2):
        columns = slice(pair * N, pair * N + N)
        grad_pair = grad_m[:, columns]
        high, low = split_two(grad_pair)
        stepped_parts = split_two(two_heads(stepped[:, columns], lane))
        grad_mixing = joined_product(stepped_parts, (high, low), 1, 1)
        mixing = []
        for k in range(2):
            head = 2 * pair + k
            span = total_rows[head : head + 1, :] - facts["total"][:, head : head + 1]
            decays = jnp.exp(jnp.minimum(span, 0.0))
            mixing.append(decays * scores)
            grad_scores = grad_scores + decays * grad_mixing[k * CHUNK : (k + 1) * CHUNK]
        grad_stepped.append(
            joined_product(
                split_two(jnp.concatenate(mixing, 1)), (two_heads(high, lane), two_heads(low, lane))
            )
        )
    grad_scores = jnp.where(inside, grad_scores, 0.0)
    carry = carried[...]
    carry_parts = split_two(carry)
    leaving = spread(facts["leaving"], lane)
    grad_stepped = jnp.concatenate(grad_stepped, 1) + leaving * joined_product(b_parts, carry_parts)
    state_in = state_all[...]
    entered = spread(facts["entering"], lane) * grad_m
    entered_parts = split_two(entered)
    grad_b = precise_product(grad_scores, state_c) + joined_product(
        split_two(leaving * stepped), carry_parts, 1, 1
    )
    grad_c = precise_product(grad_scores.T, state_b) + joined_product(
        entered_parts, split_two(state_in), 1, 1
    )
    grad_bc[0:N, :] = grad_b.T
    grad_bc[N:, :] = grad_c.T
    new_carry = spread(facts["passing"], lane[:1]) * carry + joined_product(
        split_two(state_c.T), entered_parts
    )
    carried[...] = new_carry

    grad_step = head_sums(own_x * grad_stepped)
    last_row = lax.broadcasted_iota(jnp.int32, (CHUNK, N), 0) == CHUNK - 1
    grad_total = head_sums(grad_m * scanned) - step * grad_step
    grad_total = grad_total + jnp.where(last_row, end_dot[0:1, :], 0.0)
    grad_decay = ones_product(facts["upper"], grad_total)
    end_dot[...] = head_sums(
        jnp.broadcast_to(jnp.sum(new_carry * state_in, 0, keepdims=True), (8, OWN))
    )
    grad_pre_dt = (grad_step + grad_decay * par[7:8, :N]) * jax.nn.sigmoid(facts["shifted"])
    grad_pre_dt = jnp.where(lane < OWN_H, grad_pre_dt, 0.0)
    grad_dt[...] = grad_pre_dt.astype(BF16)
    head_acc[0:1] += jnp.sum(grad_pre_dt, 0, keepdims=True)
    head_acc[1:2] += jnp.sum(grad_decay * facts["decay"], 0, keepdims=True)

    sig_x, pre_x = sig[:, :OWN], pre[:, :OWN]
    grad_pre = (step_wide * grad_stepped + skip * grad_m) * (sig_x * (1.0 + pre_x * (1.0 - sig_x)))
    extended[0:CHUNK, :] = grad_pre
    conv = conv_in[...].astype(BF16).astype(F32)
    sums[5:6] += jnp.sum(grad_pre, 0, keepdims=True)
    sums[4:5] += jnp.sum(conv * grad_pre, 0, keepdims=True)
    grad_conv = par[3:4, :OWN] * grad_pre
    for ahead in range(1, CONV):
        same = (facts["segment"](facts["column"] + ahead) == facts["here_column"]).astype(F32)
        later = extended[ahead : ahead + CHUNK, :] * same
        sums[4 - ahead : 5 - ahead] += jnp.sum(conv * later, 0, keepdims=True)
        grad_conv = grad_conv + par[3 - ahead : 4 - ahead, :OWN] * later
    extended[CHUNK : CHUNK + 8, :] = extended[0:8, :]
    grad_x[...] = grad_conv.astype(BF16)

    @pl.when(step_index == HALF - 1)
    def _():
        carry_out[:N, :] = carried[...]
        carry_out[N : N + 8, :] = extended[CHUNK : CHUNK + 8, :]
        carry_out[N + 8 :, :N] = end_dot[...]
        carry_out[N + 8 :, N:] = jnp.zeros((8, OWN - N), F32)


def run_backward(part, ends, proj, pre, mixed, grad_mixed, states, par, before=()):
    last = CHUNKS - 1 - part * HALF
    chunked = lambda width, column=0: pl.BlockSpec((CHUNK, width), lambda i: (last - i, column))
    fixed = lambda shape: pl.BlockSpec(shape, lambda i: (0, 0))
    carry = [fixed((N + 16, OWN)), fixed((8, OWN)), fixed((8, N))]
    return pl.pallas_call(
        partial(backward_kernel, part),
        grid=(HALF,),
        in_specs=[
            pl.BlockSpec(memory_space=pltpu.SMEM),
            chunked(OWN, 1),
            chunked(N, 8),
            chunked(640),
            chunked(OWN),
            chunked(OWN),
            pl.BlockSpec((N, OWN), lambda i: (last - i, 0)),
            fixed((16, 640)),
        ]
        + ([pl.BlockSpec(memory_space=pl.ANY)] * 3 + carry if part else []),
        out_specs=[
            chunked(OWN),
            chunked(N),
            pl.BlockSpec((2 * N, CHUNK), lambda i: (0, last - i)),
            carry[1],
            carry[2],
            carry[0],
        ],
        out_shape=[
            jax.ShapeDtypeStruct((PACK, OWN), BF16),
            jax.ShapeDtypeStruct((PACK, N), BF16),
            jax.ShapeDtypeStruct((2 * N, PACK), F32),
            jax.ShapeDtypeStruct((8, OWN), F32),
            jax.ShapeDtypeStruct((8, N), F32),
            jax.ShapeDtypeStruct((N + 16, OWN), F32),
        ],
        input_output_aliases={8: 0, 9: 1, 10: 2} if part else {},
        scratch_shapes=[
            pltpu.VMEM((N, OWN), F32),
            pltpu.VMEM((CHUNK + 8, OWN), F32),
            pltpu.VMEM((8, N), F32),
        ],
        compiler_params=pltpu.CompilerParams(
            dimension_semantics=("arbitrary",), vmem_limit_bytes=VMEM_LIMIT
        ),
        cost_estimate=pl.CostEstimate(flops=12_000_000_000, bytes_accessed=16_000_000, transcendentals=3_000_000),
        name="scan_backward",
    )(ends, proj, proj, pre, mixed, grad_mixed, states, par, *before)


PARTS = (1, 1, 1, 2, 2, 2, 1, 1)


def load_block(step, pieces, block):
    first = 0
    for slot, count in enumerate(PARTS):
        refs = pieces[first : first + count]
        first += count

        @pl.when(step == slot)
        def _(refs=refs):
            if len(refs) == 1:
                block[...] = refs[0][...]
            else:
                block[: ROWS // 2, :] = refs[0][...]
                block[ROWS // 2 :, :] = refs[1][...]


def piece_specs():
    return [
        pl.BlockSpec((ROWS // count, D), lambda i, table: (0, 0)) for count in PARTS for _ in range(count)
    ]


def project_kernel(table, *refs):
    pieces, (gain, weight, normed_out, proj, block) = refs[:11], refs[11:]
    load_block(pl.program_id(0), pieces, block)
    values = block[...].astype(F32)
    scale = lax.rsqrt(jnp.mean(values * values, axis=1, keepdims=True) + NORM_EPS)
    normed = (values * scale * gain[...]).astype(BF16)
    normed_out[...] = normed
    proj[...] = matmul(normed, weight[...])


def run_project(table, pieces, gain, weight):
    fixed = lambda shape: pl.BlockSpec(shape, lambda i, table: (0, 0))
    placed = lambda width: pl.BlockSpec((ROWS, width), lambda i, table: (table[i], 0))
    return pl.pallas_call(
        project_kernel,
        grid_spec=pltpu.PrefetchScalarGridSpec(
            num_scalar_prefetch=1,
            grid=(N_REP,),
            in_specs=piece_specs() + [fixed((1, D)), fixed((D, 3 * WIDE))],
            out_specs=[placed(D), placed(3 * WIDE)],
            scratch_shapes=[pltpu.VMEM((ROWS, D), BF16)],
        ),
        out_shape=[jax.ShapeDtypeStruct((PACK, D), BF16), jax.ShapeDtypeStruct((PACK, 3 * WIDE), F32)],
        compiler_params=pltpu.CompilerParams(
            dimension_semantics=("arbitrary",), vmem_limit_bytes=VMEM_LIMIT
        ),
        cost_estimate=pl.CostEstimate(flops=7_250_000_000, bytes_accessed=26_000_000, transcendentals=0),
        name="project",
    )(table, *pieces, gain, weight)


def row_sums(value):
    folded = value[:, :N] + value[:, N : 2 * N] + value[:, 2 * N :]
    return jnp.sum(folded.T, 0, keepdims=True)


def out_grad_kernel(table, *refs):
    pieces = refs[:11]
    w_out, mixed, gate_in, gain, branch_out, grad_out, sums, block, turned = refs[11:]

    @pl.when(pl.program_id(0) == 0)
    def _():
        for k in range(4):
            turned[k * WIDE : (k + 1) * WIDE, :] = w_out[k * WIDE : (k + 1) * WIDE, :].T

    load_block(pl.program_id(0), pieces, block)
    branch = block[...]
    branch_out[...] = branch
    total = matmul(branch, turned[...])
    grad_out[...] = total
    gate = gate_in[...]
    gated = mixed[...] * (gate * jax.nn.sigmoid(gate))
    row = lax.broadcasted_iota(jnp.int32, (8, ROWS), 0)
    sums[...] = jnp.where(
        row == 0, row_sums(gated * gated), jnp.where(row == 1, row_sums(total * gain[...] * gated), 0.0)
    )


def run_out_grad(table, pieces, w_out, mixed, proj, gain):
    fixed = lambda shape: pl.BlockSpec(shape, lambda i, table: (0, 0))
    placed = lambda width: pl.BlockSpec((ROWS, width), lambda i, table: (table[i], 0))
    return pl.pallas_call(
        out_grad_kernel,
        grid_spec=pltpu.PrefetchScalarGridSpec(
            num_scalar_prefetch=1,
            grid=(N_REP,),
            in_specs=piece_specs() + [fixed((D, WIDE)), placed(OWN), placed(OWN), fixed((1, OWN))],
            out_specs=[placed(D), placed(OWN), pl.BlockSpec((8, ROWS), lambda i, table: (0, table[i]))],
            scratch_shapes=[pltpu.VMEM((ROWS, D), BF16), pltpu.VMEM((D, WIDE), BF16)],
        ),
        out_shape=[
            jax.ShapeDtypeStruct((PACK, D), BF16),
            jax.ShapeDtypeStruct((PACK, OWN), F32),
            jax.ShapeDtypeStruct((8, PACK), F32),
        ],
        compiler_params=pltpu.CompilerParams(
            dimension_semantics=("arbitrary",), vmem_limit_bytes=VMEM_LIMIT
        ),
        cost_estimate=pl.CostEstimate(flops=2_420_000_000, bytes_accessed=23_000_000, transcendentals=800_000),
        name="out_grad",
    )(table, *pieces, w_out, mixed, proj, gain)


def gate_kernel(
    where, grad_out, mixed_in, gate_in, sums, gain, grad_branch, normed,
    row_zero, row_one, row_two, row_three, grad_mixed, keep, give, grad_gain, total,
):
    step = pl.program_id(0)
    rows = grad_out.shape[0]
    mixed, gate, grad_o = mixed_in[...], gate_in[...], grad_out[...]
    stats = jnp.concatenate([sums[...], jnp.zeros((N - 8, rows), F32)], 0).T
    out_scale = lax.rsqrt(stats[:, 0:1] * (1.0 / DI) + NORM_EPS)
    pull = out_scale * out_scale * out_scale * (stats[:, 1:2] * (1.0 / DI))
    gate_sig = jax.nn.sigmoid(gate)
    silu = gate * gate_sig
    gated = mixed * silu
    unit = gated * out_scale
    low = (unit * gain[...]).astype(BF16)
    grad_gated = out_scale * (grad_o * gain[...]) - gated * pull
    grad_mixed[...] = grad_gated * silu
    grad_z = (grad_gated * mixed * (gate_sig * (1.0 + gate * (1.0 - gate_sig)))).astype(BF16)
    ahead = (step - where[1] + 4) % 4
    for slot, ref in enumerate((row_zero, row_one, row_two, row_three)):

        @pl.when(ahead == slot)
        def _(ref=ref):
            ref[:, :OWN] = low
            ref[:, OWN:] = grad_z

    @pl.when(step == 0)
    def _():
        grad_gain[...] = jnp.zeros_like(grad_gain)
        total[...] = jnp.zeros_like(total)

    grad_gain[0:1] += jnp.sum(grad_o * unit, 0, keepdims=True)
    for k in range(4):
        part = product(low, grad_branch[:, k * WIDE : (k + 1) * WIDE], 0, 0)
        for m in range(4):
            total[4 * k + m, :SHARD_IN] += part[m * SHARD_IN : (m + 1) * SHARD_IN]
    part = product(normed[...], grad_z, 0, 0)
    for f in range(N_FSDP):
        total[f, SHARD_IN:] += part[f * SHARD_IN : (f + 1) * SHARD_IN]

    @pl.when(step == pl.num_programs(0) - 1)
    def _():
        for k in range(N_FSDP // 2):
            keep[k] = total[2 * k + where[0]]
            give[k] = total[2 * k + 1 - where[0]]


def run_gate(where, grad_out, mixed, proj, sums, gain, grad_branch, normed):
    count = 2 * ROWS
    rows = lambda width: pl.BlockSpec((count, width), lambda i: (i, 0))
    fixed = lambda shape: pl.BlockSpec(shape, lambda i: (0,) * len(shape))
    half = (N_FSDP // 2, 2 * SHARD_IN, WIDE)
    return pl.pallas_call(
        gate_kernel,
        grid=(PACK // count,),
        in_specs=[
            pl.BlockSpec(memory_space=pltpu.SMEM),
            rows(OWN),
            rows(OWN),
            rows(OWN),
            pl.BlockSpec((8, count), lambda i: (0, i)),
            fixed((1, OWN)),
            rows(D),
            rows(D),
        ],
        out_specs=[fixed((count, 2 * OWN))] * 4 + [rows(OWN), fixed(half), fixed(half), fixed((8, OWN))],
        out_shape=[jax.ShapeDtypeStruct((count, 2 * OWN), BF16)] * 4
        + [
            jax.ShapeDtypeStruct((PACK, OWN), F32),
            jax.ShapeDtypeStruct(half, F32),
            jax.ShapeDtypeStruct(half, F32),
            jax.ShapeDtypeStruct((8, OWN), F32),
        ],
        scratch_shapes=[pltpu.VMEM((N_FSDP, 2 * SHARD_IN, WIDE), F32)],
        compiler_params=pltpu.CompilerParams(
            dimension_semantics=("arbitrary",), vmem_limit_bytes=VMEM_LIMIT
        ),
        cost_estimate=pl.CostEstimate(flops=4_840_000_000, bytes_accessed=34_000_000, transcendentals=800_000),
        name="gate_backward",
    )(where, grad_out, mixed, proj, sums, gain, grad_branch, normed)


def own_rows(step, table, mine, other, block, columns):
    for k in range(4):

        @pl.when(step == 2 * k)
        def _(k=k):
            block[...] = mine[k][pl.ds(pl.multiple_of(table[8] * ROWS, ROWS), ROWS), columns]

        @pl.when(step == 2 * k + 1)
        def _(k=k):
            block[...] = other[k * ROWS : (k + 1) * ROWS, columns]


def block_out_kernel(table, *refs):
    mine, (other, weight, tokens, live, out, block) = refs[:4], refs[4:]
    step = pl.program_id(0)
    own_rows(step, table, mine, other, block, slice(0, OWN))
    part = matmul(block[...], weight[...])

    @pl.when(step == 0)
    def _():
        out[...] = part

    @pl.when(step > 0)
    def _():
        out[...] += part

    @pl.when(step == N_REP - 1)
    def _():
        out[...] = tokens[...].astype(F32) + live[...] * out[...]


def run_block_out(table, mine, other, weight, tokens, live):
    fixed = lambda shape: pl.BlockSpec(shape, lambda i, table: (0, 0))
    return pl.pallas_call(
        block_out_kernel,
        grid_spec=pltpu.PrefetchScalarGridSpec(
            num_scalar_prefetch=1,
            grid=(N_REP,),
            in_specs=[fixed((2 * ROWS, 2 * OWN))] * 4
            + [
                fixed((4 * ROWS, 2 * OWN)),
                pl.BlockSpec((OWN, D), lambda i, table: (table[i], 0)),
                fixed((ROWS, D)),
                fixed((ROWS, 1)),
            ],
            out_specs=fixed((ROWS, D)),
            scratch_shapes=[pltpu.VMEM((ROWS, OWN), BF16)],
        ),
        out_shape=jax.ShapeDtypeStruct((ROWS, D), F32),
        compiler_params=pltpu.CompilerParams(
            dimension_semantics=("arbitrary",), vmem_limit_bytes=VMEM_LIMIT
        ),
        cost_estimate=pl.CostEstimate(flops=2_420_000_000, bytes_accessed=14_000_000, transcendentals=0),
        name="block_out",
    )(table, *mine, other, weight, tokens, live)


def input_grad_kernel(table, *refs):
    mine, refs = refs[:4], refs[4:]
    other, tail, rest, w_z, w_x, w_bc, w_dt, tokens, cotangent, gain, out, gain_out, block = refs
    step = pl.program_id(0)
    own_rows(step, table, mine, other, block, slice(OWN, 2 * OWN))
    part = contract_cols(block[...], w_z[...]) + contract_cols(tail[0, :, :OWN], w_x[...])

    @pl.when(step == 0)
    def _():
        out[...] = part

    @pl.when(step > 0)
    def _():
        out[...] += part

    @pl.when(step == N_REP - 1)
    def _():
        grad_h = out[...] + contract_cols(rest[:, : 2 * N], w_bc[...]) + contract_cols(rest[:, 2 * N :], w_dt[...])
        values = tokens[...].astype(F32)
        scale = lax.rsqrt(jnp.mean(values * values, axis=1, keepdims=True) + NORM_EPS)
        unit = values * scale
        gain_out[...] = jnp.broadcast_to(jnp.sum(grad_h * unit, 0, keepdims=True), gain_out.shape)
        grad_unit = grad_h * gain[...]
        inner = jnp.mean(grad_unit * unit, axis=1, keepdims=True)
        out[...] = cotangent[...].astype(F32) + scale * (grad_unit - unit * inner)


def run_input_grad(table, mine, other, tail, rest, full_in, low_dt, tokens, cotangent, gain):
    fixed = lambda shape: pl.BlockSpec(shape, lambda i, table: (0, 0))
    return pl.pallas_call(
        input_grad_kernel,
        grid_spec=pltpu.PrefetchScalarGridSpec(
            num_scalar_prefetch=1,
            grid=(N_REP,),
            in_specs=[fixed((2 * ROWS, 2 * OWN))] * 4
            + [
                fixed((4 * ROWS, 2 * OWN)),
                pl.BlockSpec((1, ROWS, TAIL), lambda i, table: (table[i], 0, 0)),
                fixed((ROWS, 3 * N)),
                pl.BlockSpec((D, OWN), lambda i, table: (0, table[i])),
                pl.BlockSpec((D, OWN), lambda i, table: (0, N_REP + table[i])),
                pl.BlockSpec((D, 2 * N), lambda i, table: (0, DI // N)),
                fixed((D, N)),
                fixed((ROWS, D)),
                fixed((ROWS, D)),
                fixed((1, D)),
            ],
            out_specs=[fixed((ROWS, D)), fixed((8, D))],
            scratch_shapes=[pltpu.VMEM((ROWS, OWN), BF16)],
        ),
        out_shape=[jax.ShapeDtypeStruct((ROWS, D), F32), jax.ShapeDtypeStruct((8, D), F32)],
        compiler_params=pltpu.CompilerParams(
            dimension_semantics=("arbitrary",), vmem_limit_bytes=VMEM_LIMIT
        ),
        cost_estimate=pl.CostEstimate(flops=5_100_000_000, bytes_accessed=30_000_000, transcendentals=0),
        name="input_grad",
    )(table, *mine, other, tail, rest, full_in, full_in, full_in, low_dt, tokens, cotangent, gain)


def adam_in_kernel(table, *refs):
    early, (tail, rest, weight, first, second) = refs[:N_REP], refs[N_REP : N_REP + 5]
    grad_out, first_out, second_out, weight_out, grad = refs[N_REP + 5 :]
    step = pl.program_id(0)
    for slot in range(N_REP):

        @pl.when(step == slot)
        def _(slot=slot):
            grad[...] = early[slot][SHARD_IN:, :]

    @pl.when((step >= N_REP) & (step < 2 * N_REP))
    def _():
        grad[...] = tail[jnp.clip(step - N_REP, 0, N_REP - 1), :SHARD_IN, :OWN]

    @pl.when(step == 2 * N_REP)
    def _():
        grad[...] = rest[...]

    new_weight, new_first, new_second = adam_update(
        weight[...], grad[...], first[...], second[...], RATE_MATRIX, WEIGHT_DECAY
    )
    grad_out[...] = grad[...]
    first_out[...] = new_first
    second_out[...] = new_second
    weight_out[...] = new_weight


def run_adam_in(table, early, tail, rest, weight, first, second):
    fixed = lambda shape: pl.BlockSpec(shape, lambda i, table: (0,) * len(shape))
    column = pl.BlockSpec((SHARD_IN, WIDE), lambda i, table: (0, table[i]))
    shape = jax.ShapeDtypeStruct(weight.shape, F32)
    return pl.pallas_call(
        adam_in_kernel,
        grid_spec=pltpu.PrefetchScalarGridSpec(
            num_scalar_prefetch=1,
            grid=(2 * N_REP + 1,),
            in_specs=[fixed((2 * SHARD_IN, WIDE))] * N_REP
            + [fixed(tail.shape), fixed((SHARD_IN, WIDE)), column, column, column],
            out_specs=[column] * 4,
            scratch_shapes=[pltpu.VMEM((SHARD_IN, WIDE), F32)],
        ),
        out_shape=[shape] * 4,
        compiler_params=pltpu.CompilerParams(
            dimension_semantics=("arbitrary",), vmem_limit_bytes=VMEM_LIMIT
        ),
        cost_estimate=pl.CostEstimate(flops=10_000_000, bytes_accessed=22_000_000, transcendentals=1_200_000),
        name="adam_in",
    )(table, *early, tail, rest, weight, first, second)


def adam_out_kernel(table, *refs):
    early, (weight, first, second) = refs[:N_REP], refs[N_REP : N_REP + 3]
    grad_out, first_out, second_out, weight_out, grad = refs[N_REP + 3 :]
    for slot in range(N_REP):

        @pl.when(pl.program_id(0) == slot)
        def _(slot=slot):
            grad[...] = early[slot][:SHARD_IN, :]

    new_weight, new_first, new_second = adam_update(
        weight[...], grad[...], first[...], second[...], RATE_MATRIX, WEIGHT_DECAY
    )
    grad_out[...] = grad[...]
    first_out[...] = new_first
    second_out[...] = new_second
    weight_out[...] = new_weight


def run_adam_out(table, early, weight, first, second):
    fixed = lambda shape: pl.BlockSpec(shape, lambda i, table: (0,) * len(shape))
    part = pl.BlockSpec((SHARD_IN, WIDE), lambda i, table: (table[i] // 4, table[i] % 4))
    shape = jax.ShapeDtypeStruct(weight.shape, F32)
    return pl.pallas_call(
        adam_out_kernel,
        grid_spec=pltpu.PrefetchScalarGridSpec(
            num_scalar_prefetch=1,
            grid=(N_REP,),
            in_specs=[fixed((2 * SHARD_IN, WIDE))] * N_REP + [part] * 3,
            out_specs=[part] * 4,
            scratch_shapes=[pltpu.VMEM((SHARD_IN, WIDE), F32)],
        ),
        out_shape=[shape] * 4,
        compiler_params=pltpu.CompilerParams(
            dimension_semantics=("arbitrary",), vmem_limit_bytes=VMEM_LIMIT
        ),
        cost_estimate=pl.CostEstimate(flops=5_000_000, bytes_accessed=12_000_000, transcendentals=600_000),
        name="adam_out",
    )(table, *early, weight, first, second)


def body(
    tokens,
    cotangent,
    lengths,
    w_in,
    w_dt,
    w_out,
    small,
    first_in,
    first_dt,
    first_out,
    first_small,
    second_in,
    second_dt,
    second_out,
    second_small,
):
    place = Place()
    r = place.r
    zero = jnp.int32(0)
    pack_lengths = lax.dynamic_slice_in_dim(lengths, place.f, 1, 0)[0]
    seg_ends = jnp.cumsum(pack_lengths)
    own_positions = r * ROWS + jnp.arange(ROWS, dtype=jnp.int32)
    own_live = (segment_at(own_positions, seg_ends) < 3).astype(F32)[:, None]
    slots = jnp.arange(N_REP, dtype=jnp.int32)
    ahead = ((place.x + slots // 2) % 4) * 2 + (place.yl + slots) % 2
    behind = ((place.x - slots // 2) % 4) * 2 + (place.yl + slots) % 2
    half = ROWS // 2

    in_low = w_in.astype(BF16)
    dt_low = w_dt.astype(BF16)
    small_rows = jnp.pad(small.astype(BF16), (0, 16 * 1152 - SHARD_SMALL)).reshape(16, 1152)
    weight_block = jnp.concatenate(
        [
            jnp.concatenate(
                [
                    lax.dynamic_slice_in_dim(in_low, r * OWN, OWN, 1),
                    lax.dynamic_slice_in_dim(in_low, DI + r * OWN, OWN, 1),
                    in_low[:, 2 * DI :],
                    lax.dynamic_slice_in_dim(dt_low, r * OWN_H, OWN_H, 1),
                    jnp.zeros((SHARD_IN, 2), BF16),
                    dt_low,
                    jnp.zeros((SHARD_IN, N - 8 - H), BF16),
                ],
                1,
            ),
            small_rows,
        ],
        0,
    )
    out_low_shard = w_out.astype(BF16)
    out_piece = lax.dynamic_slice(
        out_low_shard, (SHARD_IN * (place.x // 2), WIDE * ((place.x % 2) * 2 + place.yl)), (SHARD_IN, WIDE)
    )

    from_left = move(tokens, along_x(1))
    from_right = move(tokens, along_x(-1))
    partner = move(tokens, swap_y)
    weight_pair = both(weight_block, move(weight_block, swap_y_hi), place.yh)
    out_piece = move(
        out_piece, lambda yh, z, c, x, yl: (x % 2, yl * 2 + c, x // 2, yh * 2 + z // 2, z % 2)
    )
    slice_out = lax.all_gather(out_piece, "fsdp", axis=0, tiled=True)

    from_left, from_right, partner, weight_pair = lax.optimization_barrier(
        (from_left, from_right, partner, weight_pair)
    )
    far_top = move(from_left[:half], along_x(1))
    far_low = move(from_right[half:], along_x(-1))
    partner_left = move(from_left, swap_y)
    weight_left = move(weight_pair, along_z(1))
    weight_right = move(weight_pair, along_z(-1))

    far_top, far_low, partner_left, weight_left, weight_right = lax.optimization_barrier(
        (far_top, far_low, partner_left, weight_left, weight_right)
    )
    right_top = move(partner[:half], along_x(-1))
    right_low = move(from_right[half:], swap_y)
    weight_far = jnp.concatenate(
        [move(weight_left[:1], along_z(1)), move(weight_right[1:], along_z(-1))], 0
    )

    right_top, right_low, weight_far, partner_left = lax.optimization_barrier(
        (right_top, right_low, weight_far, partner_left)
    )
    partner_far_top = move(partner_left[:half], along_x(1))
    partner_far_low = move(right_low, along_x(-1))
    weight_ring = in_ring_order([weight_pair, weight_right, weight_far, weight_left], place.z, 1)
    weight_other = move(weight_ring, swap_core)
    cores = [jnp.where(place.c == 0, weight_ring, weight_other), jnp.where(place.c == 0, weight_other, weight_ring)]
    slice_in = jnp.stack([core[:, :, :SHARD_IN] for core in cores], 2).reshape(D, 1152)
    vector = jnp.stack([core[:, :, SHARD_IN : SHARD_IN + 2] for core in cores], 2)
    vector = vector.reshape(N_FSDP, 2 * 1152)[:, :SHARD_SMALL].reshape(-1).astype(F32)
    token_pieces = [
        tokens, partner, from_right, right_top, right_low, far_top, far_low,
        partner_far_top, partner_far_low, from_left, partner_left,
    ]

    full_in = lax.all_gather(tie(in_low, slice_out), "fsdp", axis=0, tiled=True)
    full_out = lax.all_gather(tie(out_low_shard, full_in), "fsdp", axis=0, tiled=True)

    offset = 0
    gain_in = vector[None, :D]
    offset = D
    gain_row = lax.dynamic_slice_in_dim(vector, offset + r * OWN, OWN, 0)[None, :]
    offset += DI
    taps = vector[offset : offset + (CONV + 1) * CHANNELS].reshape(CONV + 1, CHANNELS)
    offset += (CONV + 1) * CHANNELS
    per_head = vector[offset:].reshape(3, H)
    dt_bias, a_log, d_skip = lax.dynamic_slice_in_dim(per_head, r * OWN_H, OWN_H, 1)
    taps_bc = taps[:, DI:]
    conv_par = jnp.concatenate([lax.dynamic_slice_in_dim(taps, r * OWN, OWN, 1), taps_bc], 1)
    head_par = jnp.stack(
        [
            jnp.pad(jnp.broadcast_to(d_skip[:, None], (OWN_H, P_SIZE)).reshape(-1), (0, 2 * N)),
            jnp.pad(dt_bias, (0, 640 - OWN_H)),
            jnp.pad(-jnp.exp(a_log), (0, 640 - OWN_H)),
        ],
        0,
    )
    par = jnp.concatenate([conv_par, head_par, jnp.zeros((8, 640), F32)], 0)

    branch = (cotangent.astype(F32) * own_live).astype(BF16)
    branch = tie(branch, partner_far_top, partner_far_low)
    b_left = move(branch, along_x(1))
    b_right = move(branch, along_x(-1))
    b_partner = move(branch, swap_y)
    normed, proj = run_project(ahead, token_pieces, gain_in, slice_in)
    b_left, b_right, b_partner, proj = lax.optimization_barrier((b_left, b_right, b_partner, proj))
    b_far_top = move(b_left[:half], along_x(1))
    b_far_low = move(b_right[half:], along_x(-1))
    b_partner_left = move(b_left, swap_y)
    b_right_top = move(b_partner[:half], along_x(-1))
    b_right_low = move(b_right[half:], swap_y)
    before = run_forward(0, seg_ends, proj, par)
    b_far_top, b_far_low, b_partner_left, b_right_top, b_right_low, before = lax.optimization_barrier(
        (b_far_top, b_far_low, b_partner_left, b_right_top, b_right_low, before)
    )
    b_partner_far_top = move(b_partner_left[:half], along_x(1))
    b_partner_far_low = move(b_right_low, along_x(-1))
    pre, mixed, states, _ = run_forward(1, seg_ends, proj, par, before)
    branch_pieces = [
        branch, b_partner, b_right, b_right_top, b_right_low, b_far_top, b_far_low,
        b_partner_far_top, b_partner_far_low, b_left, b_partner_left,
    ]
    grad_branch, grad_normed_out, sums = run_out_grad(ahead, branch_pieces, slice_out, mixed, proj, gain_row)
    sums = sum_rep(sums[:2].reshape(32, 128)).reshape(2, PACK)
    sums = jnp.concatenate([sums, jnp.zeros((6, PACK), F32)], 0)

    where = jnp.stack([place.c, place.x, place.yl])
    row_zero, row_one, row_two, row_three, grad_mixed, keep, give, grad_gain = run_gate(
        where, grad_normed_out, mixed, proj, sums, gain_row, grad_branch, normed
    )

    row_one = move(row_one, along_x(1))
    row_three = move(row_three, along_x(3))
    row_two = move(row_two, along_x(2))
    got = move(give, swap_core)
    before = run_backward(0, seg_ends, proj, pre, mixed, grad_mixed, states, par)
    row_one, row_two, row_three, got, before = lax.optimization_barrier(
        (row_one, row_two, row_three, got, before)
    )
    mine_rows = [row_zero, row_one, row_two, row_three]
    far_rows = jnp.concatenate(
        [lax.dynamic_slice_in_dim(rows, (1 - place.yl) * ROWS, ROWS, 0) for rows in mine_rows], 0
    )
    other_rows = move(far_rows, swap_y)
    split = (2, 4, 2 * SHARD_IN, WIDE)
    early_part, _ = scatter_ring(keep.reshape(split), got.reshape(split), None, place)
    grad_x, grad_dtraw, grad_bc, grad_sums, grad_heads, _ = run_backward(
        1, seg_ends, proj, pre, mixed, grad_mixed, states, par, (before[0], before[1], before[2], before[5], before[3], before[4])
    )
    out_part = move(
        early_part[:SHARD_IN],
        lambda yh, z, c, x, yl: (x // 2, (x % 2) * 2 + yl, z % 2, 2 * c + yh, z // 2),
    )
    early_parts = exchange_rep(jnp.concatenate([out_part, early_part[SHARD_IN:]], 0))

    grad_bc = lax.all_to_all(grad_bc, "rep", 0, 0, tiled=True).reshape(N_REP, OWN_BC, PACK).sum(0)
    own_taps = lax.dynamic_slice_in_dim(taps_bc, r * OWN_BC, OWN_BC, 1)
    own_pre = lax.dynamic_slice_in_dim(pre, OWN + r * OWN_BC, OWN_BC, 1).T
    own_conv = lax.dynamic_slice_in_dim(proj, 2 * OWN + r * OWN_BC, OWN_BC, 1).T
    own_conv = own_conv.astype(BF16).astype(F32)
    sig = jax.nn.sigmoid(own_pre)
    grad_pre = grad_bc * (sig * (1.0 + own_pre * (1.0 - sig)))
    positions = jnp.arange(PACK, dtype=jnp.int32)
    segments = segment_at(positions, seg_ends)
    grad_conv_bc = own_taps[CONV - 1][:, None] * grad_pre
    grad_taps_bc = [jnp.sum(own_conv * grad_pre, 1)]
    for later_by in range(1, CONV):
        same = (segment_at(positions + later_by, seg_ends) == segments) & (positions + later_by < PACK)
        later = jnp.concatenate([grad_pre[:, later_by:], jnp.zeros((OWN_BC, later_by), F32)], 1)
        later = later * same.astype(F32)[None, :]
        grad_taps_bc.insert(0, jnp.sum(own_conv * later, 1))
        grad_conv_bc = grad_conv_bc + own_taps[CONV - 1 - later_by][:, None] * later
    grad_bias_bc = jnp.sum(grad_pre, 1)
    grad_tail = jnp.concatenate(
        [
            grad_x,
            grad_conv_bc.T.astype(BF16),
            grad_dtraw[:, :OWN_H],
            jnp.zeros((PACK, TAIL - OWN - OWN_BC - OWN_H), BF16),
        ],
        1,
    )

    grad_tail_own = contract_rows(normed, grad_tail).reshape(2, 4, 2, SHARD_IN, TAIL)
    row = lambda value: jnp.pad(value, (0, OWN - value.shape[0]))[None, :]
    head_columns = jnp.concatenate(
        [grad_gain[0:1]]
        + [grad_sums[1:6]]
        + [row(grad_heads[1, :OWN_H]), row(grad_sums[6].reshape(OWN_H, P_SIZE).sum(1))],
        0,
    )
    bc_columns = jnp.stack(
        [jnp.pad(grad_heads[0, :OWN_H], (0, OWN_BC - OWN_H))]
        + grad_taps_bc
        + [grad_bias_bc, jnp.zeros_like(grad_bias_bc), jnp.zeros_like(grad_bias_bc)],
        0,
    )
    small_own = jnp.concatenate(
        [head_columns, bc_columns, jnp.zeros((8, TAIL - OWN - OWN_BC), F32)], 1
    )
    tail_keep = at(grad_tail_own, place.c, 2)
    tail_got, small_got = received(at(grad_tail_own, 1 - place.c, 2), swap_core, small_own, tail_keep)
    tail_part, small_sum = scatter_ring(tail_keep, tail_got, small_own + small_got, place)

    tail_rows = lax.all_to_all(grad_tail, "rep", 0, 0, tiled=True).reshape(N_REP, ROWS, TAIL)

    def columns(parts):
        return parts.transpose(1, 0, 2).reshape(parts.shape[1], -1)

    rest_rows = jnp.concatenate(
        [
            columns(tail_rows[:, :, OWN : OWN + OWN_BC]),
            jnp.zeros((ROWS, 8), BF16),
            columns(tail_rows[:, :, OWN + OWN_BC : OWN + OWN_BC + OWN_H]),
            jnp.zeros((ROWS, N - 8 - H), BF16),
        ],
        1,
    )
    behind_table = jnp.concatenate([behind, place.yl[None]])
    input_grad, grad_gain_in = run_input_grad(
        behind_table, mine_rows, other_rows, tail_rows, rest_rows, full_in, slice_in[:, 1024:1152],
        tokens, cotangent, gain_in,
    )
    grad_gain_in = sum_all(grad_gain_in[0].reshape(12, 128)).reshape(-1)

    block_out = run_block_out(behind_table, mine_rows, other_rows, full_out, tokens, own_live)

    tail_block = jnp.concatenate([tail_part, small_sum], 0)
    tail_parts = lax.all_to_all(
        jnp.broadcast_to(tail_block[None], (N_REP,) + tail_block.shape), "rep", 0, 0, tiled=True
    )
    small_parts = tail_parts[:, SHARD_IN:]

    def channels(row):
        return jnp.concatenate(
            [small_parts[:, row, :OWN].reshape(-1), small_parts[:, row, OWN : OWN + OWN_BC].reshape(-1)]
        )

    grad_small_all = jnp.concatenate(
        [grad_gain_in, small_parts[:, 0, :OWN].reshape(-1)]
        + [channels(row) for row in range(1, 6)]
        + [
            small_parts[:, 0, OWN : OWN + OWN_H].reshape(-1),
            small_parts[:, 6, :OWN_H].reshape(-1),
            small_parts[:, 7, :OWN_H].reshape(-1),
        ]
    )
    grad_small = lax.dynamic_slice_in_dim(grad_small_all, place.f * SHARD_SMALL, SHARD_SMALL, 0)
    grad_dt = columns(tail_parts[:, :SHARD_IN, OWN + OWN_BC : OWN + OWN_BC + OWN_H])
    rest_grad = jnp.pad(columns(tail_parts[:, :SHARD_IN, OWN : OWN + OWN_BC]), ((0, 0), (0, WIDE - 2 * N)))

    in_table = jnp.concatenate([ahead, jnp.arange(N_REP, 2 * N_REP + 1, dtype=jnp.int32)])
    grad_in, new_first_in, new_second_in, new_in = run_adam_in(
        in_table, early_parts, tail_parts, rest_grad, w_in, first_in, second_in
    )
    grad_out, new_first_out, new_second_out, new_out = run_adam_out(
        ahead, early_parts, w_out, first_out, second_out
    )
    new_dt, new_first_dt, new_second_dt = adam_update(
        w_dt, grad_dt, first_dt, second_dt, RATE_MATRIX, WEIGHT_DECAY
    )
    new_small, new_first_small, new_second_small = adam_update(
        small, grad_small, first_small, second_small, RATE_SMALL, 0.0
    )
    return (
        block_out,
        input_grad,
        grad_in,
        grad_dt,
        grad_out,
        grad_small,
        new_first_in,
        new_first_dt,
        new_first_out,
        new_first_small,
        new_second_in,
        new_second_dt,
        new_second_out,
        new_second_small,
        new_in,
        new_dt,
        new_out,
        new_small,
    )


def solution(mesh):
    rows = P(("fsdp", "rep"), None)
    matrix = P("fsdp", None)
    vector = P("fsdp")
    group = (matrix, matrix, matrix, vector)
    return jax.shard_map(
        body,
        mesh=mesh,
        in_specs=(rows, rows, P()) + group * 3,
        out_specs=(rows, rows) + group * 4,
        check_vma=False,
    )
```

time: 687 us -> 678 us (0.987)
  Pallas kernels: 94.2 us -> 147 us
  starting transfers between devices: 138 us -> 100 us
  matrix products: 27.2 us -> 6.3 us
  local copies, waits for them, and re-layouts: 135 us -> 125 us
    ppermute x81 -> x59, waiting for transfers between devices: 227 us -> 145 us  [move(): return lax.ppermute(value, ('fsdp', 'rep'), pairs)]
    all_gather x2 -> x3, waiting for transfers between devices: 0.01 us -> 55.6 us  [the longest x1 55.6 us: body(): slice_out = lax.all_gather(out_piece, 'fsdp', axis=0, tiled=True)]
    pallas_call x5 -> x11, Pallas kernels: 94.2 us -> 147 us  [the longest x2 34.6 us: run_backward(): pl.pallas_call(partial(backward_kernel, part), grid=(HALF,), in_specs=[pl...]
    ppermute x81 -> x59, starting transfers between devices: 138 us -> 87.3 us  [move(): return lax.ppermute(value, ('fsdp', 'rep'), pairs)]
    dynamic_update_slice x38 -> x0, local copies, waits for them, and re-layouts: 45.3 us -> none  [the longest x22 18.5 us: gather_rep_wide(): out = lax.dynamic_update_slice(out, piece, (offset, jnp.int32(0)))]
    unnamed x142 -> x194, local copies, waits for them, and re-layouts: 11.3 us -> 49.8 us
    all_to_all x0 -> x3, waiting for transfers between devices: none -> 29.8 us  [the longest x1 29.8 us: body(): lax.all_to_all(grad_bc, 'rep', 0, 0, tiled=True)]
    dot_general x3 -> x0, matrix products: 21.7 us -> none  [the longest x2 14.3 us: contract_cols(): lax.dot_general(left_side, right_side, (((1,), (1,)), ((), ())), preferre...]
  transfers between devices with their start and end apart: 83 -> 65, of which waited for: 36 -> 23; matrix products, arithmetic and copies ran while one was open for 27% -> 18% of each run, Pallas kernels for 14% -> 20%
where the time goes in v2:
time: 678 us; the launch traced here: 667 us
  waiting for transfers between devices  230 us (34%)
  Pallas kernels  147 us (22%)
  local copies, waits for them, and re-layouts  125 us (18%)
  starting transfers between devices  100 us (15%)
  other arithmetic  42.5 us (6%)
  between operations  15.6 us (2%)
    ppermute x59, waiting for transfers between devices, move(): return lax.ppermute(value, ('fsdp', 'rep'), pairs)  145 us
    ppermute x59, starting transfers between devices, move(): return lax.ppermute(value, ('fsdp', 'rep'), pairs)  87.3 us
    all_gather x1, waiting for transfers between devices, body(): slice_out = lax.all_gather(out_piece, 'fsdp', axis=0, tiled=True)  55.6 us
    unnamed x194, local copies, waits for them, and re-layouts  49.8 us
    pallas_call x2, Pallas kernels, run_backward(): pl.pallas_call(partial(backward_kernel, part), grid=(HALF,), in_specs=[pl...  34.6 us
    all_to_all x1, waiting for transfers between devices, body(): lax.all_to_all(grad_bc, 'rep', 0, 0, tiled=True)  29.8 us
    pallas_call x2, Pallas kernels, run_forward(): pl.pallas_call(partial(forward_kernel, part), grid=(HALF,), in_specs=[pl....  22.4 us
    pallas_call x1, Pallas kernels, run_input_grad(): pl.pallas_call(input_grad_kernel, grid_spec=pltpu.PrefetchScalarGridSpec(...  16.4 us
  transfers between devices with their start and end apart: 65, of which 23 were waited for; matrix products, arithmetic and copies ran while one was open for 18% of the time, Pallas kernels for 20%

profile of v2, /device:TPU:0, one launch (start us, length us, event | category | flops | bytes accessed | tf_op | source)
XLA Modules:
  0.0 667.1 jit_solution(15345000523896882425)
XLA Ops:
  13.0 55.6 %all-gather.4.cloned.1.call-done.refs_11_ = bf16[1536,384]{1,0:T(8,128)(2,1)} async-done(((bf16[96,384]{1,0:T(8,128)(2,1)}), bf16[1536,384]{1,0:T(8,128)(2,1)}) %all-gather.4.cloned.1.call-update) | async-done | bytes 1179664 | tf_op jit(solution)/shard_map/all_gather | solution.py:1013
  84.5 8.5 %collective-permute-done.refs_9_ = bf16[256,1536]{1,0:T(8,128)(2,1)S(1)} collective-permute-done((bf16[256,1536]{1,0:T(8,128)(2,1)S(1)}, bf16[256,1536]{1,0:T(8,128)(2,1)S(1)}, u32[]{:S(2)}, u32[]{:S(2)}) %collective-permute-start) | collective-permute-done | bytes 786464 | tf_op jit(solution)/shard_map/ppermute | solution.py:54
  93.0 17.2 %collective-permute-done.2.refs_1_ = bf16[256,1536]{1,0:T(8,128)(2,1)S(1)} collective-permute-done((bf16[256,1536]{1,0:T(8,128)(2,1)S(1)}, bf16[256,1536]{1,0:T(8,128)(2,1)S(1)}, u32[]{:S(2)}, u32[]{:S(2)}) %collective-permute-start.2) | collective-permute-done | bytes 786464 | tf_op jit(solution)/shard_map/ppermute | solution.py:54
  141.8 6.6 collective-permute-done.11
  159.0 9.4 %collective-permute-done.13.refs_7_ = bf16[128,1536]{1,0:T(8,128)(2,1)S(1)} collective-permute-done((bf16[128,1536]{1,0:T(8,128)(2,1)S(1)}, bf16[128,1536]{1,0:T(8,128)(2,1)S(1)}, u32[]{:S(2)}, u32[]{:S(2)}) %collective-permute-start.13) | collective-permute-done | bytes 393248 | tf_op jit(solution)/shard_map/ppermute | solution.py:54
  187.0 15.4 %project.1 = (bf16[2048,1536]{1,0:T(8,128)(2,1)}, f32[2048,1152]{1,0:T(8,128)}) custom-call(s32[8]{0:T(128)S(1)} %fusion.31.table, bf16[256,1536]{1,0:T(8,128)(2,1)S(1)} %copy-done.16, bf16[256,1536]{1,0:T(8,128)(2,1)S(1)} %copy-done.46, bf16[256,1536]{1,0:T(8,128)(2,1)S(1)} %copy-done.44, bf16[128,1536]{1,0:T(8,128)(2,1)S(1)} %copy-done.59, ...), custom_call_target="tpu_custom_call" | custom-call | flops 7249999872 | bytes 26000000 | tf_op jit(solution)/shard_map/project/pallas_call | solution.py:593
  202.5 7.1 %collective-permute-done.17.refs_1_ = bf16[256,1536]{1,0:T(8,128)(2,1)} collective-permute-done((bf16[256,1536]{1,0:T(8,128)(2,1)S(1)}, bf16[256,1536]{1,0:T(8,128)(2,1)}, u32[]{:S(2)}, u32[]{:S(2)}) %collective-permute-start.17) | collective-permute-done | bytes 786464 | tf_op jit(solution)/shard_map/ppermute | solution.py:54
  224.5 10.7 %scan_forward.2 = (f32[2048,640]{1,0:T(8,128)S(1)}, f32[2048,384]{1,0:T(8,128)S(1)}, f32[2048,384]{1,0:T(8,128)S(1)}, f32[136,640]{1,0:T(8,128)S(1)}) custom-call(s32[3]{0:T(128)S(1)} %bitcast.213, f32[2048,1152]{1,0:T(8,128)} %get-tuple-element.116.proj.refs_13_.gate_in.conv_in.dt_in, f32[16,640]{1,0:T(8,128)S(1)} %copy-done.47), custom_call_target="tpu_custom_call" | custom-call | flops 8000000000 | bytes 12000000 | tf_op jit(solution)/shard_map/scan_forward/pallas_call | solution.py:367
  251.1 11.7 %scan_forward.3 = (f32[2048,640]{1,0:T(8,128)S(1)}, f32[2048,384]{1,0:T(8,128)S(1)}, f32[2048,384]{1,0:T(8,128)S(1)}, f32[136,640]{1,0:T(8,128)}) custom-call(s32[3]{0:T(128)S(1)} %bitcast.214, f32[2048,1152]{1,0:T(8,128)} %get-tuple-element.116.proj.refs_13_.gate_in.conv_in.dt_in, ...), custom_call_target="tpu_custom_call", output_to_operand_aliasing={{0}: (3, {}), {1}: (4, {}), {2}: (5, {})} | custom-call | flops 8000000000 | bytes 12000000 | tf_op jit(solution)/shard_map/scan_forward/pallas_call | solution.py:367
  266.9 11.9 %out_grad.1 = (bf16[2048,1536]{1,0:T(8,128)(2,1)}, f32[2048,384]{1,0:T(8,128)S(1)}, f32[8,2048]{1,0:T(8,128)S(1)}) custom-call(s32[8]{0:T(128)S(1)} %copy-done.51, bf16[256,1536]{1,0:T(8,128)(2,1)S(1)} %copy-done.24, bf16[256,1536]{1,0:T(8,128)(2,1)} %collective-permute-done.17.refs_1_, bf16[256,1536]{1,0:T(8,128)(2,1)S(1)} %copy-done.30, ...), custom_call_target="tpu_custom_call" | custom-call | flops 2420000000 | bytes 23000000 | tf_op jit(solution)/shard_map/out_grad/pallas_call | solution.py:641
  295.7 15.6 %gate_backward.1 = (bf16[512,768]{1,0:T(8,128)(2,1)S(1)}, bf16[512,768]{1,0:T(8,128)(2,1)S(1)}, bf16[512,768]{1,0:T(8,128)(2,1)S(1)}, bf16[512,768]{1,0:T(8,128)...) custom-call(s32[3]{0:T(128)S(1)} %pad_add_fusion.1.where, ...), custom_call_target="tpu_custom_call" | custom-call | flops 4840000000 | bytes 34000000 | tf_op jit(solution)/shard_map/gate_backward/pallas_call | solution.py:715
  318.0 16.7 %scan_backward.2 = (bf16[2048,384]{1,0:T(8,128)(2,1)S(1)}, bf16[2048,128]{1,0:T(8,128)(2,1)S(1)}, f32[256,2048]{1,0:T(8,128)S(1)}, f32[8,384]{1,0:T(8,128)S(1)},...) custom-call(s32[3]{0:T(128)S(1)} %bitcast.215, f32[2048,1152]{1,0:T(8,128)} %get-tuple-element.116.proj.refs_13_.gate_in.conv_in.dt_in, ...), custom_call_target="tpu_custom_call" | custom-call | flops 12000000000 | bytes 16000000 | tf_op jit(solution)/shard_map/scan_backward/pallas_call | solution.py:512
  334.7 16.0 %collective-permute-done.30.refs_1_ = bf16[512,768]{1,0:T(8,128)(2,1)S(1)} collective-permute-done((bf16[512,768]{1,0:T(8,128)(2,1)S(1)}, bf16[512,768]{1,0:T(8,128)(2,1)S(1)}, u32[]{:S(2)}, u32[]{:S(2)}) %collective-permute-start.30) | collective-permute-done | bytes 786464 | tf_op jit(solution)/shard_map/ppermute | solution.py:54
  351.4 17.9 %scan_backward.3 = (bf16[2048,384]{1,0:T(8,128)(2,1)S(1)}, bf16[2048,128]{1,0:T(8,128)(2,1)S(1)}, f32[256,2048]{1,0:T(8,128)S(1)}, f32[8,384]{1,0:T(8,128)S(1)},...) custom-call(s32[3]{0:T(128)S(1)} %bitcast.216, ...), custom_call_target="tpu_custom_call", output_to_operand_aliasing={{0}: (8, {}), {1}: (9, {}), {2}: (10, {})} | custom-call | flops 12000000000 | bytes 16000000 | tf_op jit(solution)/shard_map/scan_backward/pallas_call | solution.py:512
  378.5 29.8 %all-to-all-done = f32[8,32,2048]{2,1,0:T(8,128)} async-done(((f32[8,32,2048]{2,1,0:T(8,128)}), f32[8,32,2048]{2,1,0:T(8,128)}, u32[]{:S(2)}, u32[]{:S(2)}) %all-to-all-start) | async-done | bytes 2097184 | tf_op jit(solution)/shard_map/all_to_all | solution.py:1129
  419.8 6.3 fusion.40
  439.4 11.1 %collective-permute-done.35 = f32[384,384]{1,0:T(8,128)S(1)} collective-permute-done((f32[384,384]{1,0:T(8,128)S(1)}, f32[384,384]{1,0:T(8,128)S(1)}, u32[]{:S(2)}, u32[]{:S(2)}) %collective-permute-start.35) | collective-permute-done | bytes 589856 | tf_op jit(solution)/shard_map/ppermute | solution.py:54
  450.4 12.0 %collective-permute-done.36 = f32[384,384]{1,0:T(8,128)S(1)} collective-permute-done((f32[384,384]{1,0:T(8,128)S(1)}, f32[384,384]{1,0:T(8,128)S(1)}, u32[]{:S(2)}, u32[]{:S(2)}) %collective-permute-start.36) | collective-permute-done | bytes 589856 | tf_op jit(solution)/shard_map/ppermute | solution.py:54
  479.6 19.3 %collective-permute-done.38 = f32[192,384]{1,0:T(8,128)S(1)} collective-permute-done((f32[192,384]{1,0:T(8,128)}, f32[192,384]{1,0:T(8,128)S(1)}, u32[]{:S(2)}, u32[]{:S(2)}) %collective-permute-start.38) | collective-permute-done | bytes 294944 | tf_op jit(solution)/shard_map/ppermute | solution.py:54
  507.4 5.7 collective-permute-start.40
  548.6 16.4 %input_grad.1 = (f32[256,1536]{1,0:T(8,128)}, f32[8,1536]{1,0:T(8,128)S(1)}) custom-call(s32[9]{0:T(128)S(1)} %pad_add_fusion.table, bf16[512,768]{1,0:T(8,128)(2,1)S(1)} %get-tuple-element.135.refs_0_, bf16[512,768]{1,0:T(8,128)(2,1)S(1)} %copy-done.6, bf16[512,768]{1,0:T(8,128)(2,1)S(1)} %copy-done.9, bf16[512,768]{1,0:T(8,128)(2,1)S(1)} %copy-done.12, ...), custom_call_target="tpu_custom_call" | custom-call | flops 5100000256 | bytes 30000000 | tf_op jit(solution)/shard_map/input_grad/pallas_call | solution.py:831
  572.9 6.5 adam_out.1
  627.3 12.7 %adam_in.1 = (f32[96,6400]{1,0:T(8,128)}, f32[96,6400]{1,0:T(8,128)}, f32[96,6400]{1,0:T(8,128)}, f32[96,6400]{1,0:T(8,128)}) custom-call(s32[17]{0:T(128)S(1)} %pad_add_fusion.2.table, f32[192,384]{1,0:T(8,128)S(1)} %pad_maximum_fusion.7.refs_0_, f32[192,384]{1,0:T(8,128)S(1)} %copy-done.34, f32[192,384]{1,0:T(8,128)} %collective-permute-done.41.refs_2_, ...), custom_call_target="tpu_custom_call" | custom-call | flops 10000000 | bytes 22000000 | tf_op jit(solution)/shard_map/adam_in/pallas_call | solution.py:892
  648.5 11.5 %block_out.1 = f32[256,1536]{1,0:T(8,128)} custom-call(s32[9]{0:T(128)S(1)} %pad_add_fusion.table, bf16[512,768]{1,0:T(8,128)(2,1)S(1)} %get-tuple-element.135.refs_0_, bf16[512,768]{1,0:T(8,128)(2,1)S(1)} %copy-done.7, bf16[512,768]{1,0:T(8,128)(2,1)S(1)} %copy-done.10, bf16[512,768]{1,0:T(8,128)(2,1)S(1)} %copy-done.13, ...), custom_call_target="tpu_custom_call" | custom-call | flops 2420000000 | bytes 14000000 | tf_op jit(solution)/shard_map/block_out/pallas_call | solution.py:778
  (503 shorter events, 299.4 us)
Async XLA Ops:
  7.2 61.4 %all-gather.4.cloned.1.call-start = ((), (), s32[]{:S(2)}) async-start(), calls=%async_computation.3 | async-start | bytes 1253376 | tf_op jit(solution)/shard_map/all_gather | solution.py:1013
  10.1 234.9 %all-gather.6.cloned.1.call-start = ((), (), s32[]{:S(2)}) async-start(), calls=%async_computation.4 | async-start | bytes 20889600 | tf_op jit(solution)/shard_map/all_gather | solution.py:1049
  68.6 574.4 %all-gather.8.cloned.1.call-start = ((), (), s32[]{:S(2)}) async-start(), calls=%async_computation.5 | async-start | bytes 10027008 | tf_op jit(solution)/shard_map/all_gather | solution.py:1050
  75.6 34.6 %collective-permute-start.2 = (bf16[256,1536]{1,0:T(8,128)(2,1)S(1)}, bf16[256,1536]{1,0:T(8,128)(2,1)S(1)}, u32[]{:S(2)}, u32[]{:S(2)}) collective-permute-start(bf16[256,1536]{1,0:T(8,128)(2,1)S(1)} %copy-done.16), channel_id=1, source_target_pairs={{0,1},{1,0},{2,3},{3,2},{4,5},{5,4},{6,7},{7,6},{8,9},{9,8},{10,11... | collective-permute-start | bytes 2359304 | tf_op jit(solution)/shard_map/ppermute | solution.py:54
  169.8 32.6 %collective-permute-start.15 = (bf16[256,1536]{1,0:T(8,128)(2,1)S(1)}, bf16[256,1536]{1,0:T(8,128)(2,1)}, u32[]{:S(2)}, u32[]{:S(2)}) collective-permute-start(bf16[256,1536]{1,0:T(8,128)(2,1)S(1)} %multiply_convert_fusion.refs_0_), channel_id=1, source_target_pairs={{0,2},{1,3},{2,4},{3,5},{4,6},{5,7},{6,0},{7,1},{8,10},{9,11},{10,... | collective-permute-start | bytes 2359304 | tf_op jit(solution)/shard_map/ppermute | solution.py:54
  170.8 31.7 %collective-permute-start.16 = (bf16[256,1536]{1,0:T(8,128)(2,1)S(1)}, bf16[256,1536]{1,0:T(8,128)(2,1)S(1)}, u32[]{:S(2)}, u32[]{:S(2)}) collective-permute-start(bf16[256,1536]{1,0:T(8,128)(2,1)S(1)} %multiply_convert_fusion.refs_0_), channel_id=1, source_target_pairs={{0,6},{1,7},{2,0},{3,1},{4,2},{5,3},{6,4},{7,5},{8,14},{9,15},{10,... | collective-permute-start | bytes 2359304 | tf_op jit(solution)/shard_map/ppermute | solution.py:54
  173.1 36.5 %collective-permute-start.17 = (bf16[256,1536]{1,0:T(8,128)(2,1)S(1)}, bf16[256,1536]{1,0:T(8,128)(2,1)}, u32[]{:S(2)}, u32[]{:S(2)}) collective-permute-start(bf16[256,1536]{1,0:T(8,128)(2,1)S(1)} %multiply_convert_fusion.refs_0_), channel_id=1, source_target_pairs={{0,1},{1,0},{2,3},{3,2},{4,5},{5,4},{6,7},{7,6},{8,9},{9,8},{10,11... | collective-permute-start | bytes 2359304 | tf_op jit(solution)/shard_map/ppermute | solution.py:54
  211.3 28.6 %collective-permute-start.21 = (bf16[256,1536]{1,0:T(8,128)(2,1)}, bf16[256,1536]{1,0:T(8,128)(2,1)}, u32[]{:S(2)}, u32[]{:S(2)}) collective-permute-start(bf16[256,1536]{1,0:T(8,128)(2,1)} %collective-permute-done.15.refs_9_), channel_id=1, source_target_pairs={{0,1},{1,0},{2,3},{3,2},{4,5},{5,4},{6,7},{7,6},{8,9},{9,8},{10,11... | collective-permute-start | bytes 2359304 | tf_op jit(solution)/shard_map/ppermute | solution.py:54
  312.7 38.6 %collective-permute-start.33 = (f32[8,192,384]{2,1,0:T(8,128)}, f32[8,192,384]{2,1,0:T(8,128)S(1)}, u32[]{:S(2)}, u32[]{:S(2)}) collective-permute-start(f32[8,192,384]{2,1,0:T(8,128)} %get-tuple-element.139), channel_id=1, source_target_pairs={{0,8},{1,9},{2,10},{3,11},{4,12},{5,13},{6,14},{7,15},{8,0},{9,1},... | collective-permute-start | bytes 7077896 | tf_op jit(solution)/shard_map/ppermute | solution.py:54
  312.7 38.0 %collective-permute-start.30 = (bf16[512,768]{1,0:T(8,128)(2,1)S(1)}, bf16[512,768]{1,0:T(8,128)(2,1)S(1)}, u32[]{:S(2)}, u32[]{:S(2)}) collective-permute-start(bf16[512,768]{1,0:T(8,128)(2,1)S(1)} %get-tuple-element.136), channel_id=1, source_target_pairs={{0,2},{1,3},{2,4},{3,5},{4,6},{5,7},{6,0},{7,1},{8,10},{9,11},{10,... | collective-permute-start | bytes 2359304 | tf_op jit(solution)/shard_map/ppermute | solution.py:54
  312.7 38.0 %collective-permute-start.31 = (bf16[512,768]{1,0:T(8,128)(2,1)S(1)}, bf16[512,768]{1,0:T(8,128)(2,1)S(1)}, u32[]{:S(2)}, u32[]{:S(2)}) collective-permute-start(bf16[512,768]{1,0:T(8,128)(2,1)S(1)} %get-tuple-element.137), channel_id=1, source_target_pairs={{0,4},{1,5},{2,6},{3,7},{4,0},{5,1},{6,2},{7,3},{8,12},{9,13},{10,... | collective-permute-start | bytes 2359304 | tf_op jit(solution)/shard_map/ppermute | solution.py:54
  313.8 37.5 %collective-permute-start.32 = (bf16[512,768]{1,0:T(8,128)(2,1)S(1)}, bf16[512,768]{1,0:T(8,128)(2,1)S(1)}, u32[]{:S(2)}, u32[]{:S(2)}) collective-permute-start(bf16[512,768]{1,0:T(8,128)(2,1)S(1)} %get-tuple-element.138), channel_id=1, source_target_pairs={{0,6},{1,7},{2,0},{3,1},{4,2},{5,3},{6,4},{7,5},{8,14},{9,15},{10,... | collective-permute-start | bytes 2359304 | tf_op jit(solution)/shard_map/ppermute | solution.py:54
  372.6 35.8 %all-to-all-start = ((f32[8,32,2048]{2,1,0:T(8,128)}), f32[8,32,2048]{2,1,0:T(8,128)}, u32[]{:S(2)}, u32[]{:S(2)}) async-start(f32[8,32,2048]{2,1,0:T(8,128)} %bitcast.210), calls=%async_computation | async-start | bytes 4194304 | tf_op jit(solution)/shard_map/all_to_all | solution.py:1129
  428.3 44.6 %collective-permute-start.47 = (f32[776,512]{1,0:T(8,128)}, f32[776,512]{1,0:T(8,128)}, u32[]{:S(2)}, u32[]{:S(2)}) collective-permute-start(f32[776,512]{1,0:T(8,128)} %maximum_maximum_fusion.1), channel_id=1, source_target_pairs={{0,8},{1,9},{2,10},{3,11},{4,12},{5,13},{6,14},{7,15},{8,0},{9,1},... | collective-permute-start | bytes 4767752 | tf_op jit(solution)/shard_map/ppermute | solution.py:54
  433.1 29.3 %collective-permute-start.36 = (f32[384,384]{1,0:T(8,128)S(1)}, f32[384,384]{1,0:T(8,128)S(1)}, u32[]{:S(2)}, u32[]{:S(2)}) collective-permute-start(f32[384,384]{1,0:T(8,128)S(1)} %bitcast.231), channel_id=1, source_target_pairs={{0,48},{1,49},{2,50},{3,51},{4,52},{5,53},{6,54},{7,55},{8,56},{9,... | collective-permute-start | bytes 1769480 | tf_op jit(solution)/shard_map/ppermute | solution.py:54
  439.3 102.6 %collective-permute-start.34 = (bf16[1024,768]{1,0:T(8,128)(2,1)}, bf16[1024,768]{1,0:T(8,128)(2,1)}, u32[]{:S(2)}, u32[]{:S(2)}) collective-permute-start(bf16[1024,768]{1,0:T(8,128)(2,1)} %pad_maximum_fusion.1), channel_id=1, source_target_pairs={{0,1},{1,0},{2,3},{3,2},{4,5},{5,4},{6,7},{7,6},{8,9},{9,8},{10,11... | collective-permute-start | bytes 4718600 | tf_op jit(solution)/shard_map/ppermute | solution.py:54
  466.6 32.4 %collective-permute-start.38 = (f32[192,384]{1,0:T(8,128)}, f32[192,384]{1,0:T(8,128)S(1)}, u32[]{:S(2)}, u32[]{:S(2)}) collective-permute-start(f32[192,384]{1,0:T(8,128)} %dynamic-slice_bitcast_fusion), channel_id=1, source_target_pairs={{0,64},{1,65},{2,66},{3,67},{4,68},{5,69},{6,70},{7,71},{8,72},{9,... | collective-permute-start | bytes 884744 | tf_op jit(solution)/shard_map/ppermute | solution.py:54
  468.0 53.4 %all-to-all-start.1 = ((bf16[8,256,512]{2,1,0:T(8,128)(2,1)}), bf16[8,256,512]{2,1,0:T(8,128)(2,1)S(1)}, u32[]{:S(2)}, u32[]{:S(2)}) async-start(bf16[8,256,512]{2,1,0:T(8,128)(2,1)} %bitcast.218), calls=%async_computation.1 | async-start | bytes 4194304 | tf_op jit(solution)/shard_map/all_to_all | solution.py:1178
  507.4 29.5 %collective-permute-start.40 = (f32[192,384]{1,0:T(8,128)S(1)}, f32[192,384]{1,0:T(8,128)S(1)}, u32[]{:S(2)}, u32[]{:S(2)}) collective-permute-start(f32[192,384]{1,0:T(8,128)S(1)} %pad_maximum_fusion.7.refs_0_), channel_id=1, source_target_pairs={{0,1},{1,0},{2,3},{3,2},{4,5},{5,4},{6,7},{7,6},{8,9},{9,8},{10,11... | collective-permute-start | bytes 884744 | tf_op jit(solution)/shard_map/ppermute | solution.py:54
  515.6 49.5 %collective-permute-start.42 = (f32[192,384]{1,0:T(8,128)S(1)}, f32[192,384]{1,0:T(8,128)}, u32[]{:S(2)}, u32[]{:S(2)}) collective-permute-start(f32[192,384]{1,0:T(8,128)S(1)} %pad_maximum_fusion.7.refs_0_), channel_id=1, source_target_pairs={{0,7},{1,6},{2,1},{3,0},{4,3},{5,2},{6,5},{7,4},{8,15},{9,14},{10,... | collective-permute-start | bytes 884744 | tf_op jit(solution)/shard_map/ppermute | solution.py:54
  515.6 53.5 %collective-permute-start.43 = (f32[192,384]{1,0:T(8,128)S(1)}, f32[192,384]{1,0:T(8,128)}, u32[]{:S(2)}, u32[]{:S(2)}) collective-permute-start(f32[192,384]{1,0:T(8,128)S(1)} %pad_maximum_fusion.7.refs_0_), channel_id=1, source_target_pairs={{0,4},{1,5},{2,6},{3,7},{4,0},{5,1},{6,2},{7,3},{8,12},{9,13},{10,... | collective-permute-start | bytes 884744 | tf_op jit(solution)/shard_map/ppermute | solution.py:54
  523.7 57.6 %all-to-all-start.2 = ((f32[8,104,512]{2,1,0:T(8,128)}), f32[8,104,512]{2,1,0:T(8,128)}, u32[]{:S(2)}, u32[]{:S(2)}) async-start(f32[8,104,512]{2,1,0:T(8,128)} %broadcast_in_dim.117), calls=%async_computation.2 | async-start | bytes 3407872 | tf_op jit(solution)/shard_map/all_to_all | solution.py:1202
  536.9 32.2 %collective-permute-start.44 = (f32[192,384]{1,0:T(8,128)S(1)}, f32[192,384]{1,0:T(8,128)}, u32[]{:S(2)}, u32[]{:S(2)}) collective-permute-start(f32[192,384]{1,0:T(8,128)S(1)} %pad_maximum_fusion.7.refs_0_), channel_id=1, source_target_pairs={{0,5},{1,4},{2,7},{3,6},{4,1},{5,0},{6,3},{7,2},{8,13},{9,12},{10,... | collective-permute-start | bytes 884744 | tf_op jit(solution)/shard_map/ppermute | solution.py:54
  604.2 35.9 %collective-permute-start.58 = (f32[12,128]{1,0:T(8,128)S(1)}, f32[12,128]{1,0:T(8,128)}, u32[]{:S(2)}, u32[]{:S(2)}) collective-permute-start(f32[12,128]{1,0:T(8,128)S(1)} %add.557), channel_id=1, source_target_pairs={{0,64},{1,65},{2,66},{3,67},{4,68},{5,69},{6,70},{7,71},{8,72},{9,... | collective-permute-start | bytes 18440 | tf_op jit(solution)/shard_map/ppermute | solution.py:54
  (138 other events, 2117.8 us)
Sparse Core Ops, SparseCore 0:
  11.1 57.4 all-gather.3
  71.7 159.0 all-gather.5
  245.1 75.1 all-gather.7

commit v3 on v2

--- a/solution.py
+++ b/solution.py
@@ -26,12 +26,11 @@
 SHARD_IN = D // N_FSDP
 SHARD_OUT = DI // N_FSDP
 SHARD_SMALL = SMALL // N_FSDP
-TAIL = 512
 WIDE = 384
 CHUNK = 128
 CHUNKS = PACK // CHUNK
 HALF = CHUNKS // 2
-VMEM_LIMIT = 40 * 1024 * 1024
+VMEM_LIMIT = 60 * 1024 * 1024
 
 NORM_EPS = 1e-05
 BETA_ONE = 0.9
@@ -111,11 +110,12 @@
     return out
 
 
-def exchange_rep(value):
-    found = {(0, 0): value}
-    for dx, dy in ((1, 0), (3, 0), (0, 1), (2, 0), (1, 1), (3, 1), (2, 1)):
-        found[dx, dy] = move(value, lambda yh, z, c, x, yl: (yh, z, c, x - dx, yl + dy))
-    return [found[k // 2, k % 2] for k in range(N_REP)]
+def exchange(value, axis):
+    return lax.all_to_all(value, axis, 0, 0, tiled=True)
+
+
+def share_rep(value):
+    return exchange(jnp.broadcast_to(value[None], (N_REP,) + value.shape), "rep")
 
 
 def sum_rep(value):
@@ -130,32 +130,6 @@
     value = value + move(value, lambda yh, z, c, x, yl: (yh, z ^ 1, c, x, yl))
     value = value + move(value, lambda yh, z, c, x, yl: (yh, z ^ 2, c, x, yl))
     return value + move(value, swap_y_hi)
-
-
-def with_rows(block, extra):
-    width = block.shape[-1]
-    flat = block.reshape(-1, width)
-    return flat if extra is None else jnp.concatenate([flat, extra], 0)
-
-
-def received(block, target, base, add_to):
-    got = move(with_rows(block, base), target)
-    rows = got.shape[0] - (0 if base is None else base.shape[0])
-    return got[:rows].reshape(add_to.shape), got[rows:]
-
-
-def scatter_ring(keep, got, extra, place):
-    z_sum = at(keep, place.z, 1) + at(got, place.z, 1)
-    found = []
-    for step in (1, 3, 2):
-        there = (place.z + step) % 4
-        found.append(received(at(keep, there, 1) + at(got, there, 1), along_z(step), extra, z_sum))
-    z_sum = z_sum + found[0][0] + found[1][0] + found[2][0]
-    if extra is not None:
-        extra = extra + found[0][1] + found[1][1] + found[2][1]
-    mine = at(z_sum, place.yh)
-    more, more_extra = received(at(z_sum, 1 - place.yh), swap_y_hi, extra, mine)
-    return mine + more, (None if extra is None else extra + more_extra)
 
 
 def adam_update(weight, gradient, moment_one, moment_two, learn_rate, decay_rate):
@@ -460,8 +434,8 @@
     grad_c = precise_product(grad_scores.T, state_b) + joined_product(
         entered_parts, split_two(state_in), 1, 1
     )
-    grad_bc[0:N, :] = grad_b.T
-    grad_bc[N:, :] = grad_c.T
+    grad_bc[0:N, :] = grad_b.T.astype(BF16)
+    grad_bc[N:, :] = grad_c.T.astype(BF16)
     new_carry = spread(facts["passing"], lane[:1]) * carry + joined_product(
         split_two(state_c.T), entered_parts
     )
@@ -534,7 +508,7 @@
         out_shape=[
             jax.ShapeDtypeStruct((PACK, OWN), BF16),
             jax.ShapeDtypeStruct((PACK, N), BF16),
-            jax.ShapeDtypeStruct((2 * N, PACK), F32),
+            jax.ShapeDtypeStruct((2 * N, PACK), BF16),
             jax.ShapeDtypeStruct((8, OWN), F32),
             jax.ShapeDtypeStruct((8, N), F32),
             jax.ShapeDtypeStruct((N + 16, OWN), F32),
@@ -553,7 +527,8 @@
     )(ends, proj, proj, pre, mixed, grad_mixed, states, par, *before)
 
 
-PARTS = (1, 1, 1, 2, 2, 2, 1, 1)
+PARTS = (1, 1, 1, 1, 2, 2, 1, 1)
+PIECES = sum(PARTS)
 
 
 def load_block(step, pieces, block):
@@ -578,7 +553,16 @@
 
 
 def project_kernel(table, *refs):
-    pieces, (gain, weight, normed_out, proj, block) = refs[:11], refs[11:]
+    pieces, (gain, mine, other, normed_out, proj, dt_out, block, weight) = refs[:PIECES], refs[PIECES:]
+
+    @pl.when(pl.program_id(0) == 0)
+    def _():
+        core = table[N_REP]
+        for k in range(N_FSDP // 2):
+            for ref, place in ((mine, 2 * k + core), (other, 2 * k + 1 - core)):
+                weight[pl.ds(pl.multiple_of(place * SHARD_IN, SHARD_IN), SHARD_IN), :] = ref[k]
+        dt_out[...] = weight[:, 1024:]
+
     load_block(pl.program_id(0), pieces, block)
     values = block[...].astype(F32)
     scale = lax.rsqrt(jnp.mean(values * values, axis=1, keepdims=True) + NORM_EPS)
@@ -587,7 +571,7 @@
     proj[...] = matmul(normed, weight[...])
 
 
-def run_project(table, pieces, gain, weight):
+def run_project(table, pieces, gain, mine, other):
     fixed = lambda shape: pl.BlockSpec(shape, lambda i, table: (0, 0))
     placed = lambda width: pl.BlockSpec((ROWS, width), lambda i, table: (table[i], 0))
     return pl.pallas_call(
@@ -595,17 +579,23 @@
         grid_spec=pltpu.PrefetchScalarGridSpec(
             num_scalar_prefetch=1,
             grid=(N_REP,),
-            in_specs=piece_specs() + [fixed((1, D)), fixed((D, 3 * WIDE))],
-            out_specs=[placed(D), placed(3 * WIDE)],
-            scratch_shapes=[pltpu.VMEM((ROWS, D), BF16)],
+            in_specs=piece_specs()
+            + [fixed((1, D))]
+            + [pl.BlockSpec((N_FSDP // 2, SHARD_IN, 3 * WIDE), lambda i, table: (0, 0, 0))] * 2,
+            out_specs=[placed(D), placed(3 * WIDE), fixed((D, N))],
+            scratch_shapes=[pltpu.VMEM((ROWS, D), BF16), pltpu.VMEM((D, 3 * WIDE), BF16)],
         ),
-        out_shape=[jax.ShapeDtypeStruct((PACK, D), BF16), jax.ShapeDtypeStruct((PACK, 3 * WIDE), F32)],
+        out_shape=[
+            jax.ShapeDtypeStruct((PACK, D), BF16),
+            jax.ShapeDtypeStruct((PACK, 3 * WIDE), F32),
+            jax.ShapeDtypeStruct((D, N), BF16),
+        ],
         compiler_params=pltpu.CompilerParams(
             dimension_semantics=("arbitrary",), vmem_limit_bytes=VMEM_LIMIT
         ),
         cost_estimate=pl.CostEstimate(flops=7_250_000_000, bytes_accessed=26_000_000, transcendentals=0),
         name="project",
-    )(table, *pieces, gain, weight)
+    )(table, *pieces, gain, mine, other)
 
 
 def row_sums(value):
@@ -614,13 +604,12 @@
 
 
 def out_grad_kernel(table, *refs):
-    pieces = refs[:11]
-    w_out, mixed, gate_in, gain, branch_out, grad_out, sums, block, turned = refs[11:]
+    pieces = refs[:PIECES]
+    w_out, mixed, gate_in, gain, branch_out, grad_out, sums, block, turned = refs[PIECES:]
 
     @pl.when(pl.program_id(0) == 0)
     def _():
-        for k in range(4):
-            turned[k * WIDE : (k + 1) * WIDE, :] = w_out[k * WIDE : (k + 1) * WIDE, :].T
+        turned[...] = w_out[...].T
 
     load_block(pl.program_id(0), pieces, block)
     branch = block[...]
@@ -643,7 +632,9 @@
         grid_spec=pltpu.PrefetchScalarGridSpec(
             num_scalar_prefetch=1,
             grid=(N_REP,),
-            in_specs=piece_specs() + [fixed((D, WIDE)), placed(OWN), placed(OWN), fixed((1, OWN))],
+            in_specs=piece_specs()
+            + [pl.BlockSpec((OWN, D), lambda i, table: (table[N_REP], 0))]
+            + [placed(OWN), placed(OWN), fixed((1, OWN))],
             out_specs=[placed(D), placed(OWN), pl.BlockSpec((8, ROWS), lambda i, table: (0, table[i]))],
             scratch_shapes=[pltpu.VMEM((ROWS, D), BF16), pltpu.VMEM((D, WIDE), BF16)],
         ),
@@ -661,8 +652,8 @@
 
 
 def gate_kernel(
-    where, grad_out, mixed_in, gate_in, sums, gain, grad_branch, normed,
-    row_zero, row_one, row_two, row_three, grad_mixed, keep, give, grad_gain, total,
+    grad_out, mixed_in, gate_in, sums, gain, grad_branch, normed,
+    low_out, grad_mixed, total, grad_gain,
 ):
     step = pl.program_id(0)
     rows = grad_out.shape[0]
@@ -678,13 +669,8 @@
     grad_gated = out_scale * (grad_o * gain[...]) - gated * pull
     grad_mixed[...] = grad_gated * silu
     grad_z = (grad_gated * mixed * (gate_sig * (1.0 + gate * (1.0 - gate_sig)))).astype(BF16)
-    ahead = (step - where[1] + 4) % 4
-    for slot, ref in enumerate((row_zero, row_one, row_two, row_three)):
-
-        @pl.when(ahead == slot)
-        def _(ref=ref):
-            ref[:, :OWN] = low
-            ref[:, OWN:] = grad_z
+    low_out[:, :OWN] = low
+    low_out[:, OWN:] = grad_z
 
     @pl.when(step == 0)
     def _():
@@ -700,23 +686,15 @@
     for f in range(N_FSDP):
         total[f, SHARD_IN:] += part[f * SHARD_IN : (f + 1) * SHARD_IN]
 
-    @pl.when(step == pl.num_programs(0) - 1)
-    def _():
-        for k in range(N_FSDP // 2):
-            keep[k] = total[2 * k + where[0]]
-            give[k] = total[2 * k + 1 - where[0]]
-
-
-def run_gate(where, grad_out, mixed, proj, sums, gain, grad_branch, normed):
+
+def run_gate(grad_out, mixed, proj, sums, gain, grad_branch, normed):
     count = 2 * ROWS
     rows = lambda width: pl.BlockSpec((count, width), lambda i: (i, 0))
     fixed = lambda shape: pl.BlockSpec(shape, lambda i: (0,) * len(shape))
-    half = (N_FSDP // 2, 2 * SHARD_IN, WIDE)
     return pl.pallas_call(
         gate_kernel,
         grid=(PACK // count,),
         in_specs=[
-            pl.BlockSpec(memory_space=pltpu.SMEM),
             rows(OWN),
             rows(OWN),
             rows(OWN),
@@ -725,40 +703,24 @@
             rows(D),
             rows(D),
         ],
-        out_specs=[fixed((count, 2 * OWN))] * 4 + [rows(OWN), fixed(half), fixed(half), fixed((8, OWN))],
-        out_shape=[jax.ShapeDtypeStruct((count, 2 * OWN), BF16)] * 4
-        + [
+        out_specs=[rows(2 * OWN), rows(OWN), fixed((N_FSDP, 2 * SHARD_IN, WIDE)), fixed((8, OWN))],
+        out_shape=[
+            jax.ShapeDtypeStruct((PACK, 2 * OWN), BF16),
             jax.ShapeDtypeStruct((PACK, OWN), F32),
-            jax.ShapeDtypeStruct(half, F32),
-            jax.ShapeDtypeStruct(half, F32),
+            jax.ShapeDtypeStruct((N_FSDP, 2 * SHARD_IN, WIDE), F32),
             jax.ShapeDtypeStruct((8, OWN), F32),
         ],
-        scratch_shapes=[pltpu.VMEM((N_FSDP, 2 * SHARD_IN, WIDE), F32)],
         compiler_params=pltpu.CompilerParams(
             dimension_semantics=("arbitrary",), vmem_limit_bytes=VMEM_LIMIT
         ),
         cost_estimate=pl.CostEstimate(flops=4_840_000_000, bytes_accessed=34_000_000, transcendentals=800_000),
         name="gate_backward",
-    )(where, grad_out, mixed, proj, sums, gain, grad_branch, normed)
-
-
-def own_rows(step, table, mine, other, block, columns):
-    for k in range(4):
-
-        @pl.when(step == 2 * k)
-        def _(k=k):
-            block[...] = mine[k][pl.ds(pl.multiple_of(table[8] * ROWS, ROWS), ROWS), columns]
-
-        @pl.when(step == 2 * k + 1)
-        def _(k=k):
-            block[...] = other[k * ROWS : (k + 1) * ROWS, columns]
-
-
-def block_out_kernel(table, *refs):
-    mine, (other, weight, tokens, live, out, block) = refs[:4], refs[4:]
+    )(grad_out, mixed, proj, sums, gain, grad_branch, normed)
+
+
+def block_out_kernel(rows, weight, tokens, live, out):
     step = pl.program_id(0)
-    own_rows(step, table, mine, other, block, slice(0, OWN))
-    part = matmul(block[...], weight[...])
+    part = matmul(rows[0], weight[...])
 
     @pl.when(step == 0)
     def _():
@@ -773,42 +735,64 @@
         out[...] = tokens[...].astype(F32) + live[...] * out[...]
 
 
-def run_block_out(table, mine, other, weight, tokens, live):
-    fixed = lambda shape: pl.BlockSpec(shape, lambda i, table: (0, 0))
+def run_block_out(rows, weight, tokens, live):
+    fixed = lambda shape: pl.BlockSpec(shape, lambda i: (0, 0))
     return pl.pallas_call(
         block_out_kernel,
-        grid_spec=pltpu.PrefetchScalarGridSpec(
-            num_scalar_prefetch=1,
-            grid=(N_REP,),
-            in_specs=[fixed((2 * ROWS, 2 * OWN))] * 4
-            + [
-                fixed((4 * ROWS, 2 * OWN)),
-                pl.BlockSpec((OWN, D), lambda i, table: (table[i], 0)),
-                fixed((ROWS, D)),
-                fixed((ROWS, 1)),
-            ],
-            out_specs=fixed((ROWS, D)),
-            scratch_shapes=[pltpu.VMEM((ROWS, OWN), BF16)],
-        ),
+        grid=(N_REP,),
+        in_specs=[
+            pl.BlockSpec((1, ROWS, OWN), lambda i: (i, 0, 0)),
+            pl.BlockSpec((OWN, D), lambda i: (i, 0)),
+            fixed((ROWS, D)),
+            fixed((ROWS, 1)),
+        ],
+        out_specs=fixed((ROWS, D)),
         out_shape=jax.ShapeDtypeStruct((ROWS, D), F32),
         compiler_params=pltpu.CompilerParams(
             dimension_semantics=("arbitrary",), vmem_limit_bytes=VMEM_LIMIT
         ),
         cost_estimate=pl.CostEstimate(flops=2_420_000_000, bytes_accessed=14_000_000, transcendentals=0),
         name="block_out",
-    )(table, *mine, other, weight, tokens, live)
-
-
-def input_grad_kernel(table, *refs):
-    mine, refs = refs[:4], refs[4:]
-    other, tail, rest, w_z, w_x, w_bc, w_dt, tokens, cotangent, gain, out, gain_out, block = refs
+    )(rows, weight, tokens, live)
+
+
+def z_grad_kernel(rows, weight, out):
+    part = contract_cols(rows[0], weight[...])
+
+    @pl.when(pl.program_id(0) == 0)
+    def _():
+        out[...] = part
+
+    @pl.when(pl.program_id(0) > 0)
+    def _():
+        out[...] += part
+
+
+def run_z_grad(rows, full_in):
+    return pl.pallas_call(
+        z_grad_kernel,
+        grid=(N_REP,),
+        in_specs=[
+            pl.BlockSpec((1, ROWS, OWN), lambda i: (i, 0, 1)),
+            pl.BlockSpec((D, OWN), lambda i: (0, i)),
+        ],
+        out_specs=pl.BlockSpec((ROWS, D), lambda i: (0, 0)),
+        out_shape=jax.ShapeDtypeStruct((ROWS, D), F32),
+        compiler_params=pltpu.CompilerParams(
+            dimension_semantics=("arbitrary",), vmem_limit_bytes=VMEM_LIMIT
+        ),
+        cost_estimate=pl.CostEstimate(flops=2_420_000_000, bytes_accessed=14_000_000, transcendentals=0),
+        name="z_grad",
+    )(rows, full_in)
+
+
+def input_grad_kernel(grad_z, rows, rest, w_x, w_bc, w_dt, tokens, cotangent, gain, out, gain_out):
     step = pl.program_id(0)
-    own_rows(step, table, mine, other, block, slice(OWN, 2 * OWN))
-    part = contract_cols(block[...], w_z[...]) + contract_cols(tail[0, :, :OWN], w_x[...])
+    part = contract_cols(rows[0], w_x[...])
 
     @pl.when(step == 0)
     def _():
-        out[...] = part
+        out[...] = grad_z[...] + part
 
     @pl.when(step > 0)
     def _():
@@ -826,126 +810,113 @@
         out[...] = cotangent[...].astype(F32) + scale * (grad_unit - unit * inner)
 
 
-def run_input_grad(table, mine, other, tail, rest, full_in, low_dt, tokens, cotangent, gain):
-    fixed = lambda shape: pl.BlockSpec(shape, lambda i, table: (0, 0))
+def run_input_grad(grad_z, rows, rest, full_in, low_dt, tokens, cotangent, gain):
+    fixed = lambda shape: pl.BlockSpec(shape, lambda i: (0, 0))
     return pl.pallas_call(
         input_grad_kernel,
-        grid_spec=pltpu.PrefetchScalarGridSpec(
-            num_scalar_prefetch=1,
-            grid=(N_REP,),
-            in_specs=[fixed((2 * ROWS, 2 * OWN))] * 4
-            + [
-                fixed((4 * ROWS, 2 * OWN)),
-                pl.BlockSpec((1, ROWS, TAIL), lambda i, table: (table[i], 0, 0)),
-                fixed((ROWS, 3 * N)),
-                pl.BlockSpec((D, OWN), lambda i, table: (0, table[i])),
-                pl.BlockSpec((D, OWN), lambda i, table: (0, N_REP + table[i])),
-                pl.BlockSpec((D, 2 * N), lambda i, table: (0, DI // N)),
-                fixed((D, N)),
-                fixed((ROWS, D)),
-                fixed((ROWS, D)),
-                fixed((1, D)),
-            ],
-            out_specs=[fixed((ROWS, D)), fixed((8, D))],
-            scratch_shapes=[pltpu.VMEM((ROWS, OWN), BF16)],
-        ),
+        grid=(N_REP,),
+        in_specs=[
+            fixed((ROWS, D)),
+            pl.BlockSpec((1, ROWS, OWN), lambda i: (i, 0, 0)),
+            fixed((ROWS, 3 * N)),
+            pl.BlockSpec((D, OWN), lambda i: (0, N_REP + i)),
+            pl.BlockSpec((D, 2 * N), lambda i: (0, DI // N)),
+            fixed((D, N)),
+            fixed((ROWS, D)),
+            fixed((ROWS, D)),
+            fixed((1, D)),
+        ],
+        out_specs=[fixed((ROWS, D)), fixed((8, D))],
         out_shape=[jax.ShapeDtypeStruct((ROWS, D), F32), jax.ShapeDtypeStruct((8, D), F32)],
         compiler_params=pltpu.CompilerParams(
             dimension_semantics=("arbitrary",), vmem_limit_bytes=VMEM_LIMIT
         ),
-        cost_estimate=pl.CostEstimate(flops=5_100_000_000, bytes_accessed=30_000_000, transcendentals=0),
+        cost_estimate=pl.CostEstimate(flops=2_700_000_000, bytes_accessed=18_000_000, transcendentals=0),
         name="input_grad",
-    )(table, *mine, other, tail, rest, full_in, full_in, full_in, low_dt, tokens, cotangent, gain)
-
-
-def adam_in_kernel(table, *refs):
-    early, (tail, rest, weight, first, second) = refs[:N_REP], refs[N_REP : N_REP + 5]
-    grad_out, first_out, second_out, weight_out, grad = refs[N_REP + 5 :]
-    step = pl.program_id(0)
-    for slot in range(N_REP):
-
-        @pl.when(step == slot)
-        def _(slot=slot):
-            grad[...] = early[slot][SHARD_IN:, :]
-
-    @pl.when((step >= N_REP) & (step < 2 * N_REP))
-    def _():
-        grad[...] = tail[jnp.clip(step - N_REP, 0, N_REP - 1), :SHARD_IN, :OWN]
-
-    @pl.when(step == 2 * N_REP)
-    def _():
-        grad[...] = rest[...]
-
+    )(grad_z, rows, rest, full_in, full_in, low_dt, tokens, cotangent, gain)
+
+
+def adam_step(grad, weight, first, second, grad_out, first_out, second_out, weight_out):
     new_weight, new_first, new_second = adam_update(
-        weight[...], grad[...], first[...], second[...], RATE_MATRIX, WEIGHT_DECAY
-    )
-    grad_out[...] = grad[...]
+        weight[...], grad, first[...], second[...], RATE_MATRIX, WEIGHT_DECAY
+    )
+    grad_out[...] = grad
     first_out[...] = new_first
     second_out[...] = new_second
     weight_out[...] = new_weight
 
 
-def run_adam_in(table, early, tail, rest, weight, first, second):
-    fixed = lambda shape: pl.BlockSpec(shape, lambda i, table: (0,) * len(shape))
-    column = pl.BlockSpec((SHARD_IN, WIDE), lambda i, table: (0, table[i]))
+def adam_in_kernel(early, tail, rest, *refs):
+    arrays, grad = refs[:7], refs[7]
+    step = pl.program_id(0)
+    half = N_REP // 2
+
+    @pl.when(step < half)
+    def _():
+        grad[:, :WIDE] = early[0, SHARD_IN:]
+        grad[:, WIDE:] = early[1, SHARD_IN:]
+
+    @pl.when((step >= half) & (step < 2 * half))
+    def _():
+        grad[:, :WIDE] = tail[0]
+        grad[:, WIDE:] = tail[1]
+
+    @pl.when(step == 2 * half)
+    def _():
+        grad[...] = rest[...]
+
+    adam_step(grad[...], *arrays)
+
+
+def run_adam_in(early, tail, rest, weight, first, second):
+    half = N_REP // 2
+    column = pl.BlockSpec((SHARD_IN, 2 * WIDE), lambda i: (0, i))
     shape = jax.ShapeDtypeStruct(weight.shape, F32)
     return pl.pallas_call(
         adam_in_kernel,
-        grid_spec=pltpu.PrefetchScalarGridSpec(
-            num_scalar_prefetch=1,
-            grid=(2 * N_REP + 1,),
-            in_specs=[fixed((2 * SHARD_IN, WIDE))] * N_REP
-            + [fixed(tail.shape), fixed((SHARD_IN, WIDE)), column, column, column],
-            out_specs=[column] * 4,
-            scratch_shapes=[pltpu.VMEM((SHARD_IN, WIDE), F32)],
-        ),
+        grid=(2 * half + 1,),
+        in_specs=[
+            pl.BlockSpec((2, 2 * SHARD_IN, WIDE), lambda i: (jnp.minimum(i, half - 1), 0, 0)),
+            pl.BlockSpec((2, SHARD_IN, WIDE), lambda i: (jnp.clip(i - half, 0, half - 1), 0, 0)),
+            pl.BlockSpec((SHARD_IN, 2 * WIDE), lambda i: (0, 0)),
+            column,
+            column,
+            column,
+        ],
+        out_specs=[column] * 4,
         out_shape=[shape] * 4,
+        scratch_shapes=[pltpu.VMEM((SHARD_IN, 2 * WIDE), F32)],
         compiler_params=pltpu.CompilerParams(
             dimension_semantics=("arbitrary",), vmem_limit_bytes=VMEM_LIMIT
         ),
         cost_estimate=pl.CostEstimate(flops=10_000_000, bytes_accessed=22_000_000, transcendentals=1_200_000),
         name="adam_in",
-    )(table, *early, tail, rest, weight, first, second)
-
-
-def adam_out_kernel(table, *refs):
-    early, (weight, first, second) = refs[:N_REP], refs[N_REP : N_REP + 3]
-    grad_out, first_out, second_out, weight_out, grad = refs[N_REP + 3 :]
-    for slot in range(N_REP):
-
-        @pl.when(pl.program_id(0) == slot)
-        def _(slot=slot):
-            grad[...] = early[slot][:SHARD_IN, :]
-
-    new_weight, new_first, new_second = adam_update(
-        weight[...], grad[...], first[...], second[...], RATE_MATRIX, WEIGHT_DECAY
-    )
-    grad_out[...] = grad[...]
-    first_out[...] = new_first
-    second_out[...] = new_second
-    weight_out[...] = new_weight
-
-
-def run_adam_out(table, early, weight, first, second):
-    fixed = lambda shape: pl.BlockSpec(shape, lambda i, table: (0,) * len(shape))
-    part = pl.BlockSpec((SHARD_IN, WIDE), lambda i, table: (table[i] // 4, table[i] % 4))
+    )(early, tail, rest, weight, first, second)
+
+
+def adam_out_kernel(early, *refs):
+    arrays, grad = refs[:7], refs[7]
+    for k in range(4):
+        grad[:, k * WIDE : (k + 1) * WIDE] = early[k, :SHARD_IN]
+    adam_step(grad[...], *arrays)
+
+
+def run_adam_out(early, weight, first, second):
+    part = pl.BlockSpec((SHARD_IN, D), lambda i: (i, 0))
     shape = jax.ShapeDtypeStruct(weight.shape, F32)
     return pl.pallas_call(
         adam_out_kernel,
-        grid_spec=pltpu.PrefetchScalarGridSpec(
-            num_scalar_prefetch=1,
-            grid=(N_REP,),
-            in_specs=[fixed((2 * SHARD_IN, WIDE))] * N_REP + [part] * 3,
-            out_specs=[part] * 4,
-            scratch_shapes=[pltpu.VMEM((SHARD_IN, WIDE), F32)],
-        ),
+        grid=(2,),
+        in_specs=[pl.BlockSpec((4, 2 * SHARD_IN, WIDE), lambda i: (i, 0, 0))] + [part] * 3,
+        out_specs=[part] * 4,
         out_shape=[shape] * 4,
+        scratch_shapes=[pltpu.VMEM((SHARD_IN, D), F32)],
         compiler_params=pltpu.CompilerParams(
             dimension_semantics=("arbitrary",), vmem_limit_bytes=VMEM_LIMIT
         ),
         cost_estimate=pl.CostEstimate(flops=5_000_000, bytes_accessed=12_000_000, transcendentals=600_000),
         name="adam_out",
-    )(table, *early, weight, first, second)
+    )(early, weight, first, second)
 
 
 def body(
@@ -974,80 +945,61 @@
     own_live = (segment_at(own_positions, seg_ends) < 3).astype(F32)[:, None]
     slots = jnp.arange(N_REP, dtype=jnp.int32)
     ahead = ((place.x + slots // 2) % 4) * 2 + (place.yl + slots) % 2
-    behind = ((place.x - slots // 2) % 4) * 2 + (place.yl + slots) % 2
     half = ROWS // 2
 
     in_low = w_in.astype(BF16)
     dt_low = w_dt.astype(BF16)
-    small_rows = jnp.pad(small.astype(BF16), (0, 16 * 1152 - SHARD_SMALL)).reshape(16, 1152)
+    full_out = lax.all_gather(w_out.astype(BF16), "fsdp", axis=0, tiled=True)
+    full_in = lax.all_gather(tie(in_low, full_out), "fsdp", axis=0, tiled=True)
+
+    small_block = jnp.pad(small.astype(BF16), (0, 16 * N - SHARD_SMALL)).reshape(1, 16, N)
+    small_all = exchange(jnp.broadcast_to(small_block, (N_FSDP, 16, N)), "fsdp")
+    vector = small_all.reshape(N_FSDP, 16 * N)[:, :SHARD_SMALL].reshape(-1).astype(F32)
+
     weight_block = jnp.concatenate(
         [
-            jnp.concatenate(
-                [
-                    lax.dynamic_slice_in_dim(in_low, r * OWN, OWN, 1),
-                    lax.dynamic_slice_in_dim(in_low, DI + r * OWN, OWN, 1),
-                    in_low[:, 2 * DI :],
-                    lax.dynamic_slice_in_dim(dt_low, r * OWN_H, OWN_H, 1),
-                    jnp.zeros((SHARD_IN, 2), BF16),
-                    dt_low,
-                    jnp.zeros((SHARD_IN, N - 8 - H), BF16),
-                ],
-                1,
-            ),
-            small_rows,
-        ],
-        0,
-    )
-    out_low_shard = w_out.astype(BF16)
-    out_piece = lax.dynamic_slice(
-        out_low_shard, (SHARD_IN * (place.x // 2), WIDE * ((place.x % 2) * 2 + place.yl)), (SHARD_IN, WIDE)
-    )
-
+            lax.dynamic_slice_in_dim(in_low, r * OWN, OWN, 1),
+            lax.dynamic_slice_in_dim(in_low, DI + r * OWN, OWN, 1),
+            in_low[:, 2 * DI :],
+            lax.dynamic_slice_in_dim(dt_low, r * OWN_H, OWN_H, 1),
+            jnp.zeros((SHARD_IN, 2), BF16),
+            dt_low,
+            jnp.zeros((SHARD_IN, N - 8 - H), BF16),
+        ],
+        1,
+    )
     from_left = move(tokens, along_x(1))
     from_right = move(tokens, along_x(-1))
     partner = move(tokens, swap_y)
     weight_pair = both(weight_block, move(weight_block, swap_y_hi), place.yh)
-    out_piece = move(
-        out_piece, lambda yh, z, c, x, yl: (x % 2, yl * 2 + c, x // 2, yh * 2 + z // 2, z % 2)
-    )
-    slice_out = lax.all_gather(out_piece, "fsdp", axis=0, tiled=True)
-
-    from_left, from_right, partner, weight_pair = lax.optimization_barrier(
-        (from_left, from_right, partner, weight_pair)
-    )
+
+    from_left, from_right, weight_pair = lax.optimization_barrier((from_left, from_right, weight_pair))
     far_top = move(from_left[:half], along_x(1))
     far_low = move(from_right[half:], along_x(-1))
     partner_left = move(from_left, swap_y)
     weight_left = move(weight_pair, along_z(1))
     weight_right = move(weight_pair, along_z(-1))
 
-    far_top, far_low, partner_left, weight_left, weight_right = lax.optimization_barrier(
-        (far_top, far_low, partner_left, weight_left, weight_right)
-    )
-    right_top = move(partner[:half], along_x(-1))
-    right_low = move(from_right[half:], swap_y)
+    far_top, far_low, partner, weight_left, weight_right = lax.optimization_barrier(
+        (far_top, far_low, partner, weight_left, weight_right)
+    )
+    partner_right = move(partner, along_x(-1))
     weight_far = jnp.concatenate(
         [move(weight_left[:1], along_z(1)), move(weight_right[1:], along_z(-1))], 0
     )
 
-    right_top, right_low, weight_far, partner_left = lax.optimization_barrier(
-        (right_top, right_low, weight_far, partner_left)
+    partner_right, weight_far, partner_left = lax.optimization_barrier(
+        (partner_right, weight_far, partner_left)
     )
     partner_far_top = move(partner_left[:half], along_x(1))
-    partner_far_low = move(right_low, along_x(-1))
+    partner_far_low = move(partner_right[half:], along_x(-1))
     weight_ring = in_ring_order([weight_pair, weight_right, weight_far, weight_left], place.z, 1)
+    weight_ring = weight_ring.reshape(N_FSDP // 2, SHARD_IN, 3 * WIDE)
     weight_other = move(weight_ring, swap_core)
-    cores = [jnp.where(place.c == 0, weight_ring, weight_other), jnp.where(place.c == 0, weight_other, weight_ring)]
-    slice_in = jnp.stack([core[:, :, :SHARD_IN] for core in cores], 2).reshape(D, 1152)
-    vector = jnp.stack([core[:, :, SHARD_IN : SHARD_IN + 2] for core in cores], 2)
-    vector = vector.reshape(N_FSDP, 2 * 1152)[:, :SHARD_SMALL].reshape(-1).astype(F32)
     token_pieces = [
-        tokens, partner, from_right, right_top, right_low, far_top, far_low,
+        tokens, partner, from_right, partner_right, far_top, far_low,
         partner_far_top, partner_far_low, from_left, partner_left,
     ]
-
-    full_in = lax.all_gather(tie(in_low, slice_out), "fsdp", axis=0, tiled=True)
-    full_out = lax.all_gather(tie(out_low_shard, full_in), "fsdp", axis=0, tiled=True)
 
     offset = 0
     gain_in = vector[None, :D]
@@ -1071,62 +1023,57 @@
     par = jnp.concatenate([conv_par, head_par, jnp.zeros((8, 640), F32)], 0)
 
     branch = (cotangent.astype(F32) * own_live).astype(BF16)
-    branch = tie(branch, partner_far_top, partner_far_low)
+    branch = tie(branch, partner_left, partner_right)
     b_left = move(branch, along_x(1))
     b_right = move(branch, along_x(-1))
     b_partner = move(branch, swap_y)
-    normed, proj = run_project(ahead, token_pieces, gain_in, slice_in)
+    core_table = jnp.concatenate([ahead, place.c[None]])
+    normed, proj, low_dt = run_project(core_table, token_pieces, gain_in, weight_ring, weight_other)
     b_left, b_right, b_partner, proj = lax.optimization_barrier((b_left, b_right, b_partner, proj))
     b_far_top = move(b_left[:half], along_x(1))
     b_far_low = move(b_right[half:], along_x(-1))
     b_partner_left = move(b_left, swap_y)
-    b_right_top = move(b_partner[:half], along_x(-1))
-    b_right_low = move(b_right[half:], swap_y)
+    b_partner_right = move(b_partner, along_x(-1))
     before = run_forward(0, seg_ends, proj, par)
-    b_far_top, b_far_low, b_partner_left, b_right_top, b_right_low, before = lax.optimization_barrier(
-        (b_far_top, b_far_low, b_partner_left, b_right_top, b_right_low, before)
-    )
+    b_partner_left, b_partner_right, before = lax.optimization_barrier((b_partner_left, b_partner_right, before))
     b_partner_far_top = move(b_partner_left[:half], along_x(1))
-    b_partner_far_low = move(b_right_low, along_x(-1))
+    b_partner_far_low = move(b_partner_right[half:], along_x(-1))
     pre, mixed, states, _ = run_forward(1, seg_ends, proj, par, before)
     branch_pieces = [
-        branch, b_partner, b_right, b_right_top, b_right_low, b_far_top, b_far_low,
+        branch, b_partner, b_right, b_partner_right, b_far_top, b_far_low,
         b_partner_far_top, b_partner_far_low, b_left, b_partner_left,
     ]
-    grad_branch, grad_normed_out, sums = run_out_grad(ahead, branch_pieces, slice_out, mixed, proj, gain_row)
+    rep_table = jnp.concatenate([ahead, r[None]])
+    grad_branch, grad_normed_out, sums = run_out_grad(rep_table, branch_pieces, full_out, mixed, proj, gain_row)
     sums = sum_rep(sums[:2].reshape(32, 128)).reshape(2, PACK)
     sums = jnp.concatenate([sums, jnp.zeros((6, PACK), F32)], 0)
 
-    where = jnp.stack([place.c, place.x, place.yl])
-    row_zero, row_one, row_two, row_three, grad_mixed, keep, give, grad_gain = run_gate(
-        where, grad_normed_out, mixed, proj, sums, gain_row, grad_branch, normed
-    )
-
-    row_one = move(row_one, along_x(1))
-    row_three = move(row_three, along_x(3))
-    row_two = move(row_two, along_x(2))
-    got = move(give, swap_core)
+    low_rows, grad_mixed, early, grad_gain = run_gate(
+        grad_normed_out, mixed, proj, sums, gain_row, grad_branch, normed
+    )
+
+    low_rows = exchange(low_rows.reshape(N_REP, ROWS, 2 * OWN), "rep")
+    early = exchange(early, "fsdp")
     before = run_backward(0, seg_ends, proj, pre, mixed, grad_mixed, states, par)
-    row_one, row_two, row_three, got, before = lax.optimization_barrier(
-        (row_one, row_two, row_three, got, before)
-    )
-    mine_rows = [row_zero, row_one, row_two, row_three]
-    far_rows = jnp.concatenate(
-        [lax.dynamic_slice_in_dim(rows, (1 - place.yl) * ROWS, ROWS, 0) for rows in mine_rows], 0
-    )
-    other_rows = move(far_rows, swap_y)
-    split = (2, 4, 2 * SHARD_IN, WIDE)
-    early_part, _ = scatter_ring(keep.reshape(split), got.reshape(split), None, place)
     grad_x, grad_dtraw, grad_bc, grad_sums, grad_heads, _ = run_backward(
-        1, seg_ends, proj, pre, mixed, grad_mixed, states, par, (before[0], before[1], before[2], before[5], before[3], before[4])
-    )
+        1, seg_ends, proj, pre, mixed, grad_mixed, states, par,
+        (before[0], before[1], before[2], before[5], before[3], before[4]),
+    )
+
+    grad_bc = exchange(grad_bc, "rep")
+    x_rows = exchange(grad_x.reshape(N_REP, ROWS, OWN), "rep")
+    grad_x_own = contract_rows(normed, grad_x).reshape(N_FSDP, SHARD_IN, OWN)
+    x_part = exchange(grad_x_own, "fsdp")
+    block_out = run_block_out(low_rows, full_out, tokens, own_live)
+    grad_z_rows = run_z_grad(low_rows, full_in)
+    grad_bc, block_out, grad_z_rows = lax.optimization_barrier((grad_bc, block_out, grad_z_rows))
+    grad_bc = grad_bc.reshape(N_REP, OWN_BC, PACK).astype(F32).sum(0)
+    early = early.sum(0)
     out_part = move(
-        early_part[:SHARD_IN],
+        early[:SHARD_IN],
         lambda yh, z, c, x, yl: (x // 2, (x % 2) * 2 + yl, z % 2, 2 * c + yh, z // 2),
     )
-    early_parts = exchange_rep(jnp.concatenate([out_part, early_part[SHARD_IN:]], 0))
-
-    grad_bc = lax.all_to_all(grad_bc, "rep", 0, 0, tiled=True).reshape(N_REP, OWN_BC, PACK).sum(0)
+    early_parts = share_rep(jnp.concatenate([out_part, early[SHARD_IN:]], 0))
     own_taps = lax.dynamic_slice_in_dim(taps_bc, r * OWN_BC, OWN_BC, 1)
     own_pre = lax.dynamic_slice_in_dim(pre, OWN + r * OWN_BC, OWN_BC, 1).T
     own_conv = lax.dynamic_slice_in_dim(proj, 2 * OWN + r * OWN_BC, OWN_BC, 1).T
@@ -1144,17 +1091,11 @@
         grad_taps_bc.insert(0, jnp.sum(own_conv * later, 1))
         grad_conv_bc = grad_conv_bc + own_taps[CONV - 1 - later_by][:, None] * later
     grad_bias_bc = jnp.sum(grad_pre, 1)
-    grad_tail = jnp.concatenate(
-        [
-            grad_x,
-            grad_conv_bc.T.astype(BF16),
-            grad_dtraw[:, :OWN_H],
-            jnp.zeros((PACK, TAIL - OWN - OWN_BC - OWN_H), BF16),
-        ],
-        1,
-    )
-
-    grad_tail_own = contract_rows(normed, grad_tail).reshape(2, 4, 2, SHARD_IN, TAIL)
+    rest = jnp.concatenate(
+        [grad_conv_bc.T.astype(BF16), grad_dtraw[:, :OWN_H], jnp.zeros((PACK, N - OWN_BC - OWN_H), BF16)], 1
+    )
+    rest_rows = exchange(rest.reshape(N_REP, ROWS, N), "rep")
+
     row = lambda value: jnp.pad(value, (0, OWN - value.shape[0]))[None, :]
     head_columns = jnp.concatenate(
         [grad_gain[0:1]]
@@ -1169,66 +1110,60 @@
         0,
     )
     small_own = jnp.concatenate(
-        [head_columns, bc_columns, jnp.zeros((8, TAIL - OWN - OWN_BC), F32)], 1
-    )
-    tail_keep = at(grad_tail_own, place.c, 2)
-    tail_got, small_got = received(at(grad_tail_own, 1 - place.c, 2), swap_core, small_own, tail_keep)
-    tail_part, small_sum = scatter_ring(tail_keep, tail_got, small_own + small_got, place)
-
-    tail_rows = lax.all_to_all(grad_tail, "rep", 0, 0, tiled=True).reshape(N_REP, ROWS, TAIL)
+        [
+            head_columns[:, :N],
+            head_columns[:, N : 2 * N],
+            head_columns[:, 2 * N :],
+            jnp.pad(bc_columns, ((0, 0), (0, N - OWN_BC))),
+        ],
+        0,
+    )
+    grad_rest = contract_rows(normed, rest).reshape(N_FSDP, SHARD_IN, N)
+    grad_rest = jnp.concatenate([grad_rest, jnp.broadcast_to(small_own[None], (N_FSDP, 32, N))], 1)
+    rest_part = exchange(grad_rest, "fsdp")
+    x_parts = share_rep(x_part.sum(0))
+    rest_parts = share_rep(rest_part.sum(0))
 
     def columns(parts):
         return parts.transpose(1, 0, 2).reshape(parts.shape[1], -1)
 
     rest_rows = jnp.concatenate(
         [
-            columns(tail_rows[:, :, OWN : OWN + OWN_BC]),
+            columns(rest_rows[:, :, :OWN_BC]),
             jnp.zeros((ROWS, 8), BF16),
-            columns(tail_rows[:, :, OWN + OWN_BC : OWN + OWN_BC + OWN_H]),
+            columns(rest_rows[:, :, OWN_BC : OWN_BC + OWN_H]),
             jnp.zeros((ROWS, N - 8 - H), BF16),
         ],
         1,
     )
-    behind_table = jnp.concatenate([behind, place.yl[None]])
     input_grad, grad_gain_in = run_input_grad(
-        behind_table, mine_rows, other_rows, tail_rows, rest_rows, full_in, slice_in[:, 1024:1152],
-        tokens, cotangent, gain_in,
+        grad_z_rows, x_rows, rest_rows, full_in, low_dt, tokens, cotangent, gain_in
     )
     grad_gain_in = sum_all(grad_gain_in[0].reshape(12, 128)).reshape(-1)
 
-    block_out = run_block_out(behind_table, mine_rows, other_rows, full_out, tokens, own_live)
-
-    tail_block = jnp.concatenate([tail_part, small_sum], 0)
-    tail_parts = lax.all_to_all(
-        jnp.broadcast_to(tail_block[None], (N_REP,) + tail_block.shape), "rep", 0, 0, tiled=True
-    )
-    small_parts = tail_parts[:, SHARD_IN:]
+    small_parts = rest_parts[:, SHARD_IN:].reshape(N_REP, 4, 8, N)
+    small_x = small_parts[:, :3].transpose(2, 0, 1, 3).reshape(8, DI)
+    small_bc = small_parts[:, 3].transpose(1, 0, 2)
 
     def channels(row):
-        return jnp.concatenate(
-            [small_parts[:, row, :OWN].reshape(-1), small_parts[:, row, OWN : OWN + OWN_BC].reshape(-1)]
-        )
+        return jnp.concatenate([small_x[row], small_bc[row, :, :OWN_BC].reshape(-1)])
 
     grad_small_all = jnp.concatenate(
-        [grad_gain_in, small_parts[:, 0, :OWN].reshape(-1)]
+        [grad_gain_in, small_x[0]]
         + [channels(row) for row in range(1, 6)]
         + [
-            small_parts[:, 0, OWN : OWN + OWN_H].reshape(-1),
-            small_parts[:, 6, :OWN_H].reshape(-1),
-            small_parts[:, 7, :OWN_H].reshape(-1),
+            small_bc[0, :, :OWN_H].reshape(-1),
+            small_parts[:, 0, 6, :OWN_H].reshape(-1),
+            small_parts[:, 0, 7, :OWN_H].reshape(-1),
         ]
     )
     grad_small = lax.dynamic_slice_in_dim(grad_small_all, place.f * SHARD_SMALL, SHARD_SMALL, 0)
-    grad_dt = columns(tail_parts[:, :SHARD_IN, OWN + OWN_BC : OWN + OWN_BC + OWN_H])
-    rest_grad = jnp.pad(columns(tail_parts[:, :SHARD_IN, OWN : OWN + OWN_BC]), ((0, 0), (0, WIDE - 2 * N)))
-
-    in_table = jnp.concatenate([ahead, jnp.arange(N_REP, 2 * N_REP + 1, dtype=jnp.int32)])
+    grad_dt = columns(rest_parts[:, :SHARD_IN, OWN_BC : OWN_BC + OWN_H])
+    rest_grad = jnp.pad(columns(rest_parts[:, :SHARD_IN, :OWN_BC]), ((0, 0), (0, 2 * WIDE - 2 * N)))
     grad_in, new_first_in, new_second_in, new_in = run_adam_in(
-        in_table, early_parts, tail_parts, rest_grad, w_in, first_in, second_in
-    )
-    grad_out, new_first_out, new_second_out, new_out = run_adam_out(
-        ahead, early_parts, w_out, first_out, second_out
-    )
+        early_parts, x_parts, rest_grad, w_in, first_in, second_in
+    )
+    grad_out, new_first_out, new_second_out, new_out = run_adam_out(early_parts, w_out, first_out, second_out)
     new_dt, new_first_dt, new_second_dt = adam_update(
         w_dt, grad_dt, first_dt, second_dt, RATE_MATRIX, WEIGHT_DECAY
     )

time: 678 us -> 691 us (1.019)
  blocking collectives: 0 us -> 95.8 us
  local copies, waits for them, and re-layouts: 125 us -> 30.7 us
  other arithmetic: 42.5 us -> 21.2 us
  waiting for transfers between devices: 230 us -> 251 us
  Pallas kernels: 147 us -> 158 us
    all_to_all x0 -> x3, blocking collectives: none -> 95.8 us  [exchange(): return lax.all_to_all(value, axis, 0, 0, tiled=True)]
    ppermute x59 -> x35, waiting for transfers between devices: 145 us -> 98.2 us  [move(): return lax.ppermute(value, ('fsdp', 'rep'), pairs)]
    unnamed x194 -> x78, local copies, waits for them, and re-layouts: 49.8 us -> 4.93 us
    all_to_all x3 -> x8, waiting for transfers between devices: 29.8 us -> 74.3 us  [exchange(): return lax.all_to_all(value, axis, 0, 0, tiled=True)]
    ppermute x59 -> x35, starting transfers between devices: 87.3 us -> 48.8 us  [move(): return lax.ppermute(value, ('fsdp', 'rep'), pairs)]
    all_to_all x3 -> x8, starting transfers between devices: 12.9 us -> 45.6 us  [exchange(): return lax.all_to_all(value, axis, 0, 0, tiled=True)]
    all_gather x3 -> x2, waiting for transfers between devices: 55.6 us -> 78.8 us  [the longest x1 78.8 us: body(): full_out = lax.all_gather(w_out.astype(BF16), 'fsdp', axis=0, tiled=True)]
    another operation x11 -> x8, local copies, waits for them, and re-layouts: 13.3 us -> 0.63 us  [the longest x5 0.39 us: channels(): small_bc[row, :, :OWN_BC].reshape(-1)]
  transfers between devices with their start and end apart: 65 -> 45, of which waited for: 23 -> 25; matrix products, arithmetic and copies ran while one was open for 18% -> 8% of each run, Pallas kernels for 20% -> 22%
where the time goes in v3:
time: 691 us; the launch traced here: 680 us
  waiting for transfers between devices  251 us (36%)
  Pallas kernels  158 us (23%)
  blocking collectives  95.8 us (14%)
  starting transfers between devices  94.5 us (14%)
  local copies, waits for them, and re-layouts  30.7 us (4%)
  other arithmetic  21.2 us (3%)
  between operations  15.4 us (2%)
  matrix products  12.8 us (2%)
    ppermute x35, waiting for transfers between devices, move(): return lax.ppermute(value, ('fsdp', 'rep'), pairs)  98.2 us
    all_to_all x3, blocking collectives, exchange(): return lax.all_to_all(value, axis, 0, 0, tiled=True)  95.8 us
    all_gather x1, waiting for transfers between devices, body(): full_out = lax.all_gather(w_out.astype(BF16), 'fsdp', axis=0, tiled=True)  78.8 us
    all_to_all x8, waiting for transfers between devices, exchange(): return lax.all_to_all(value, axis, 0, 0, tiled=True)  74.3 us
    ppermute x35, starting transfers between devices, move(): return lax.ppermute(value, ('fsdp', 'rep'), pairs)  48.8 us
    all_to_all x8, starting transfers between devices, exchange(): return lax.all_to_all(value, axis, 0, 0, tiled=True)  45.6 us
    pallas_call x2, Pallas kernels, run_backward(): pl.pallas_call(partial(backward_kernel, part), grid=(HALF,), in_specs=[pl...  35 us
    pallas_call x2, Pallas kernels, run_forward(): pl.pallas_call(partial(forward_kernel, part), grid=(HALF,), in_specs=[pl....  24.3 us
  transfers between devices with their start and end apart: 45, of which 25 were waited for; matrix products, arithmetic and copies ran while one was open for 8% of the time, Pallas kernels for 22%

profile of v3, /device:TPU:0, one launch (start us, length us, event | category | flops | bytes accessed | tf_op | source)
XLA Modules:
  0.0 680.1 jit_solution(17718642292180952382)
XLA Ops:
  12.4 78.8 %all-gather.3.cloned.1.call-done.refs_10_.weight = bf16[3072,1536]{1,0:T(8,128)(2,1)} async-done(((bf16[192,1536]{1,0:T(8,128)(2,1)}), bf16[3072,1536]{1,0:T(8,128)(2,1)}) %all-gather.3.cloned.1.call-update) | async-done | bytes 9437200 | tf_op jit(solution)/shard_map/all_gather | solution.py:952
  103.3 11.3 %collective-permute-done.refs_8_ = bf16[256,1536]{1,0:T(8,128)(2,1)S(1)} collective-permute-done((bf16[256,1536]{1,0:T(8,128)(2,1)S(1)}, bf16[256,1536]{1,0:T(8,128)(2,1)S(1)}, u32[]{:S(2)}, u32[]{:S(2)}) %collective-permute-start) | collective-permute-done | bytes 786464 | tf_op jit(solution)/shard_map/ppermute | solution.py:53
  168.4 17.8 %project.1 = (bf16[2048,1536]{1,0:T(8,128)(2,1)}, f32[2048,1152]{1,0:T(8,128)}, bf16[1536,128]{1,0:T(8,128)(2,1)}) custom-call(s32[9]{0:T(128)} %get-tuple-element.198.table, bf16[256,1536]{1,0:T(8,128)(2,1)} %tokens.3, bf16[256,1536]{1,0:T(8,128)(2,1)} %collective-permute-done.5.refs_1_, bf16[256,1536]{1,0:T(8,128)(2,1)} %collective-permute-done.1.refs_2_, ...), custom_call_target="tpu_custom_call" | custom-call | flops 7249999872 | bytes 26000000 | tf_op jit(solution)/shard_map/project/pallas_call | solution.py:577
  186.3 16.7 %collective-permute-done.14.refs_1_ = bf16[256,1536]{1,0:T(8,128)(2,1)S(1)} collective-permute-done((bf16[256,1536]{1,0:T(8,128)(2,1)S(1)}, bf16[256,1536]{1,0:T(8,128)(2,1)S(1)}, u32[]{:S(2)}, u32[]{:S(2)}) %collective-permute-start.14) | collective-permute-done | bytes 786464 | tf_op jit(solution)/shard_map/ppermute | solution.py:53
  214.2 12.1 %scan_forward.2 = (f32[2048,640]{1,0:T(8,128)}, f32[2048,384]{1,0:T(8,128)}, f32[2048,384]{1,0:T(8,128)}, f32[136,640]{1,0:T(8,128)}) custom-call(s32[3]{0:T(128)} %bitcast.154, f32[2048,1152]{1,0:T(8,128)} %get-tuple-element.95.proj.refs_12_.gate_in.conv_in.dt_in, f32[16,640]{1,0:T(8,128)} %concatenate.55.par), custom_call_target="tpu_custom_call" | custom-call | flops 8000000000 | bytes 12000000 | tf_op jit(solution)/shard_map/scan_forward/pallas_call | solution.py:341
  226.3 14.1 %collective-permute-done.18.refs_9_ = bf16[256,1536]{1,0:T(8,128)(2,1)S(1)} collective-permute-done((bf16[256,1536]{1,0:T(8,128)(2,1)S(1)}, bf16[256,1536]{1,0:T(8,128)(2,1)S(1)}, u32[]{:S(2)}, u32[]{:S(2)}) %collective-permute-start.18) | collective-permute-done | bytes 786464 | tf_op jit(solution)/shard_map/ppermute | solution.py:53
  243.8 12.2 %scan_forward.3 = (f32[2048,640]{1,0:T(8,128)}, f32[2048,384]{1,0:T(8,128)}, f32[2048,384]{1,0:T(8,128)}, f32[136,640]{1,0:T(8,128)}) custom-call(s32[3]{0:T(128)} %bitcast.155, f32[2048,1152]{1,0:T(8,128)} %get-tuple-element.95.proj.refs_12_.gate_in.conv_in.dt_in, ...), custom_call_target="tpu_custom_call", output_to_operand_aliasing={{0}: (3, {}), {1}: (4, {}), {2}: (5, {})} | custom-call | flops 8000000000 | bytes 12000000 | tf_op jit(solution)/shard_map/scan_forward/pallas_call | solution.py:341
  257.2 14.0 %out_grad.1 = (bf16[2048,1536]{1,0:T(8,128)(2,1)}, f32[2048,384]{1,0:T(8,128)}, f32[8,2048]{1,0:T(8,128)}) custom-call(s32[9]{0:T(128)} %get-tuple-element.197.table, bf16[256,1536]{1,0:T(8,128)(2,1)} %copy-done.7, bf16[256,1536]{1,0:T(8,128)(2,1)} %copy-done.15, bf16[256,1536]{1,0:T(8,128)(2,1)} %copy-done.12, bf16[256,1536]{1,0:T(8,128)(2,1)} %copy-done.14, ...), custom_call_target="tpu_custom_call" | custom-call | flops 2420000000 | bytes 23000000 | tf_op jit(solution)/shard_map/out_grad/pallas_call | solution.py:630
  285.6 16.5 %gate_backward.1 = (bf16[2048,768]{1,0:T(8,128)(2,1)}, f32[2048,384]{1,0:T(8,128)}, f32[16,192,384]{2,1,0:T(8,128)}, f32[8,384]{1,0:T(8,128)}) custom-call(f32[2048,384]{1,0:T(8,128)} %get-tuple-element.111.grad_out, f32[2048,384]{1,0:T(8,128)} %get-tuple-element.107.refs_11_.mixed_in, f32[2048,1152]{1,0:T(8,128)} %get-tuple-element.95.proj.refs_12_.gate_in.conv_in.dt_in, ...), custom_call_target="tpu_custom_call" | custom-call | flops 4840000000 | bytes 34000000 | tf_op jit(solution)/shard_map/gate_backward/pallas_call | solution.py:694
  302.1 17.4 %scan_backward.2 = (bf16[2048,384]{1,0:T(8,128)(2,1)}, bf16[2048,128]{1,0:T(8,128)(2,1)}, bf16[256,2048]{1,0:T(8,128)(2,1)}, f32[8,384]{1,0:T(8,128)}, f32[8,128]{1,0:T(8,128)}, /*index=5*/f32[144,384]{1,0:T(8,128)}) custom-call(s32[3]{0:T(128)} %bitcast.156, f32[2048,1152]{1,0:T(8,128)} %get-tuple-element.95.proj.refs_12_.gate_in.conv_in.dt_in, ...), custom_call_target="tpu_custom_call" | custom-call | flops 12000000000 | bytes 16000000 | tf_op jit(solution)/shard_map/scan_backward/pallas_call | solution.py:486
  319.5 17.6 %scan_backward.3 = (bf16[2048,384]{1,0:T(8,128)(2,1)}, bf16[2048,128]{1,0:T(8,128)(2,1)}, bf16[256,2048]{1,0:T(8,128)(2,1)}, f32[8,384]{1,0:T(8,128)}, f32[8,128]{1,0:T(8,128)}, /*index=5*/f32[144,384]{1,0:T(8,128)}) custom-call(s32[3]{0:T(128)} %bitcast.157, ...), custom_call_target="tpu_custom_call", output_to_operand_aliasing={{0}: (8, {}), {1}: (9, {}), {2}: (10, {})} | custom-call | flops 12000000000 | bytes 16000000 | tf_op jit(solution)/shard_map/scan_backward/pallas_call | solution.py:486
  337.1 14.7 %all_to_all.62 = bf16[8,32,2048]{2,1,0:T(8,128)(2,1)S(1)} all-to-all(bf16[8,32,2048]{2,1,0:T(8,128)(2,1)} %bitcast.142), channel_id=1, replica_groups=mesh['fsdp'=16,'rep'=8] {'rep'}, dimensions={0} | all-to-all | bytes 2097152 | tf_op jit(solution)/shard_map/all_to_all | solution.py:114
  370.7 39.9 %all_to_all.63 = f32[16,96,384]{2,1,0:T(8,128)} all-to-all(f32[16,96,384]{2,1,0:T(8,128)} %bitcast.140), channel_id=1, replica_groups=mesh['fsdp'=16,'rep'=8] {'fsdp'}, dimensions={0} | all-to-all | bytes 4718592 | tf_op jit(solution)/shard_map/all_to_all | solution.py:114
  410.6 41.2 %all_to_all.64.rows = bf16[8,256,768]{2,1,0:T(8,128)(2,1)} all-to-all(bf16[8,256,768]{2,1,0:T(8,128)(2,1)S(1)} %bitcast.138), channel_id=1, replica_groups=mesh['fsdp'=16,'rep'=8] {'rep'}, dimensions={0} | all-to-all | bytes 6291456 | tf_op jit(solution)/shard_map/all_to_all | solution.py:114
  459.6 10.9 %block_out.1 = f32[256,1536]{1,0:T(8,128)} custom-call(bf16[8,256,768]{2,1,0:T(8,128)(2,1)} %all_to_all.64.rows, bf16[3072,1536]{1,0:T(8,128)(2,1)} %all-gather.3.cloned.1.call-done.refs_10_.weight, bf16[256,1536]{1,0:T(8,128)(2,1)} %tokens.3, f32[256,1]{1,0:T(8,128)} %fusion.11.live), custom_call_target="tpu_custom_call" | custom-call | flops 2420000000 | bytes 14000000 | tf_op jit(solution)/shard_map/block_out/pallas_call | solution.py:740
  470.6 10.6 %z_grad.1.grad_z = f32[256,1536]{1,0:T(8,128)} custom-call(bf16[8,256,768]{2,1,0:T(8,128)(2,1)} %all_to_all.64.rows, bf16[1536,6400]{1,0:T(8,128)(2,1)} %all-gather.5.cloned.1.call-done.weight.w_x.w_bc), custom_call_target="tpu_custom_call" | custom-call | flops 2420000000 | bytes 14000000 | tf_op jit(solution)/shard_map/z_grad/pallas_call | solution.py:772
  487.9 31.0 %all-to-all-done.5 = f32[16,192,384]{2,1,0:T(8,128)} async-done(((f32[16,192,384]{2,1,0:T(8,128)}), f32[16,192,384]{2,1,0:T(8,128)}, u32[]{:S(2)}, u32[]{:S(2)}) %all-to-all-start.5) | async-done | bytes 4718624 | tf_op jit(solution)/shard_map/all_to_all | solution.py:114
  532.0 13.9 %all-to-all-start.9 = ((f32[16,128,128]{2,1,0:T(8,128)}), f32[16,128,128]{2,1,0:T(8,128)S(1)}, u32[]{:S(2)}, u32[]{:S(2)}) async-start(f32[16,128,128]{2,1,0:T(8,128)} %pad_maximum_fusion), calls=%async_computation.9 | async-start | bytes 2097152 | tf_op jit(solution)/shard_map/all_to_all | solution.py:114
  549.2 15.4 %all-to-all-done.9 = f32[16,128,128]{2,1,0:T(8,128)S(1)} async-done(((f32[16,128,128]{2,1,0:T(8,128)}), f32[16,128,128]{2,1,0:T(8,128)S(1)}, u32[]{:S(2)}, u32[]{:S(2)}) %all-to-all-start.9) | async-done | bytes 1048608 | tf_op jit(solution)/shard_map/all_to_all | solution.py:114
  566.4 8.4 %all-to-all-start.6 = ((f32[8,192,384]{2,1,0:T(8,128)}), f32[8,192,384]{2,1,0:T(8,128)S(1)}, u32[]{:S(2)}, u32[]{:S(2)}) async-start(f32[8,192,384]{2,1,0:T(8,128)} %broadcast_in_dim.142), calls=%async_computation.6 | async-start | bytes 4718592 | tf_op jit(solution)/shard_map/all_to_all | solution.py:114
  576.5 13.3 %input_grad.1 = (f32[256,1536]{1,0:T(8,128)}, f32[8,1536]{1,0:T(8,128)}) custom-call(f32[256,1536]{1,0:T(8,128)} %z_grad.1.grad_z, bf16[8,256,384]{2,1,0:T(8,128)(2,1)} %copy-done.3, bf16[256,384]{1,0:T(8,128)(2,1)} %maximum_maximum_fusion.1.rest, bf16[1536,6400]{1,0:T(8,128)(2,1)} %all-gather.5.cloned.1.call-done.weight.w_x.w_bc, ...), custom_call_target="tpu_custom_call" | custom-call | flops 2700000000 | bytes 18000000 | tf_op jit(solution)/shard_map/input_grad/pallas_call | solution.py:815
  592.8 10.0 %collective-permute-done.28 = f32[12,128]{1,0:T(8,128)S(1)} collective-permute-done((f32[12,128]{1,0:T(8,128)S(1)}, f32[12,128]{1,0:T(8,128)S(1)}, u32[]{:S(2)}, u32[]{:S(2)}) %collective-permute-start.28) | collective-permute-done | bytes 6176 | tf_op jit(solution)/shard_map/ppermute | solution.py:53
  648.8 11.5 %all-to-all-done.8.tail = f32[8,96,384]{2,1,0:T(8,128)S(1)} async-done(((f32[8,96,384]{2,1,0:T(8,128)}), f32[8,96,384]{2,1,0:T(8,128)S(1)}, u32[]{:S(2)}, u32[]{:S(2)}) %all-to-all-start.8) | async-done | bytes 1179680 | tf_op jit(solution)/shard_map/all_to_all | solution.py:114
  661.3 11.7 %adam_in.1 = (f32[96,6400]{1,0:T(8,128)}, f32[96,6400]{1,0:T(8,128)}, f32[96,6400]{1,0:T(8,128)}, f32[96,6400]{1,0:T(8,128)}) custom-call(f32[8,192,384]{2,1,0:T(8,128)} %copy-done.2, f32[8,96,384]{2,1,0:T(8,128)} %copy-done.4, f32[96,768]{1,0:T(8,128)} %pad.46.rest, f32[96,6400]{1,0:T(8,128)} %refs_0_.4, f32[96,6400]{1,0:T(8,128)} %refs_1_.2, ...), custom_call_target="tpu_custom_call" | custom-call | flops 10000000 | bytes 22000000 | tf_op jit(solution)/shard_map/adam_in/pallas_call | solution.py:875
  (333 shorter events, 203.9 us)
Async XLA Ops:
  7.2 84.0 %all-gather.3.cloned.1.call-start = ((), (), s32[]{:S(2)}) async-start(), calls=%async_computation.11 | async-start | bytes 10027008 | tf_op jit(solution)/shard_map/all_gather | solution.py:952
  9.4 461.1 %all-gather.5.cloned.1.call-start = ((), (), s32[]{:S(2)}) async-start(), calls=%async_computation.12 | async-start | bytes 20889600 | tf_op jit(solution)/shard_map/all_gather | solution.py:953
  93.9 20.6 %collective-permute-start = (bf16[256,1536]{1,0:T(8,128)(2,1)S(1)}, bf16[256,1536]{1,0:T(8,128)(2,1)S(1)}, u32[]{:S(2)}, u32[]{:S(2)}) collective-permute-start(bf16[256,1536]{1,0:T(8,128)(2,1)S(1)} %copy-done.8), channel_id=1, source_target_pairs={{0,2},{1,3},{2,4},{3,5},{4,6},{5,7},{6,0},{7,1},{8,10},{9,11},{10,... | collective-permute-start | bytes 2359304 | tf_op jit(solution)/shard_map/ppermute | solution.py:53
  95.4 20.1 %collective-permute-start.1 = (bf16[256,1536]{1,0:T(8,128)(2,1)S(1)}, bf16[256,1536]{1,0:T(8,128)(2,1)}, u32[]{:S(2)}, u32[]{:S(2)}) collective-permute-start(bf16[256,1536]{1,0:T(8,128)(2,1)S(1)} %copy-done.8), channel_id=1, source_target_pairs={{0,6},{1,7},{2,0},{3,1},{4,2},{5,3},{6,4},{7,5},{8,14},{9,15},{10,... | collective-permute-start | bytes 2359304 | tf_op jit(solution)/shard_map/ppermute | solution.py:53
  97.1 33.9 %collective-permute-start.5 = (bf16[256,1536]{1,0:T(8,128)(2,1)S(1)}, bf16[256,1536]{1,0:T(8,128)(2,1)}, u32[]{:S(2)}, u32[]{:S(2)}) collective-permute-start(bf16[256,1536]{1,0:T(8,128)(2,1)S(1)} %copy-done.8), channel_id=1, source_target_pairs={{0,1},{1,0},{2,3},{3,2},{4,5},{5,4},{6,7},{7,6},{8,9},{9,8},{10,11... | collective-permute-start | bytes 2359304 | tf_op jit(solution)/shard_map/ppermute | solution.py:53
  115.4 16.2 %collective-permute-start.6 = (bf16[2,96,1152]{2,1,0:T(8,128)(2,1)S(1)}, bf16[2,96,1152]{2,1,0:T(8,128)(2,1)S(1)}, u32[]{:S(2)}, u32[]{:S(2)}) collective-permute-start(bf16[2,96,1152]{2,1,0:T(8,128)(2,1)S(1)} %pad_maximum_fusion.1), channel_id=1, source_target_pairs={{0,16},{1,17},{2,18},{3,19},{4,20},{5,21},{6,22},{7,23},{8,24},{9,... | collective-permute-start | bytes 1327112 | tf_op jit(solution)/shard_map/ppermute | solution.py:53
  115.5 16.1 %collective-permute-start.7 = (bf16[2,96,1152]{2,1,0:T(8,128)(2,1)S(1)}, bf16[2,96,1152]{2,1,0:T(8,128)(2,1)S(1)}, u32[]{:S(2)}, u32[]{:S(2)}) collective-permute-start(bf16[2,96,1152]{2,1,0:T(8,128)(2,1)S(1)} %pad_maximum_fusion.1), channel_id=1, source_target_pairs={{0,48},{1,49},{2,50},{3,51},{4,52},{5,53},{6,54},{7,55},{8,56},{9,... | collective-permute-start | bytes 1327112 | tf_op jit(solution)/shard_map/ppermute | solution.py:53
  124.8 28.0 %all-to-all-start = ((bf16[16,16,128]{2,1,0:T(8,128)(2,1)}), bf16[16,16,128]{2,1,0:T(8,128)(2,1)S(1)}, u32[]{:S(2)}, u32[]{:S(2)}) async-start(bf16[16,16,128]{2,1,0:T(8,128)(2,1)} %broadcast_in_dim.125), calls=%async_computation | async-start | bytes 131072 | tf_op jit(solution)/shard_map/all_to_all | solution.py:114
  131.1 18.7 %collective-permute-start.11 = (bf16[256,1536]{1,0:T(8,128)(2,1)}, bf16[256,1536]{1,0:T(8,128)(2,1)S(1)}, u32[]{:S(2)}, u32[]{:S(2)}) collective-permute-start(bf16[256,1536]{1,0:T(8,128)(2,1)} %copy-done.21), channel_id=1, source_target_pairs={{0,1},{1,0},{2,3},{3,2},{4,5},{5,4},{6,7},{7,6},{8,9},{9,8},{10,11... | collective-permute-start | bytes 2359304 | tf_op jit(solution)/shard_map/ppermute | solution.py:53
  131.7 18.5 %collective-permute-start.8 = (bf16[256,1536]{1,0:T(8,128)(2,1)}, bf16[256,1536]{1,0:T(8,128)(2,1)S(1)}, u32[]{:S(2)}, u32[]{:S(2)}) collective-permute-start(bf16[256,1536]{1,0:T(8,128)(2,1)} %collective-permute-done.5.refs_1_), channel_id=1, source_target_pairs={{0,6},{1,7},{2,0},{3,1},{4,2},{5,3},{6,4},{7,5},{8,14},{9,15},{10,... | collective-permute-start | bytes 2359304 | tf_op jit(solution)/shard_map/ppermute | solution.py:53
  151.8 15.9 %collective-permute-start.17 = (bf16[8,96,1152]{2,1,0:T(8,128)(2,1)}, bf16[8,96,1152]{2,1,0:T(8,128)(2,1)}, u32[]{:S(2)}, u32[]{:S(2)}) collective-permute-start(bf16[8,96,1152]{2,1,0:T(8,128)(2,1)} %bitcast.13.refs_11_), channel_id=1, source_target_pairs={{0,8},{1,9},{2,10},{3,11},{4,12},{5,13},{6,14},{7,15},{8,0},{9,1},... | collective-permute-start | bytes 5308424 | tf_op jit(solution)/shard_map/ppermute | solution.py:53
  157.2 29.0 %collective-permute-start.12 = (bf16[256,1536]{1,0:T(8,128)(2,1)S(1)}, bf16[256,1536]{1,0:T(8,128)(2,1)S(1)}, u32[]{:S(2)}, u32[]{:S(2)}) collective-permute-start(bf16[256,1536]{1,0:T(8,128)(2,1)S(1)} %multiply_convert_fusion.refs_0_), channel_id=1, source_target_pairs={{0,2},{1,3},{2,4},{3,5},{4,6},{5,7},{6,0},{7,1},{8,10},{9,11},{10,... | collective-permute-start | bytes 2359304 | tf_op jit(solution)/shard_map/ppermute | solution.py:53
  157.2 29.0 %collective-permute-start.13 = (bf16[256,1536]{1,0:T(8,128)(2,1)S(1)}, bf16[256,1536]{1,0:T(8,128)(2,1)S(1)}, u32[]{:S(2)}, u32[]{:S(2)}) collective-permute-start(bf16[256,1536]{1,0:T(8,128)(2,1)S(1)} %multiply_convert_fusion.refs_0_), channel_id=1, source_target_pairs={{0,6},{1,7},{2,0},{3,1},{4,2},{5,3},{6,4},{7,5},{8,14},{9,15},{10,... | collective-permute-start | bytes 2359304 | tf_op jit(solution)/shard_map/ppermute | solution.py:53
  166.2 36.8 %collective-permute-start.14 = (bf16[256,1536]{1,0:T(8,128)(2,1)S(1)}, bf16[256,1536]{1,0:T(8,128)(2,1)S(1)}, u32[]{:S(2)}, u32[]{:S(2)}) collective-permute-start(bf16[256,1536]{1,0:T(8,128)(2,1)S(1)} %multiply_convert_fusion.refs_0_), channel_id=1, source_target_pairs={{0,1},{1,0},{2,3},{3,2},{4,5},{5,4},{6,7},{7,6},{8,9},{9,8},{10,11... | collective-permute-start | bytes 2359304 | tf_op jit(solution)/shard_map/ppermute | solution.py:53
  203.9 36.5 %collective-permute-start.18 = (bf16[256,1536]{1,0:T(8,128)(2,1)S(1)}, bf16[256,1536]{1,0:T(8,128)(2,1)S(1)}, u32[]{:S(2)}, u32[]{:S(2)}) collective-permute-start(bf16[256,1536]{1,0:T(8,128)(2,1)S(1)} %collective-permute-done.12.refs_8_), channel_id=1, source_target_pairs={{0,1},{1,0},{2,3},{3,2},{4,5},{5,4},{6,7},{7,6},{8,9},{9,8},{10,11... | collective-permute-start | bytes 2359304 | tf_op jit(solution)/shard_map/ppermute | solution.py:53
  205.3 35.1 %collective-permute-start.19 = (bf16[256,1536]{1,0:T(8,128)(2,1)}, bf16[256,1536]{1,0:T(8,128)(2,1)S(1)}, u32[]{:S(2)}, u32[]{:S(2)}) collective-permute-start(bf16[256,1536]{1,0:T(8,128)(2,1)} %copy-done.15), channel_id=1, source_target_pairs={{0,6},{1,7},{2,0},{3,1},{4,2},{5,3},{6,4},{7,5},{8,14},{9,15},{10,... | collective-permute-start | bytes 2359304 | tf_op jit(solution)/shard_map/ppermute | solution.py:53
  209.9 46.2 %collective-permute-start.20 = (bf16[128,1536]{1,0:T(8,128)(2,1)}, bf16[128,1536]{1,0:T(8,128)(2,1)S(1)}, u32[]{:S(2)}, u32[]{:S(2)}) collective-permute-start(bf16[128,1536]{1,0:T(8,128)(2,1)} %slice.189), channel_id=1, source_target_pairs={{0,2},{1,3},{2,4},{3,5},{4,6},{5,7},{6,0},{7,1},{8,10},{9,11},{10,... | collective-permute-start | bytes 1179656 | tf_op jit(solution)/shard_map/ppermute | solution.py:53
  211.3 44.9 %collective-permute-start.21 = (bf16[128,1536]{1,0:T(8,128)(2,1)}, bf16[128,1536]{1,0:T(8,128)(2,1)S(1)}, u32[]{:S(2)}, u32[]{:S(2)}) collective-permute-start(bf16[128,1536]{1,0:T(8,128)(2,1)} %slice.190), channel_id=1, source_target_pairs={{0,6},{1,7},{2,0},{3,1},{4,2},{5,3},{6,4},{7,5},{8,14},{9,15},{10,... | collective-permute-start | bytes 1179656 | tf_op jit(solution)/shard_map/ppermute | solution.py:53
  351.8 18.9 %all-to-all-start.3 = ((bf16[8,256,384]{2,1,0:T(8,128)(2,1)}), bf16[8,256,384]{2,1,0:T(8,128)(2,1)S(1)}, u32[]{:S(2)}, u32[]{:S(2)}) async-start(bf16[8,256,384]{2,1,0:T(8,128)(2,1)} %bitcast.141), calls=%async_computation.3 | async-start | bytes 3145728 | tf_op jit(solution)/shard_map/all_to_all | solution.py:114
  451.8 67.1 %all-to-all-start.5 = ((f32[16,192,384]{2,1,0:T(8,128)}), f32[16,192,384]{2,1,0:T(8,128)}, u32[]{:S(2)}, u32[]{:S(2)}) async-start(f32[16,192,384]{2,1,0:T(8,128)} %get-tuple-element.133), calls=%async_computation.5 | async-start | bytes 9437184 | tf_op jit(solution)/shard_map/all_to_all | solution.py:114
  532.0 32.6 %all-to-all-start.9 = ((f32[16,128,128]{2,1,0:T(8,128)}), f32[16,128,128]{2,1,0:T(8,128)S(1)}, u32[]{:S(2)}, u32[]{:S(2)}) async-start(f32[16,128,128]{2,1,0:T(8,128)} %pad_maximum_fusion), calls=%async_computation.9 | async-start | bytes 2097152 | tf_op jit(solution)/shard_map/all_to_all | solution.py:114
  566.4 43.0 %all-to-all-start.6 = ((f32[8,192,384]{2,1,0:T(8,128)}), f32[8,192,384]{2,1,0:T(8,128)S(1)}, u32[]{:S(2)}, u32[]{:S(2)}) async-start(f32[8,192,384]{2,1,0:T(8,128)} %broadcast_in_dim.142), calls=%async_computation.6 | async-start | bytes 4718592 | tf_op jit(solution)/shard_map/all_to_all | solution.py:114
  610.2 30.3 %all-to-all-start.10 = ((f32[8,128,128]{1,2,0:T(8,128)}), f32[8,128,128]{1,2,0:T(8,128)S(1)}, u32[]{:S(2)}, u32[]{:S(2)}) async-start(f32[8,128,128]{1,2,0:T(8,128)} %broadcast_in_dim.147), calls=%async_computation.10 | async-start | bytes 1048576 | tf_op jit(solution)/shard_map/all_to_all | solution.py:114
  641.6 18.7 %all-to-all-start.8 = ((f32[8,96,384]{2,1,0:T(8,128)}), f32[8,96,384]{2,1,0:T(8,128)S(1)}, u32[]{:S(2)}, u32[]{:S(2)}) async-start(f32[8,96,384]{2,1,0:T(8,128)} %broadcast_in_dim.143), calls=%async_computation.8 | async-start | bytes 2359296 | tf_op jit(solution)/shard_map/all_to_all | solution.py:114
  (59 other events, 897.9 us)
Sparse Core Ops, SparseCore 0:
  11.1 80.0 all-gather.2
  94.2 170.6 all-gather.4
